TPU v7x, 32 devices: a whole 2x2x4 slice. The times are simulated.
32 devices in a mesh: gx: 2 (over x), gy: 4 (over z), gz: 4 (over y, core).
Axes of the slice: x: 2, y: 2, z: 4, core: 2. Of those that a mesh axis runs over, the one named last changes fastest.
Arguments:
- species_field: float32 [256, 128, 512], P('gx', 'gy', 'gz'), may hold values from -40 to 40
- test_matrix: float32 [48, 128, 512], P(None, 'gy', 'gz'), may hold values from -0.0234375 to 0.0234375
Outputs:
- core_tensor: float32 [48, 128, 512], P('gx', 'gy', 'gz')
All inputs are finite; a program needn't handle non-finite values.
Results may differ from a plain program's by a relative error of at most 0.000075.
Values sent between devices are 32-bit elements; how exact they have to be, the bound alone decides.
No kernel may reach another device: no remote copies, remote signals or barrier semaphores. Data moves between devices by JAX's collectives and lax.ppermute only.
A program may use at most 64 MiB of HBM per device.

v0:
```python
import jax
import jax.numpy as jnp
from jax import lax
from jax.sharding import PartitionSpec as P

PRECISE = lax.Precision.HIGHEST


def body(species_field, test_matrix):
    rows_here, span_second, span_third = species_field.shape
    columns = test_matrix.shape[0]
    unfolded = species_field.reshape(rows_here, span_second * span_third)
    sketch_matrix = test_matrix.reshape(columns, span_second * span_third)
    partial_sketch = lax.dot_general(
        unfolded, sketch_matrix, (((1,), (1,)), ((), ())), precision=PRECISE
    )
    sketch = lax.psum(partial_sketch, ("gy", "gz"))
    gram_matrix = lax.psum(jnp.dot(sketch.T, sketch, precision=PRECISE), "gx")
    cholesky_factor = jnp.linalg.cholesky(gram_matrix)
    factor_t = lax.linalg.triangular_solve(cholesky_factor, sketch.T, left_side=True, lower=True)
    product = jnp.dot(factor_t, unfolded, precision=PRECISE)
    return lax.psum_scatter(
        product.reshape(
            columns // lax.axis_size("gx") * lax.axis_size("gx"), span_second, span_third
        ),
        "gx",
        scatter_dimension=0,
        tiled=True,
    )


def solution(mesh):
    in_specs = (P("gx", "gy", "gz"), P(None, "gy", "gz"))
    out_specs = P("gx", "gy", "gz")
    return jax.shard_map(body, mesh=mesh, in_specs=in_specs, out_specs=out_specs, check_vma=False)
```

profile of v0, /device:TPU:0, one launch (start us, length us, event | category | flops | bytes accessed | tf_op | source)
XLA Modules:
  0.0 124.5 jit_solution(2674919262730058612)
XLA Ops:
  6.5 0.0 copy-start
  6.5 0.0 copy-start.1
  6.5 0.0 reduce-scatter.2.cloned.1.call-start
  6.5 1.1 copy-done
  7.7 5.0 %fusion.2 = f32[128,48]{0,1:T(8,128)S(1)} fusion(f32[128,32,128]{2,1,0:T(8,128)} %param.2, f32[48,32,128]{2,1,0:T(8,128)S(1)} %copy-done), kind=kOutput, calls=%fused_computation.3 | convolution fusion | flops 301989888 | bytes 2908160 | tf_op jit(solution)/shard_map/dot_general | solution.py:14
  12.7 63.0 %psum.14 = f32[128,48]{0,1:T(8,128)S(1)} all-reduce(f32[128,48]{0,1:T(8,128)S(1)} %fusion.2), channel_id=1, replica_groups=mesh['gx'=2,'gy'=4,'gz'=4] {'gy','gz'}, use_global_device_ids=true, to_apply=%region_0.0 | all-reduce | flops 6144 | bytes 49152 | tf_op jit(solution)/shard_map/psum | solution.py:17
  75.7 0.2 fusion.9
  75.8 8.3 %psum.15 = f32[48,48]{0,1:T(8,128)S(1)} all-reduce(f32[48,48]{0,1:T(8,128)S(1)} %fusion.9), channel_id=1, replica_groups=mesh['gx'=2,'gy'=4,'gz'=4] {'gx'}, use_global_device_ids=true, to_apply=%region_1.0 | all-reduce | flops 2304 | bytes 18432 | tf_op jit(solution)/shard_map/psum | solution.py:18
  84.1 0.1 copy.6
  84.2 4.4 %cholesky.16 = f32[48,48]{1,0:T(8,128)S(1)} custom-call(f32[48,48]{1,0:T(8,128)S(1)} %fusion.8), custom_call_target="Cholesky" | custom-call | tf_op jit(solution)/shard_map/jit(cholesky)/cholesky | solution.py:19
  88.6 0.6 compare_reduce_fusion
  89.3 0.7 fusion.6
  89.9 3.7 %custom-call.6 = f32[1,48,48]{1,2,0:T(8,128)S(1)} custom-call(f32[1,48,48]{2,1,0:T(8,128)S(1)} %fusion.6), custom_call_target="InvertDiagBlocksLowerTriangular" | custom-call | tf_op jit(solution)/shard_map/triangular_solve | solution.py:20
  93.6 0.2 convolution_bitcast_fusion
  93.8 0.0 copy-done.1
  93.8 3.0 %copy.18 = f32[16,8,32,128]{3,1,2,0:T(8,128)} copy(f32[16,8,32,128]{3,2,1,0:T(8,128)S(1)} %bitcast.26) | data formatting | bytes 4194304
  96.8 1.9 %copy.7 = f32[4096,128]{1,0:T(8,128)S(1)} copy(f32[4096,128]{0,1:T(8,128)} %bitcast.28) | data formatting | bytes 4194304 | tf_op jit(solution)/shard_map/dot_general | solution.py:21
  98.8 3.2 %fusion.10 = f32[48,32,128]{2,0,1:T(8,128)} fusion(f32[48,128,1]{1,0,2:T(8,128)S(1)} %convolution_bitcast_fusion, f32[32,128,128]{2,1,0:T(8,128)S(1)} %bitcast.27), kind=kOutput, calls=%fused_computation.16 | convolution fusion | flops 301989888 | bytes 2908160 | tf_op jit(solution)/shard_map/dot_general | solution.py:21
  101.9 0.0 reduce-scatter.2.cloned.1.call-update
  102.0 13.9 %reduce-scatter.2.cloned.1.call-done = f32[24,32,128]{2,0,1:T(8,128)} async-done(((f32[48,32,128]{2,0,1:T(8,128)}), f32[24,32,128]{2,0,1:T(8,128)}) %reduce-scatter.2.cloned.1.call-update) | async-done | bytes 393232 | tf_op jit(solution)/shard_map/reduce_scatter | solution.py:22
  115.8 1.8 %copy.8 = f32[24,32,128]{2,1,0:T(8,128)} copy(f32[24,32,128]{2,0,1:T(8,128)} %reduce-scatter.2.cloned.1.call-done) | data formatting | bytes 786432 | tf_op jit(solution)/shard_map/reduce_scatter | solution.py:22
  (2 shorter events, 0.0 us)
Async XLA Ops:
  6.5 1.1 copy-start
  6.5 87.3 %copy-start.1 = (f32[128,32,128]{2,1,0:T(8,128)S(1)}, f32[128,32,128]{2,1,0:T(8,128)}, u32[]{:S(2)}) copy-start(f32[128,32,128]{2,1,0:T(8,128)} %param.2) | copy-start | bytes 6291460
  6.5 109.3 %reduce-scatter.2.cloned.1.call-start = ((), (), s32[]{:S(2)}) async-start(), calls=%async_computation.1 | async-start | bytes 1179648 | tf_op jit(solution)/shard_map/reduce_scatter | solution.py:22
Sparse Core Ops, SparseCore 0:
  102.1 13.7 reduce-scatter.1
where the time goes:
time: 125 us; the launch traced here: 124 us
  blocking collectives  71.2 us (57%)
  waiting for transfers between devices  13.9 us (11%)
  between operations  13.5 us (11%)
  other arithmetic  9.4 us (8%)
  matrix products  8.58 us (7%)
  local copies, waits for them, and re-layouts  7.92 us (6%)
    psum x1, blocking collectives, body(): sketch = lax.psum(partial_sketch, ('gy', 'gz'))  63 us
    reduce_scatter x1, waiting for transfers between devices, body(): lax.psum_scatter(product.reshape(columns // lax.axis_size('gx') * lax.axi...  13.9 us
    psum x1, blocking collectives, body(): gram_matrix = lax.psum(jnp.dot(sketch.T, sketch, precision=PRECISE), 'gx')  8.29 us
    another operation x3, other arithmetic, body(): cholesky_factor = jnp.linalg.cholesky(gram_matrix)  5.05 us
    dot_general x1, matrix products, body(): lax.dot_general(unfolded, sketch_matrix, (((1,), (1,)), ((), ())), precis...  5.02 us
    another operation x2, other arithmetic, body(): lax.linalg.triangular_solve(cholesky_factor, sketch.T, left_side=True, lo...  4.34 us
    unnamed x5, local copies, waits for them, and re-layouts  4.12 us
    dot_general x1, matrix products, body(): product = jnp.dot(factor_t, unfolded, precision=PRECISE)  3.18 us
  transfers between devices with their start and end apart: 1, of which 1 were waited for; matrix products, arithmetic and copies ran while one was open for 0% of the time, Pallas kernels for 0%

commit v1 on v0

v1 whole, which is shorter than its diff:
```python
import functools

import jax
import jax.numpy as jnp
from jax import lax
from jax.experimental import pallas as pl
from jax.experimental.pallas import tpu as pltpu
from jax.sharding import PartitionSpec as P

F32, BF16 = jnp.float32, jnp.bfloat16
PRECISE = lax.Precision.HIGHEST
NT = (((1,), (1,)), ((), ()))
NN = (((1,), (0,)), ((), ()))
LANES, SUBLANES = 128, 8
VMEM_LIMIT = 48 << 20


def split(x, parts):
    terms = []
    for _ in range(parts - 1):
        terms.append(x.astype(BF16))
        x = x - terms[-1].astype(F32)
    return terms + [x.astype(BF16)]


def sketch_kernel(span, field_hbm, test_hbm, sketch_ref, pairs_ref, field, test, sems):
    rows, second, lanes = field_hbm.shape
    columns = test_hbm.shape[0]
    steps = second // span
    copies = []
    for step in range(steps):
        part = pl.ds(step * span, span)
        for which, (source, target) in enumerate(((field_hbm, field), (test_hbm, test))):
            copy = pltpu.make_async_copy(source.at[:, part], target.at[step], sems.at[which, step])
            copy.start()
            copies.append(copy)
    total = low = None
    for step in range(steps):
        copies[2 * step].wait()
        copies[2 * step + 1].wait()
        flat_field = field.at[step].reshape(rows * span, lanes)
        flat_test = test.at[step].reshape(columns * span, lanes)
        for pair in range(span // 2):
            x = jnp.concatenate([flat_field[pl.ds(2 * pair + q, rows, stride=span), :] for q in range(2)], axis=1)
            t = jnp.concatenate([flat_test[pl.ds(2 * pair + q, columns, stride=span), :] for q in range(2)], axis=1)
            x = split(x, 3)
            t = split(t, 3)
            weights = jnp.concatenate(x[:2], axis=0)
            pairs_ref[step * span // 2 + pair] = weights
            term = lax.dot_general(jnp.concatenate(t, axis=0), weights, NT, preferred_element_type=F32)
            rest = lax.dot_general(t[0], x[2], NT, preferred_element_type=F32)
            total = term if total is None else total + term
            low = rest if low is None else low + rest
    for part in reversed(range(3)):
        block = total[part * columns : (part + 1) * columns]
        low = low + block[:, rows:] + block[:, :rows] if part else (low + block[:, rows:]) + block[:, :rows]
    sketch_ref[...] = low


def partial_sketch(field, test):
    rows, second, lanes = field.shape
    columns = test.shape[0]
    span = SUBLANES
    steps = second // span
    return pl.pallas_call(
        functools.partial(sketch_kernel, span),
        in_specs=[pl.BlockSpec(memory_space=pl.ANY)] * 2,
        out_shape=[
            jax.ShapeDtypeStruct((columns, rows), F32),
            jax.ShapeDtypeStruct((second // 2, 2 * rows, 2 * lanes), BF16),
        ],
        scratch_shapes=[
            pltpu.VMEM((steps, rows, span, lanes), F32),
            pltpu.VMEM((steps, columns, span, lanes), F32),
            pltpu.SemaphoreType.DMA((2, steps)),
        ],
        compiler_params=pltpu.CompilerParams(vmem_limit_bytes=VMEM_LIMIT),
        name="partial_sketch",
    )(field, test)


def eliminate(gram, right):
    size = gram.shape[0]
    whole = jnp.concatenate([jnp.pad(gram, ((0, 0), (0, LANES - size))), right], axis=1)
    tiles = [whole[i : i + SUBLANES] for i in range(0, size, SUBLANES)]
    row_ids = lax.broadcasted_iota(jnp.int32, (SUBLANES, 1), 0)
    solved = []
    for k in range(size):
        first, at = divmod(k, SUBLANES)
        row = tiles[first][at : at + 1]
        pivot = row[:, k : k + 1]
        scaled = row * (1.0 / pivot)
        solved.append(row[:, LANES:] * lax.rsqrt(pivot))
        for i in range(first, len(tiles)):
            column = tiles[i][:, k : k + 1]
            if i == first:
                column = jnp.where(row_ids > at, column, 0.0)
            tiles[i] = tiles[i] - column * scaled
    return jnp.concatenate(solved, axis=0)


def project_kernel(axis, sketch_ref, pairs_ref, *out_refs):
    pairs, rows, lanes = pairs_ref.shape[0], pairs_ref.shape[1] // 2, pairs_ref.shape[2] // 2
    sketch = sketch_ref[...]
    gram = lax.dot_general(sketch, sketch, NT, precision=PRECISE, preferred_element_type=F32)
    factor = eliminate(gram, sketch[:, :rows])
    parties = len(out_refs)
    ranks = factor.shape[0] // parties
    me = lax.axis_index(axis)
    ordered = []
    for d in range(parties):
        rank_rows = factor[:ranks]
        for e in range(1, parties):
            rank_rows = jnp.where((me ^ d) == e, factor[e * ranks : (e + 1) * ranks], rank_rows)
        ordered.append(rank_rows)
    factor = jnp.concatenate(ordered, axis=0)
    high, low = split(factor, 2)
    left = jnp.concatenate([jnp.concatenate([high, high], axis=1), jnp.concatenate([low, low], axis=1)], axis=0)
    flat = [ref.reshape(ranks * 2 * pairs, lanes) for ref in out_refs]
    for pair in range(pairs):
        product = lax.dot_general(left, pairs_ref[pair], NN, preferred_element_type=F32)
        product = product[: factor.shape[0]] + product[factor.shape[0] :]
        for q in range(2):
            for d in range(parties):
                flat[d][pl.ds(2 * pair + q, ranks, stride=2 * pairs), :] = product[
                    d * ranks : (d + 1) * ranks, q * lanes : (q + 1) * lanes
                ]


def project(sketch, pairs, axis, parties):
    columns = sketch.shape[0]
    out = jax.ShapeDtypeStruct((columns // parties, 2 * pairs.shape[0], pairs.shape[2] // 2), F32)
    return pl.pallas_call(
        functools.partial(project_kernel, axis),
        out_shape=[out] * parties,
        compiler_params=pltpu.CompilerParams(vmem_limit_bytes=VMEM_LIMIT),
        name="project",
    )(sketch, pairs)


def exchange(x, axis, size, bit):
    return lax.ppermute(x, axis, [(i, i ^ bit) for i in range(size)])


def bits(size):
    return [1 << b for b in range(size.bit_length() - 1)]


def body(sizes, field, test):
    sketch, pairs = partial_sketch(field, test)
    for axis in ("gz", "gy"):
        for bit in bits(sizes[axis]):
            sketch = sketch + exchange(sketch, axis, sizes[axis], bit)
    for bit in bits(sizes["gx"]):
        sketch = jnp.concatenate([sketch, exchange(sketch, "gx", sizes["gx"], bit)], axis=1)
    products = project(sketch, pairs, "gx", sizes["gx"])
    core = products[0]
    for d in range(1, sizes["gx"]):
        core = core + exchange(products[d], "gx", sizes["gx"], d)
    return core


def solution(mesh):
    in_specs = (P("gx", "gy", "gz"), P(None, "gy", "gz"))
    out_specs = P("gx", "gy", "gz")
    step = functools.partial(body, dict(mesh.shape))
    return jax.shard_map(step, mesh=mesh, in_specs=in_specs, out_specs=out_specs, check_vma=False)
```

time: 125 us -> 37.2 us (0.30)
  blocking collectives: 71.2 us -> 0 us
  between operations: 13.5 us -> 0.03 us
  starting transfers between devices: 0.01 us -> 12.2 us
  matrix products: 8.58 us -> 0 us
  other arithmetic: 9.4 us -> 0.83 us
  Pallas kernels: 0 us -> 6.98 us
  local copies, waits for them, and re-layouts: 7.92 us -> 2.72 us
    psum x2 -> x0, blocking collectives: 71.2 us -> none  [the longest x1 63 us: body(): sketch = lax.psum(partial_sketch, ('gy', 'gz'))]
    ppermute x0 -> x6, waiting for transfers between devices: none -> 14.2 us  [exchange(): return lax.ppermute(x, axis, [(i, i ^ bit) for i in range(size)])]
    reduce_scatter x1 -> x0, waiting for transfers between devices: 13.9 us -> none  [body(): lax.psum_scatter(product.reshape(columns // lax.axis_size('gx') * lax.axi...]
    ppermute x0 -> x6, starting transfers between devices: none -> 12.2 us  [exchange(): return lax.ppermute(x, axis, [(i, i ^ bit) for i in range(size)])]
    another operation x5 -> x0, other arithmetic: 9.39 us -> none  [the longest x3 5.05 us: body(): cholesky_factor = jnp.linalg.cholesky(gram_matrix)]
    dot_general x3 -> x0, matrix products: 8.36 us -> none  [the longest x1 5.02 us: body(): lax.dot_general(unfolded, sketch_matrix, (((1,), (1,)), ((), ())), precis...]
    pallas_call x0 -> x2, Pallas kernels: none -> 6.98 us  [the longest x1 4.82 us: project(): pl.pallas_call(functools.partial(project_kernel, axis), out_shape=[out] *...]
    dot_general x1 -> x0, local copies, waits for them, and re-layouts: 1.91 us -> none  [body(): product = jnp.dot(factor_t, unfolded, precision=PRECISE)]
  transfers between devices with their start and end apart: 1 -> 6, of which waited for: 1 -> 6; matrix products, arithmetic and copies ran while one was open for 0% -> 0% of each run, Pallas kernels for 0% -> 0%
where the time goes in v1:
time: 37.2 us; the launch traced here: 37 us
  waiting for transfers between devices  14.2 us (38%)
  starting transfers between devices  12.2 us (33%)
  Pallas kernels  6.98 us (19%)
  local copies, waits for them, and re-layouts  2.72 us (7%)
  other arithmetic  0.83 us (2%)
    ppermute x6, waiting for transfers between devices, exchange(): return lax.ppermute(x, axis, [(i, i ^ bit) for i in range(size)])  14.2 us
    ppermute x6, starting transfers between devices, exchange(): return lax.ppermute(x, axis, [(i, i ^ bit) for i in range(size)])  12.2 us
    pallas_call x1, Pallas kernels, project(): pl.pallas_call(functools.partial(project_kernel, axis), out_shape=[out] *...  4.82 us
    unnamed x4, local copies, waits for them, and re-layouts  2.72 us
    pallas_call x1, Pallas kernels, partial_sketch(): pl.pallas_call(functools.partial(sketch_kernel, span), in_specs=[pl.Block...  2.16 us
    add x1, other arithmetic, body(): core = core + exchange(products[d], 'gx', sizes['gx'], d)  0.81 us
  transfers between devices with their start and end apart: 6, of which 6 were waited for; matrix products, arithmetic and copies ran while one was open for 0% of the time, Pallas kernels for 0%

profile of v1, /device:TPU:0, one launch (start us, length us, event | category | flops | bytes accessed | tf_op | source)
XLA Modules:
  0.0 37.0 jit_solution(9938662840449481038)
XLA Ops:
  0.0 0.0 copy-start
  0.0 1.6 %copy-done = f32[128,32,128]{2,1,0:T(8,128)S(1)} copy-done((f32[128,32,128]{2,1,0:T(8,128)S(1)}, f32[128,32,128]{2,1,0:T(8,128)}, u32[]{:S(2)}) %copy-start) | copy-done | bytes 2097176
  1.6 0.0 copy-start.1
  1.6 1.1 %copy-done.1 = f32[48,32,128]{2,1,0:T(8,128)S(1)} copy-done((f32[48,32,128]{2,1,0:T(8,128)S(1)}, f32[48,32,128]{2,1,0:T(8,128)}, u32[]{:S(2)}) %copy-start.1) | copy-done | bytes 786456
  2.7 2.2 %partial_sketch.1 = (f32[48,128]{1,0:T(8,128)S(1)}, bf16[16,256,256]{2,1,0:T(8,128)(2,1)S(1)}) custom-call(f32[128,32,128]{2,1,0:T(8,128)S(1)} %copy-done, f32[48,32,128]{2,1,0:T(8,128)S(1)} %copy-done.1), custom_call_target="tpu_custom_call" | custom-call | tf_op jit(solution)/shard_map/partial_sketch/pallas_call | solution.py:65
  4.9 0.5 %collective-permute-start = (f32[48,128]{1,0:T(8,128)S(1)}, f32[48,128]{1,0:T(8,128)S(1)}, u32[]{:S(2)}, u32[]{:S(2)}) collective-permute-start(f32[48,128]{1,0:T(8,128)S(1)} %get-tuple-element.9), channel_id=1, source_target_pairs={{0,1},{1,0},{2,3},{3,2},{4,5},{5,4},{6,7},{7,6},{8,9},{9,8},{10,11... | collective-permute-start | bytes 73736 | tf_op jit(solution)/shard_map/ppermute | solution.py:142
  5.4 0.8 %collective-permute-done = f32[48,128]{1,0:T(8,128)S(1)} collective-permute-done((f32[48,128]{1,0:T(8,128)S(1)}, f32[48,128]{1,0:T(8,128)S(1)}, u32[]{:S(2)}, u32[]{:S(2)}) %collective-permute-start) | collective-permute-done | bytes 24608 | tf_op jit(solution)/shard_map/ppermute | solution.py:142
  6.3 2.9 %collective-permute-start.1 = (f32[48,128]{1,0:T(8,128)S(1)}, f32[48,128]{1,0:T(8,128)S(1)}, u32[]{:S(2)}, u32[]{:S(2)}) collective-permute-start(f32[48,128]{1,0:T(8,128)S(1)} %add.15), channel_id=1, source_target_pairs={{0,2},{1,3},{2,0},{3,1},{4,6},{5,7},{6,4},{7,5},{8,10},{9,11},{10,... | collective-permute-start | bytes 73736 | tf_op jit(solution)/shard_map/ppermute | solution.py:142
  9.1 1.8 %collective-permute-done.1 = f32[48,128]{1,0:T(8,128)S(1)} collective-permute-done((f32[48,128]{1,0:T(8,128)S(1)}, f32[48,128]{1,0:T(8,128)S(1)}, u32[]{:S(2)}, u32[]{:S(2)}) %collective-permute-start.1) | collective-permute-done | bytes 24608 | tf_op jit(solution)/shard_map/ppermute | solution.py:142
  10.9 2.1 %collective-permute-start.2 = (f32[48,128]{1,0:T(8,128)S(1)}, f32[48,128]{1,0:T(8,128)S(1)}, u32[]{:S(2)}, u32[]{:S(2)}) collective-permute-start(f32[48,128]{1,0:T(8,128)S(1)} %add.16), channel_id=1, source_target_pairs={{0,4},{4,0},{8,12},{12,8},{1,5},{5,1},{9,13},{13,9},{2,6},{6,2},{1... | collective-permute-start | bytes 73736 | tf_op jit(solution)/shard_map/ppermute | solution.py:142
  13.0 1.8 %collective-permute-done.2 = f32[48,128]{1,0:T(8,128)S(1)} collective-permute-done((f32[48,128]{1,0:T(8,128)S(1)}, f32[48,128]{1,0:T(8,128)S(1)}, u32[]{:S(2)}, u32[]{:S(2)}) %collective-permute-start.2) | collective-permute-done | bytes 24608 | tf_op jit(solution)/shard_map/ppermute | solution.py:142
  14.8 3.0 %collective-permute-start.3 = (f32[48,128]{1,0:T(8,128)S(1)}, f32[48,128]{1,0:T(8,128)S(1)}, u32[]{:S(2)}, u32[]{:S(2)}) collective-permute-start(f32[48,128]{1,0:T(8,128)S(1)} %add.17), channel_id=1, source_target_pairs={{0,8},{4,12},{8,0},{12,4},{1,9},{5,13},{9,1},{13,5},{2,10},{6,14},... | collective-permute-start | bytes 73736 | tf_op jit(solution)/shard_map/ppermute | solution.py:142
  17.9 1.8 %collective-permute-done.3 = f32[48,128]{1,0:T(8,128)S(1)} collective-permute-done((f32[48,128]{1,0:T(8,128)S(1)}, f32[48,128]{1,0:T(8,128)S(1)}, u32[]{:S(2)}, u32[]{:S(2)}) %collective-permute-start.3) | collective-permute-done | bytes 24608 | tf_op jit(solution)/shard_map/ppermute | solution.py:142
  19.7 1.8 %collective-permute-start.4 = (f32[48,128]{1,0:T(8,128)S(1)}, f32[48,128]{1,0:T(8,128)S(1)}, u32[]{:S(2)}, u32[]{:S(2)}) collective-permute-start(f32[48,128]{1,0:T(8,128)S(1)} %add.18), channel_id=1, source_target_pairs={{0,16},{16,0},{1,17},{17,1},{2,18},{18,2},{3,19},{19,3},{4,20},{20... | collective-permute-start | bytes 73736 | tf_op jit(solution)/shard_map/ppermute | solution.py:142
  21.5 2.0 %collective-permute-done.4 = f32[48,128]{1,0:T(8,128)S(1)} collective-permute-done((f32[48,128]{1,0:T(8,128)S(1)}, f32[48,128]{1,0:T(8,128)S(1)}, u32[]{:S(2)}, u32[]{:S(2)}) %collective-permute-start.4) | collective-permute-done | bytes 24608 | tf_op jit(solution)/shard_map/ppermute | solution.py:142
  23.5 4.8 %project.1 = (f32[24,32,128]{2,1,0:T(8,128)S(1)}, f32[24,32,128]{2,1,0:T(8,128)S(1)}) custom-call(f32[48,256]{1,0:T(8,128)S(1)} %pad_maximum_fusion.sketch_ref, bf16[16,256,256]{2,1,0:T(8,128)(2,1)S(1)} %get-tuple-element.10.pairs_ref), custom_call_target="tpu_custom_call" | custom-call | tf_op jit(solution)/shard_map/project/pallas_call | solution.py:133
  28.3 1.9 %collective-permute-start.5 = (f32[24,32,128]{2,1,0:T(8,128)S(1)}, f32[24,32,128]{2,1,0:T(8,128)S(1)}, u32[]{:S(2)}, u32[]{:S(2)}) collective-permute-start(f32[24,32,128]{2,1,0:T(8,128)S(1)} %get-tuple-element.12), channel_id=1, source_target_pairs={{0,16},{16,0},{1,17},{17,1},{2,18},{18,2},{3,19},{19,3},{4,20},{20... | collective-permute-start | bytes 1179656 | tf_op jit(solution)/shard_map/ppermute | solution.py:142
  30.2 6.0 %collective-permute-done.5 = f32[24,32,128]{2,1,0:T(8,128)S(1)} collective-permute-done((f32[24,32,128]{2,1,0:T(8,128)S(1)}, f32[24,32,128]{2,1,0:T(8,128)S(1)}, u32[]{:S(2)}, u32[]{:S(2)}) %collective-permute-start.5) | collective-permute-done | bytes 393248 | tf_op jit(solution)/shard_map/ppermute | solution.py:142
  36.2 0.8 %add.19 = f32[24,32,128]{2,1,0:T(8,128)} add(f32[24,32,128]{2,1,0:T(8,128)S(1)} %get-tuple-element.11, f32[24,32,128]{2,1,0:T(8,128)S(1)} %collective-permute-done.5) | non-fusion elementwise | flops 98304 | bytes 1179648 | tf_op jit(solution)/shard_map/add | solution.py:159
  (5 shorter events, 0.0 us)
Async XLA Ops:
  0.0 1.6 %copy-start = (f32[128,32,128]{2,1,0:T(8,128)S(1)}, f32[128,32,128]{2,1,0:T(8,128)}, u32[]{:S(2)}) copy-start(f32[128,32,128]{2,1,0:T(8,128)} %field_hbm.1) | copy-start | bytes 6291460
  1.6 1.1 %copy-start.1 = (f32[48,32,128]{2,1,0:T(8,128)S(1)}, f32[48,32,128]{2,1,0:T(8,128)}, u32[]{:S(2)}) copy-start(f32[48,32,128]{2,1,0:T(8,128)} %test_hbm.1) | copy-start | bytes 2359300
  4.9 1.4 %collective-permute-start = (f32[48,128]{1,0:T(8,128)S(1)}, f32[48,128]{1,0:T(8,128)S(1)}, u32[]{:S(2)}, u32[]{:S(2)}) collective-permute-start(f32[48,128]{1,0:T(8,128)S(1)} %get-tuple-element.9), channel_id=1, source_target_pairs={{0,1},{1,0},{2,3},{3,2},{4,5},{5,4},{6,7},{7,6},{8,9},{9,8},{10,11... | collective-permute-start | bytes 73736 | tf_op jit(solution)/shard_map/ppermute | solution.py:142
  6.3 4.7 %collective-permute-start.1 = (f32[48,128]{1,0:T(8,128)S(1)}, f32[48,128]{1,0:T(8,128)S(1)}, u32[]{:S(2)}, u32[]{:S(2)}) collective-permute-start(f32[48,128]{1,0:T(8,128)S(1)} %add.15), channel_id=1, source_target_pairs={{0,2},{1,3},{2,0},{3,1},{4,6},{5,7},{6,4},{7,5},{8,10},{9,11},{10,... | collective-permute-start | bytes 73736 | tf_op jit(solution)/shard_map/ppermute | solution.py:142
  10.9 3.9 %collective-permute-start.2 = (f32[48,128]{1,0:T(8,128)S(1)}, f32[48,128]{1,0:T(8,128)S(1)}, u32[]{:S(2)}, u32[]{:S(2)}) collective-permute-start(f32[48,128]{1,0:T(8,128)S(1)} %add.16), channel_id=1, source_target_pairs={{0,4},{4,0},{8,12},{12,8},{1,5},{5,1},{9,13},{13,9},{2,6},{6,2},{1... | collective-permute-start | bytes 73736 | tf_op jit(solution)/shard_map/ppermute | solution.py:142
  14.8 4.8 %collective-permute-start.3 = (f32[48,128]{1,0:T(8,128)S(1)}, f32[48,128]{1,0:T(8,128)S(1)}, u32[]{:S(2)}, u32[]{:S(2)}) collective-permute-start(f32[48,128]{1,0:T(8,128)S(1)} %add.17), channel_id=1, source_target_pairs={{0,8},{4,12},{8,0},{12,4},{1,9},{5,13},{9,1},{13,5},{2,10},{6,14},... | collective-permute-start | bytes 73736 | tf_op jit(solution)/shard_map/ppermute | solution.py:142
  19.7 3.8 %collective-permute-start.4 = (f32[48,128]{1,0:T(8,128)S(1)}, f32[48,128]{1,0:T(8,128)S(1)}, u32[]{:S(2)}, u32[]{:S(2)}) collective-permute-start(f32[48,128]{1,0:T(8,128)S(1)} %add.18), channel_id=1, source_target_pairs={{0,16},{16,0},{1,17},{17,1},{2,18},{18,2},{3,19},{19,3},{4,20},{20... | collective-permute-start | bytes 73736 | tf_op jit(solution)/shard_map/ppermute | solution.py:142
  28.3 7.8 %collective-permute-start.5 = (f32[24,32,128]{2,1,0:T(8,128)S(1)}, f32[24,32,128]{2,1,0:T(8,128)S(1)}, u32[]{:S(2)}, u32[]{:S(2)}) collective-permute-start(f32[24,32,128]{2,1,0:T(8,128)S(1)} %get-tuple-element.12), channel_id=1, source_target_pairs={{0,16},{16,0},{1,17},{17,1},{2,18},{18,2},{3,19},{19,3},{4,20},{20... | collective-permute-start | bytes 1179656 | tf_op jit(solution)/shard_map/ppermute | solution.py:142

commit v2 on v1

--- a/solution.py
+++ b/solution.py
@@ -76,7 +76,7 @@
         ],
         compiler_params=pltpu.CompilerParams(vmem_limit_bytes=VMEM_LIMIT),
         name="partial_sketch",
-    )(field, test)
+    )(*(pltpu.with_memory_space_constraint(array, pltpu.HBM) for array in (field, test)))
 
 
 def eliminate(gram, right):

time: 37.2 us -> 35.1 us (0.944)
  local copies, waits for them, and re-layouts: 2.72 us -> 0 us
  Pallas kernels: 6.98 us -> 7.7 us
    unnamed x4 -> x0, local copies, waits for them, and re-layouts: 2.72 us -> none
    pallas_call x1, Pallas kernels: 2.16 us -> 2.87 us  [partial_sketch(): pl.pallas_call(functools.partial(sketch_kernel, span), in_specs=[pl.Block...]
where the time goes in v2:
time: 35.1 us; the launch traced here: 35 us
  waiting for transfers between devices  14.2 us (40%)
  starting transfers between devices  12.2 us (35%)
  Pallas kernels  7.7 us (22%)
  other arithmetic  0.83 us (2%)
    ppermute x6, waiting for transfers between devices, exchange(): return lax.ppermute(x, axis, [(i, i ^ bit) for i in range(size)])  14.2 us
    ppermute x6, starting transfers between devices, exchange(): return lax.ppermute(x, axis, [(i, i ^ bit) for i in range(size)])  12.2 us
    pallas_call x1, Pallas kernels, project(): pl.pallas_call(functools.partial(project_kernel, axis), out_shape=[out] *...  4.82 us
    pallas_call x1, Pallas kernels, partial_sketch(): pl.pallas_call(functools.partial(sketch_kernel, span), in_specs=[pl.Block...  2.87 us
    add x1, other arithmetic, body(): core = core + exchange(products[d], 'gx', sizes['gx'], d)  0.81 us
  transfers between devices with their start and end apart: 6, of which 6 were waited for; matrix products, arithmetic and copies ran while one was open for 0% of the time, Pallas kernels for 0%

profile of v2, /device:TPU:0, one launch (start us, length us, event | category | flops | bytes accessed | tf_op | source)
XLA Modules:
  0.0 35.0 jit_solution(3956234156695594125)
XLA Ops:
  0.0 2.9 %partial_sketch.1 = (f32[48,128]{1,0:T(8,128)S(1)}, bf16[16,256,256]{2,1,0:T(8,128)(2,1)S(1)}) custom-call(f32[128,32,128]{2,1,0:T(8,128)} %field_hbm.1, f32[48,32,128]{2,1,0:T(8,128)} %test_hbm.1), custom_call_target="tpu_custom_call" | custom-call | tf_op jit(solution)/shard_map/partial_sketch/pallas_call | solution.py:65
  2.9 0.5 %collective-permute-start = (f32[48,128]{1,0:T(8,128)S(1)}, f32[48,128]{1,0:T(8,128)S(1)}, u32[]{:S(2)}, u32[]{:S(2)}) collective-permute-start(f32[48,128]{1,0:T(8,128)S(1)} %get-tuple-element.9), channel_id=1, source_target_pairs={{0,1},{1,0},{2,3},{3,2},{4,5},{5,4},{6,7},{7,6},{8,9},{9,8},{10,11... | collective-permute-start | bytes 73736 | tf_op jit(solution)/shard_map/ppermute | solution.py:142
  3.4 0.8 %collective-permute-done = f32[48,128]{1,0:T(8,128)S(1)} collective-permute-done((f32[48,128]{1,0:T(8,128)S(1)}, f32[48,128]{1,0:T(8,128)S(1)}, u32[]{:S(2)}, u32[]{:S(2)}) %collective-permute-start) | collective-permute-done | bytes 24608 | tf_op jit(solution)/shard_map/ppermute | solution.py:142
  4.3 2.9 %collective-permute-start.1 = (f32[48,128]{1,0:T(8,128)S(1)}, f32[48,128]{1,0:T(8,128)S(1)}, u32[]{:S(2)}, u32[]{:S(2)}) collective-permute-start(f32[48,128]{1,0:T(8,128)S(1)} %add.15), channel_id=1, source_target_pairs={{0,2},{1,3},{2,0},{3,1},{4,6},{5,7},{6,4},{7,5},{8,10},{9,11},{10,... | collective-permute-start | bytes 73736 | tf_op jit(solution)/shard_map/ppermute | solution.py:142
  7.1 1.8 %collective-permute-done.1 = f32[48,128]{1,0:T(8,128)S(1)} collective-permute-done((f32[48,128]{1,0:T(8,128)S(1)}, f32[48,128]{1,0:T(8,128)S(1)}, u32[]{:S(2)}, u32[]{:S(2)}) %collective-permute-start.1) | collective-permute-done | bytes 24608 | tf_op jit(solution)/shard_map/ppermute | solution.py:142
  8.9 2.1 %collective-permute-start.2 = (f32[48,128]{1,0:T(8,128)S(1)}, f32[48,128]{1,0:T(8,128)S(1)}, u32[]{:S(2)}, u32[]{:S(2)}) collective-permute-start(f32[48,128]{1,0:T(8,128)S(1)} %add.16), channel_id=1, source_target_pairs={{0,4},{4,0},{8,12},{12,8},{1,5},{5,1},{9,13},{13,9},{2,6},{6,2},{1... | collective-permute-start | bytes 73736 | tf_op jit(solution)/shard_map/ppermute | solution.py:142
  11.0 1.8 %collective-permute-done.2 = f32[48,128]{1,0:T(8,128)S(1)} collective-permute-done((f32[48,128]{1,0:T(8,128)S(1)}, f32[48,128]{1,0:T(8,128)S(1)}, u32[]{:S(2)}, u32[]{:S(2)}) %collective-permute-start.2) | collective-permute-done | bytes 24608 | tf_op jit(solution)/shard_map/ppermute | solution.py:142
  12.8 3.0 %collective-permute-start.3 = (f32[48,128]{1,0:T(8,128)S(1)}, f32[48,128]{1,0:T(8,128)S(1)}, u32[]{:S(2)}, u32[]{:S(2)}) collective-permute-start(f32[48,128]{1,0:T(8,128)S(1)} %add.17), channel_id=1, source_target_pairs={{0,8},{4,12},{8,0},{12,4},{1,9},{5,13},{9,1},{13,5},{2,10},{6,14},... | collective-permute-start | bytes 73736 | tf_op jit(solution)/shard_map/ppermute | solution.py:142
  15.8 1.8 %collective-permute-done.3 = f32[48,128]{1,0:T(8,128)S(1)} collective-permute-done((f32[48,128]{1,0:T(8,128)S(1)}, f32[48,128]{1,0:T(8,128)S(1)}, u32[]{:S(2)}, u32[]{:S(2)}) %collective-permute-start.3) | collective-permute-done | bytes 24608 | tf_op jit(solution)/shard_map/ppermute | solution.py:142
  17.7 1.8 %collective-permute-start.4 = (f32[48,128]{1,0:T(8,128)S(1)}, f32[48,128]{1,0:T(8,128)S(1)}, u32[]{:S(2)}, u32[]{:S(2)}) collective-permute-start(f32[48,128]{1,0:T(8,128)S(1)} %add.18), channel_id=1, source_target_pairs={{0,16},{16,0},{1,17},{17,1},{2,18},{18,2},{3,19},{19,3},{4,20},{20... | collective-permute-start | bytes 73736 | tf_op jit(solution)/shard_map/ppermute | solution.py:142
  19.5 2.0 %collective-permute-done.4 = f32[48,128]{1,0:T(8,128)S(1)} collective-permute-done((f32[48,128]{1,0:T(8,128)S(1)}, f32[48,128]{1,0:T(8,128)S(1)}, u32[]{:S(2)}, u32[]{:S(2)}) %collective-permute-start.4) | collective-permute-done | bytes 24608 | tf_op jit(solution)/shard_map/ppermute | solution.py:142
  21.5 4.8 %project.1 = (f32[24,32,128]{2,1,0:T(8,128)S(1)}, f32[24,32,128]{2,1,0:T(8,128)S(1)}) custom-call(f32[48,256]{1,0:T(8,128)S(1)} %pad_maximum_fusion.sketch_ref, bf16[16,256,256]{2,1,0:T(8,128)(2,1)S(1)} %get-tuple-element.10.pairs_ref), custom_call_target="tpu_custom_call" | custom-call | tf_op jit(solution)/shard_map/project/pallas_call | solution.py:133
  26.3 1.9 %collective-permute-start.5 = (f32[24,32,128]{2,1,0:T(8,128)S(1)}, f32[24,32,128]{2,1,0:T(8,128)S(1)}, u32[]{:S(2)}, u32[]{:S(2)}) collective-permute-start(f32[24,32,128]{2,1,0:T(8,128)S(1)} %get-tuple-element.12), channel_id=1, source_target_pairs={{0,16},{16,0},{1,17},{17,1},{2,18},{18,2},{3,19},{19,3},{4,20},{20... | collective-permute-start | bytes 1179656 | tf_op jit(solution)/shard_map/ppermute | solution.py:142
  28.2 6.0 %collective-permute-done.5 = f32[24,32,128]{2,1,0:T(8,128)S(1)} collective-permute-done((f32[24,32,128]{2,1,0:T(8,128)S(1)}, f32[24,32,128]{2,1,0:T(8,128)S(1)}, u32[]{:S(2)}, u32[]{:S(2)}) %collective-permute-start.5) | collective-permute-done | bytes 393248 | tf_op jit(solution)/shard_map/ppermute | solution.py:142
  34.2 0.8 %add.19 = f32[24,32,128]{2,1,0:T(8,128)} add(f32[24,32,128]{2,1,0:T(8,128)S(1)} %get-tuple-element.11, f32[24,32,128]{2,1,0:T(8,128)S(1)} %collective-permute-done.5) | non-fusion elementwise | flops 98304 | bytes 1179648 | tf_op jit(solution)/shard_map/add | solution.py:159
  (5 shorter events, 0.0 us)
Async XLA Ops:
  2.9 1.4 %collective-permute-start = (f32[48,128]{1,0:T(8,128)S(1)}, f32[48,128]{1,0:T(8,128)S(1)}, u32[]{:S(2)}, u32[]{:S(2)}) collective-permute-start(f32[48,128]{1,0:T(8,128)S(1)} %get-tuple-element.9), channel_id=1, source_target_pairs={{0,1},{1,0},{2,3},{3,2},{4,5},{5,4},{6,7},{7,6},{8,9},{9,8},{10,11... | collective-permute-start | bytes 73736 | tf_op jit(solution)/shard_map/ppermute | solution.py:142
  4.3 4.7 %collective-permute-start.1 = (f32[48,128]{1,0:T(8,128)S(1)}, f32[48,128]{1,0:T(8,128)S(1)}, u32[]{:S(2)}, u32[]{:S(2)}) collective-permute-start(f32[48,128]{1,0:T(8,128)S(1)} %add.15), channel_id=1, source_target_pairs={{0,2},{1,3},{2,0},{3,1},{4,6},{5,7},{6,4},{7,5},{8,10},{9,11},{10,... | collective-permute-start | bytes 73736 | tf_op jit(solution)/shard_map/ppermute | solution.py:142
  8.9 3.9 %collective-permute-start.2 = (f32[48,128]{1,0:T(8,128)S(1)}, f32[48,128]{1,0:T(8,128)S(1)}, u32[]{:S(2)}, u32[]{:S(2)}) collective-permute-start(f32[48,128]{1,0:T(8,128)S(1)} %add.16), channel_id=1, source_target_pairs={{0,4},{4,0},{8,12},{12,8},{1,5},{5,1},{9,13},{13,9},{2,6},{6,2},{1... | collective-permute-start | bytes 73736 | tf_op jit(solution)/shard_map/ppermute | solution.py:142
  12.8 4.8 %collective-permute-start.3 = (f32[48,128]{1,0:T(8,128)S(1)}, f32[48,128]{1,0:T(8,128)S(1)}, u32[]{:S(2)}, u32[]{:S(2)}) collective-permute-start(f32[48,128]{1,0:T(8,128)S(1)} %add.17), channel_id=1, source_target_pairs={{0,8},{4,12},{8,0},{12,4},{1,9},{5,13},{9,1},{13,5},{2,10},{6,14},... | collective-permute-start | bytes 73736 | tf_op jit(solution)/shard_map/ppermute | solution.py:142
  17.7 3.8 %collective-permute-start.4 = (f32[48,128]{1,0:T(8,128)S(1)}, f32[48,128]{1,0:T(8,128)S(1)}, u32[]{:S(2)}, u32[]{:S(2)}) collective-permute-start(f32[48,128]{1,0:T(8,128)S(1)} %add.18), channel_id=1, source_target_pairs={{0,16},{16,0},{1,17},{17,1},{2,18},{18,2},{3,19},{19,3},{4,20},{20... | collective-permute-start | bytes 73736 | tf_op jit(solution)/shard_map/ppermute | solution.py:142
  26.3 7.8 %collective-permute-start.5 = (f32[24,32,128]{2,1,0:T(8,128)S(1)}, f32[24,32,128]{2,1,0:T(8,128)S(1)}, u32[]{:S(2)}, u32[]{:S(2)}) collective-permute-start(f32[24,32,128]{2,1,0:T(8,128)S(1)} %get-tuple-element.12), channel_id=1, source_target_pairs={{0,16},{16,0},{1,17},{17,1},{2,18},{18,2},{3,19},{19,3},{4,20},{20... | collective-permute-start | bytes 1179656 | tf_op jit(solution)/shard_map/ppermute | solution.py:142

commit v3 on v2

--- a/solution.py
+++ b/solution.py
@@ -80,31 +80,72 @@
 
 
 def eliminate(gram, right):
-    size = gram.shape[0]
+    size, width = gram.shape[0], LANES + right.shape[1]
     whole = jnp.concatenate([jnp.pad(gram, ((0, 0), (0, LANES - size))), right], axis=1)
     tiles = [whole[i : i + SUBLANES] for i in range(0, size, SUBLANES)]
-    row_ids = lax.broadcasted_iota(jnp.int32, (SUBLANES, 1), 0)
+    spread = lambda x: jnp.broadcast_to(x, (SUBLANES, LANES))
+    widen = lambda x: jnp.concatenate([x] * (width // LANES), axis=1)
+    block = range(SUBLANES)
     solved = []
-    for k in range(size):
-        first, at = divmod(k, SUBLANES)
-        row = tiles[first][at : at + 1]
-        pivot = row[:, k : k + 1]
-        scaled = row * (1.0 / pivot)
-        solved.append(row[:, LANES:] * lax.rsqrt(pivot))
-        for i in range(first, len(tiles)):
-            column = tiles[i][:, k : k + 1]
-            if i == first:
-                column = jnp.where(row_ids > at, column, 0.0)
-            tiles[i] = tiles[i] - column * scaled
+    for t, tile in enumerate(tiles):
+        start = t * SUBLANES
+        columns = [spread(tile[:, start + j : start + j + 1]) for j in block]
+        entry = {(i, j): spread(columns[j][i : i + 1]) for j in block for i in range(j, SUBLANES)}
+        inverse, lower = [], {}
+        for j in block:
+            inverse.append(1.0 / entry[j, j])
+            for i in range(j + 1, SUBLANES):
+                lower[i, j] = entry[i, j] * inverse[j]
+            for m in range(j + 1, SUBLANES):
+                for i in range(m, SUBLANES):
+                    entry[i, m] = entry[i, m] - lower[i, j] * entry[m, j]
+        lower = {at: widen(x) for at, x in lower.items()}
+        reduced = []
+        for i in block:
+            row = jnp.broadcast_to(tile[i : i + 1], (SUBLANES, width))
+            for j in range(i):
+                row = row - lower[i, j] * reduced[j]
+            reduced.append(row)
+            solved.append(row[:1, LANES:] * widen(lax.rsqrt(entry[i, i]))[:1, LANES:])
+        if t == len(tiles) - 1:
+            break
+        scaled = [None] * SUBLANES
+        for i in reversed(block):
+            row = reduced[i] * widen(inverse[i])
+            for j in range(i + 1, SUBLANES):
+                row = row - lower[j, i] * scaled[j]
+            scaled[i] = row
+        for later in range(t + 1, len(tiles)):
+            rest = tiles[later]
+            for j in block:
+                rest = rest - tiles[later][:, start + j : start + j + 1] * scaled[j]
+            tiles[later] = rest
     return jnp.concatenate(solved, axis=0)
 
 
-def project_kernel(axis, sketch_ref, pairs_ref, *out_refs):
-    pairs, rows, lanes = pairs_ref.shape[0], pairs_ref.shape[1] // 2, pairs_ref.shape[2] // 2
+def multiply(factor, pairs_ref, first, out_refs):
+    count = factor.shape[0]
+    ranks, span, lanes = out_refs[0].shape
+    high, low = (part.astype(F32) for part in split(factor, 2))
+    left = jnp.concatenate([high, low], axis=0)
+    left = jnp.concatenate([left, left], axis=1).astype(BF16)
+    flat = [ref.reshape(ranks * span, lanes) for ref in out_refs]
+    for pair in range(span // 2):
+        product = lax.dot_general(left, pairs_ref[first + pair], NN, preferred_element_type=F32)
+        product = product[:count] + product[count:]
+        for q in range(2):
+            for d, ref in enumerate(flat):
+                ref[pl.ds(2 * pair + q, ranks, stride=span), :] = product[
+                    d * ranks : (d + 1) * ranks, q * lanes : (q + 1) * lanes
+                ]
+
+
+def solve_kernel(axis, sketch_ref, pairs_ref, factor_ref, *out_refs):
+    rows = pairs_ref.shape[1] // 2
     sketch = sketch_ref[...]
     gram = lax.dot_general(sketch, sketch, NT, precision=PRECISE, preferred_element_type=F32)
     factor = eliminate(gram, sketch[:, :rows])
-    parties = len(out_refs)
+    parties = len(out_refs) + 1
     ranks = factor.shape[0] // parties
     me = lax.axis_index(axis)
     ordered = []
@@ -113,29 +154,56 @@
         for e in range(1, parties):
             rank_rows = jnp.where((me ^ d) == e, factor[e * ranks : (e + 1) * ranks], rank_rows)
         ordered.append(rank_rows)
-    factor = jnp.concatenate(ordered, axis=0)
-    high, low = split(factor, 2)
-    left = jnp.concatenate([jnp.concatenate([high, high], axis=1), jnp.concatenate([low, low], axis=1)], axis=0)
-    flat = [ref.reshape(ranks * 2 * pairs, lanes) for ref in out_refs]
-    for pair in range(pairs):
-        product = lax.dot_general(left, pairs_ref[pair], NN, preferred_element_type=F32)
-        product = product[: factor.shape[0]] + product[factor.shape[0] :]
-        for q in range(2):
-            for d in range(parties):
-                flat[d][pl.ds(2 * pair + q, ranks, stride=2 * pairs), :] = product[
-                    d * ranks : (d + 1) * ranks, q * lanes : (q + 1) * lanes
-                ]
-
-
-def project(sketch, pairs, axis, parties):
-    columns = sketch.shape[0]
-    out = jax.ShapeDtypeStruct((columns // parties, 2 * pairs.shape[0], pairs.shape[2] // 2), F32)
-    return pl.pallas_call(
-        functools.partial(project_kernel, axis),
-        out_shape=[out] * parties,
-        compiler_params=pltpu.CompilerParams(vmem_limit_bytes=VMEM_LIMIT),
-        name="project",
+    factor_ref[...] = jnp.concatenate(ordered, axis=0)
+    multiply(jnp.concatenate(ordered[1:], axis=0), pairs_ref, 0, out_refs)
+
+
+def more_kernel(first, begin, factor_ref, pairs_ref, *out_refs):
+    ranks = out_refs[0].shape[0]
+    multiply(factor_ref[begin : begin + ranks * len(out_refs), :], pairs_ref, first, out_refs)
+
+
+def add_kernel(own_ref, *refs):
+    *others, out_ref = refs
+    place = 0
+    span = others[0].shape[1]
+    parties = len(others) * span // own_ref.shape[1]
+    for chunk in range(len(others) // parties):
+        part = pl.ds(chunk * span, span)
+        total = own_ref[:, part, :]
+        for ref in others[chunk * parties : (chunk + 1) * parties]:
+            total = total + ref[...]
+        out_ref[:, part, :] = total
+
+
+PARAMS = pltpu.CompilerParams(vmem_limit_bytes=VMEM_LIMIT)
+
+
+def project(sketch, pairs, axis, parties, chunks):
+    columns, rows = sketch.shape[0], pairs.shape[1] // 2
+    lanes = pairs.shape[2] // 2
+    ranks, second = columns // parties, 2 * pairs.shape[0]
+    chunk = jax.ShapeDtypeStruct((ranks, second // chunks, lanes), F32)
+    factor, *sent = pl.pallas_call(
+        functools.partial(solve_kernel, axis),
+        out_shape=[jax.ShapeDtypeStruct((columns, rows), F32)] + [chunk] * (parties - 1),
+        compiler_params=PARAMS,
+        name="solve",
     )(sketch, pairs)
+    received = [exchange(x, axis, parties, d + 1) for d, x in enumerate(sent)]
+    for step in range(1, chunks):
+        sent = pl.pallas_call(
+            functools.partial(more_kernel, step * (second // chunks) // 2, ranks),
+            out_shape=[chunk] * (parties - 1),
+            compiler_params=PARAMS,
+            name="others_ranks",
+        )(factor, pairs)
+        received += [exchange(x, axis, parties, d + 1) for d, x in enumerate(sent)]
+    own = jax.ShapeDtypeStruct((ranks, second, lanes), F32)
+    (core,) = pl.pallas_call(
+        functools.partial(more_kernel, 0, 0), out_shape=[own], compiler_params=PARAMS, name="own_ranks"
+    )(factor, pairs)
+    return pl.pallas_call(add_kernel, out_shape=own, compiler_params=PARAMS, name="add_ranks")(core, *received)
 
 
 def exchange(x, axis, size, bit):
@@ -153,11 +221,7 @@
             sketch = sketch + exchange(sketch, axis, sizes[axis], bit)
     for bit in bits(sizes["gx"]):
         sketch = jnp.concatenate([sketch, exchange(sketch, "gx", sizes["gx"], bit)], axis=1)
-    products = project(sketch, pairs, "gx", sizes["gx"])
-    core = products[0]
-    for d in range(1, sizes["gx"]):
-        core = core + exchange(products[d], "gx", sizes["gx"], d)
-    return core
+    return project(sketch, pairs, "gx", sizes["gx"], 2)
 
 
 def solution(mesh):

time: 35.1 us -> 32.7 us (0.932)
  Pallas kernels: 7.7 us -> 6.6 us
  other arithmetic: 0.83 us -> 0.02 us
  waiting for transfers between devices: 14.2 us -> 13.5 us
    pallas_call x1 -> x4, Pallas kernels: 4.82 us -> 3.73 us  [the longest x1 2.08 us: project(): pl.pallas_call(functools.partial(solve_kernel, axis), out_shape=[jax.Shap...]
    add x1 -> x0, other arithmetic: 0.81 us -> none  [body(): core = core + exchange(products[d], 'gx', sizes['gx'], d)]
    ppermute x6 -> x7, waiting for transfers between devices: 14.2 us -> 13.5 us  [exchange(): return lax.ppermute(x, axis, [(i, i ^ bit) for i in range(size)])]
    ppermute x6 -> x7, starting transfers between devices: 12.2 us -> 12.4 us  [exchange(): return lax.ppermute(x, axis, [(i, i ^ bit) for i in range(size)])]
  transfers between devices with their start and end apart: 6 -> 7, of which waited for: 6 -> 7; matrix products, arithmetic and copies ran while one was open for 0% -> 0% of each run, Pallas kernels for 0% -> 2%
where the time goes in v3:
time: 32.7 us; the launch traced here: 32.5 us
  waiting for transfers between devices  13.5 us (41%)
  starting transfers between devices  12.4 us (38%)
  Pallas kernels  6.6 us (20%)
    ppermute x7, waiting for transfers between devices, exchange(): return lax.ppermute(x, axis, [(i, i ^ bit) for i in range(size)])  13.5 us
    ppermute x7, starting transfers between devices, exchange(): return lax.ppermute(x, axis, [(i, i ^ bit) for i in range(size)])  12.4 us
    pallas_call x1, Pallas kernels, partial_sketch(): pl.pallas_call(functools.partial(sketch_kernel, span), in_specs=[pl.Block...  2.87 us
    pallas_call x1, Pallas kernels, project(): pl.pallas_call(functools.partial(solve_kernel, axis), out_shape=[jax.Shap...  2.08 us
    pallas_call x1, Pallas kernels, project(): pl.pallas_call(add_kernel, out_shape=own, compiler_params=PARAMS, name='a...  0.81 us
  transfers between devices with their start and end apart: 7, of which 7 were waited for; matrix products, arithmetic and copies ran while one was open for 0% of the time, Pallas kernels for 2%

profile of v3, /device:TPU:0, one launch (start us, length us, event | category | flops | bytes accessed | tf_op | source)
XLA Modules:
  0.0 32.5 jit_solution(14369357269337056269)
XLA Ops:
  0.0 2.9 %partial_sketch.1 = (f32[48,128]{1,0:T(8,128)S(1)}, bf16[16,256,256]{2,1,0:T(8,128)(2,1)S(1)}) custom-call(f32[128,32,128]{2,1,0:T(8,128)} %field_hbm.1, f32[48,32,128]{2,1,0:T(8,128)} %test_hbm.1), custom_call_target="tpu_custom_call" | custom-call | tf_op jit(solution)/shard_map/partial_sketch/pallas_call | solution.py:65
  2.9 0.5 %collective-permute-start = (f32[48,128]{1,0:T(8,128)S(1)}, f32[48,128]{1,0:T(8,128)S(1)}, u32[]{:S(2)}, u32[]{:S(2)}) collective-permute-start(f32[48,128]{1,0:T(8,128)S(1)} %get-tuple-element.9), channel_id=1, source_target_pairs={{0,1},{1,0},{2,3},{3,2},{4,5},{5,4},{6,7},{7,6},{8,9},{9,8},{10,11... | collective-permute-start | bytes 73736 | tf_op jit(solution)/shard_map/ppermute | solution.py:210
  3.4 0.8 %collective-permute-done = f32[48,128]{1,0:T(8,128)S(1)} collective-permute-done((f32[48,128]{1,0:T(8,128)S(1)}, f32[48,128]{1,0:T(8,128)S(1)}, u32[]{:S(2)}, u32[]{:S(2)}) %collective-permute-start) | collective-permute-done | bytes 24608 | tf_op jit(solution)/shard_map/ppermute | solution.py:210
  4.3 2.9 %collective-permute-start.1 = (f32[48,128]{1,0:T(8,128)S(1)}, f32[48,128]{1,0:T(8,128)S(1)}, u32[]{:S(2)}, u32[]{:S(2)}) collective-permute-start(f32[48,128]{1,0:T(8,128)S(1)} %add.12), channel_id=1, source_target_pairs={{0,2},{1,3},{2,0},{3,1},{4,6},{5,7},{6,4},{7,5},{8,10},{9,11},{10,... | collective-permute-start | bytes 73736 | tf_op jit(solution)/shard_map/ppermute | solution.py:210
  7.1 1.8 %collective-permute-done.1 = f32[48,128]{1,0:T(8,128)S(1)} collective-permute-done((f32[48,128]{1,0:T(8,128)S(1)}, f32[48,128]{1,0:T(8,128)S(1)}, u32[]{:S(2)}, u32[]{:S(2)}) %collective-permute-start.1) | collective-permute-done | bytes 24608 | tf_op jit(solution)/shard_map/ppermute | solution.py:210
  8.9 2.1 %collective-permute-start.2 = (f32[48,128]{1,0:T(8,128)S(1)}, f32[48,128]{1,0:T(8,128)S(1)}, u32[]{:S(2)}, u32[]{:S(2)}) collective-permute-start(f32[48,128]{1,0:T(8,128)S(1)} %add.13), channel_id=1, source_target_pairs={{0,4},{4,0},{8,12},{12,8},{1,5},{5,1},{9,13},{13,9},{2,6},{6,2},{1... | collective-permute-start | bytes 73736 | tf_op jit(solution)/shard_map/ppermute | solution.py:210
  11.0 1.8 %collective-permute-done.2 = f32[48,128]{1,0:T(8,128)S(1)} collective-permute-done((f32[48,128]{1,0:T(8,128)S(1)}, f32[48,128]{1,0:T(8,128)S(1)}, u32[]{:S(2)}, u32[]{:S(2)}) %collective-permute-start.2) | collective-permute-done | bytes 24608 | tf_op jit(solution)/shard_map/ppermute | solution.py:210
  12.8 3.0 %collective-permute-start.3 = (f32[48,128]{1,0:T(8,128)S(1)}, f32[48,128]{1,0:T(8,128)S(1)}, u32[]{:S(2)}, u32[]{:S(2)}) collective-permute-start(f32[48,128]{1,0:T(8,128)S(1)} %add.14), channel_id=1, source_target_pairs={{0,8},{4,12},{8,0},{12,4},{1,9},{5,13},{9,1},{13,5},{2,10},{6,14},... | collective-permute-start | bytes 73736 | tf_op jit(solution)/shard_map/ppermute | solution.py:210
  15.8 1.8 %collective-permute-done.3 = f32[48,128]{1,0:T(8,128)S(1)} collective-permute-done((f32[48,128]{1,0:T(8,128)S(1)}, f32[48,128]{1,0:T(8,128)S(1)}, u32[]{:S(2)}, u32[]{:S(2)}) %collective-permute-start.3) | collective-permute-done | bytes 24608 | tf_op jit(solution)/shard_map/ppermute | solution.py:210
  17.7 1.8 %collective-permute-start.4 = (f32[48,128]{1,0:T(8,128)S(1)}, f32[48,128]{1,0:T(8,128)S(1)}, u32[]{:S(2)}, u32[]{:S(2)}) collective-permute-start(f32[48,128]{1,0:T(8,128)S(1)} %add.15), channel_id=1, source_target_pairs={{0,16},{16,0},{1,17},{17,1},{2,18},{18,2},{3,19},{19,3},{4,20},{20... | collective-permute-start | bytes 73736 | tf_op jit(solution)/shard_map/ppermute | solution.py:210
  19.5 2.0 %collective-permute-done.4 = f32[48,128]{1,0:T(8,128)S(1)} collective-permute-done((f32[48,128]{1,0:T(8,128)S(1)}, f32[48,128]{1,0:T(8,128)S(1)}, u32[]{:S(2)}, u32[]{:S(2)}) %collective-permute-start.4) | collective-permute-done | bytes 24608 | tf_op jit(solution)/shard_map/ppermute | solution.py:210
  21.5 2.1 %solve.1 = (f32[48,128]{1,0:T(8,128)S(1)}, f32[24,16,128]{2,1,0:T(8,128)S(1)}) custom-call(f32[48,256]{1,0:T(8,128)S(1)} %pad_maximum_fusion.sketch_ref, bf16[16,256,256]{2,1,0:T(8,128)(2,1)S(1)} %get-tuple-element.10.pairs_ref), custom_call_target="tpu_custom_call" | custom-call | tf_op jit(solution)/shard_map/solve/pallas_call | solution.py:187
  23.6 0.3 others_ranks.1
  23.9 1.9 %collective-permute-start.6 = (f32[24,16,128]{2,1,0:T(8,128)S(1)}, f32[24,16,128]{2,1,0:T(8,128)S(1)}, u32[]{:S(2)}, u32[]{:S(2)}) collective-permute-start(f32[24,16,128]{2,1,0:T(8,128)S(1)} %others_ranks.1), channel_id=1, source_target_pairs={{0,16},{16,0},{1,17},{17,1},{2,18},{18,2},{3,19},{19,3},{4,20},{20... | collective-permute-start | bytes 589832 | tf_op jit(solution)/shard_map/ppermute | solution.py:210
  25.8 0.2 collective-permute-start.5
  26.0 0.5 %own_ranks.1.own_ref = f32[24,32,128]{2,1,0:T(8,128)S(1)} custom-call(f32[48,128]{1,0:T(8,128)S(1)} %get-tuple-element.11.factor_ref, bf16[16,256,256]{2,1,0:T(8,128)(2,1)S(1)} %get-tuple-element.10.pairs_ref), custom_call_target="tpu_custom_call" | custom-call | tf_op jit(solution)/shard_map/own_ranks/pallas_call | solution.py:203
  26.5 3.1 %collective-permute-done.6.refs_1_ = f32[24,16,128]{2,1,0:T(8,128)S(1)} collective-permute-done((f32[24,16,128]{2,1,0:T(8,128)S(1)}, f32[24,16,128]{2,1,0:T(8,128)S(1)}, u32[]{:S(2)}, u32[]{:S(2)}) %collective-permute-start.6) | collective-permute-done | bytes 196640 | tf_op jit(solution)/shard_map/ppermute | solution.py:210
  29.6 2.1 %collective-permute-done.5.refs_0_ = f32[24,16,128]{2,1,0:T(8,128)S(1)} collective-permute-done((f32[24,16,128]{2,1,0:T(8,128)S(1)}, f32[24,16,128]{2,1,0:T(8,128)S(1)}, u32[]{:S(2)}, u32[]{:S(2)}) %collective-permute-start.5) | collective-permute-done | bytes 196640 | tf_op jit(solution)/shard_map/ppermute | solution.py:210
  31.7 0.8 %add_ranks.1 = f32[24,32,128]{2,1,0:T(8,128)} custom-call(f32[24,32,128]{2,1,0:T(8,128)S(1)} %own_ranks.1.own_ref, f32[24,16,128]{2,1,0:T(8,128)S(1)} %collective-permute-done.5.refs_0_, f32[24,16,128]{2,1,0:T(8,128)S(1)} %collective-permute-done.6.refs_1_), custom_call_target="tpu_custom_call" | custom-call | tf_op jit(solution)/shard_map/add_ranks/pallas_call | solution.py:206
  (5 shorter events, 0.0 us)
Async XLA Ops:
  2.9 1.4 %collective-permute-start = (f32[48,128]{1,0:T(8,128)S(1)}, f32[48,128]{1,0:T(8,128)S(1)}, u32[]{:S(2)}, u32[]{:S(2)}) collective-permute-start(f32[48,128]{1,0:T(8,128)S(1)} %get-tuple-element.9), channel_id=1, source_target_pairs={{0,1},{1,0},{2,3},{3,2},{4,5},{5,4},{6,7},{7,6},{8,9},{9,8},{10,11... | collective-permute-start | bytes 73736 | tf_op jit(solution)/shard_map/ppermute | solution.py:210
  4.3 4.7 %collective-permute-start.1 = (f32[48,128]{1,0:T(8,128)S(1)}, f32[48,128]{1,0:T(8,128)S(1)}, u32[]{:S(2)}, u32[]{:S(2)}) collective-permute-start(f32[48,128]{1,0:T(8,128)S(1)} %add.12), channel_id=1, source_target_pairs={{0,2},{1,3},{2,0},{3,1},{4,6},{5,7},{6,4},{7,5},{8,10},{9,11},{10,... | collective-permute-start | bytes 73736 | tf_op jit(solution)/shard_map/ppermute | solution.py:210
  8.9 3.9 %collective-permute-start.2 = (f32[48,128]{1,0:T(8,128)S(1)}, f32[48,128]{1,0:T(8,128)S(1)}, u32[]{:S(2)}, u32[]{:S(2)}) collective-permute-start(f32[48,128]{1,0:T(8,128)S(1)} %add.13), channel_id=1, source_target_pairs={{0,4},{4,0},{8,12},{12,8},{1,5},{5,1},{9,13},{13,9},{2,6},{6,2},{1... | collective-permute-start | bytes 73736 | tf_op jit(solution)/shard_map/ppermute | solution.py:210
  12.8 4.8 %collective-permute-start.3 = (f32[48,128]{1,0:T(8,128)S(1)}, f32[48,128]{1,0:T(8,128)S(1)}, u32[]{:S(2)}, u32[]{:S(2)}) collective-permute-start(f32[48,128]{1,0:T(8,128)S(1)} %add.14), channel_id=1, source_target_pairs={{0,8},{4,12},{8,0},{12,4},{1,9},{5,13},{9,1},{13,5},{2,10},{6,14},... | collective-permute-start | bytes 73736 | tf_op jit(solution)/shard_map/ppermute | solution.py:210
  17.7 3.8 %collective-permute-start.4 = (f32[48,128]{1,0:T(8,128)S(1)}, f32[48,128]{1,0:T(8,128)S(1)}, u32[]{:S(2)}, u32[]{:S(2)}) collective-permute-start(f32[48,128]{1,0:T(8,128)S(1)} %add.15), channel_id=1, source_target_pairs={{0,16},{16,0},{1,17},{17,1},{2,18},{18,2},{3,19},{19,3},{4,20},{20... | collective-permute-start | bytes 73736 | tf_op jit(solution)/shard_map/ppermute | solution.py:210
  23.9 5.7 %collective-permute-start.6 = (f32[24,16,128]{2,1,0:T(8,128)S(1)}, f32[24,16,128]{2,1,0:T(8,128)S(1)}, u32[]{:S(2)}, u32[]{:S(2)}) collective-permute-start(f32[24,16,128]{2,1,0:T(8,128)S(1)} %others_ranks.1), channel_id=1, source_target_pairs={{0,16},{16,0},{1,17},{17,1},{2,18},{18,2},{3,19},{19,3},{4,20},{20... | collective-permute-start | bytes 589832 | tf_op jit(solution)/shard_map/ppermute | solution.py:210
  25.8 5.9 %collective-permute-start.5 = (f32[24,16,128]{2,1,0:T(8,128)S(1)}, f32[24,16,128]{2,1,0:T(8,128)S(1)}, u32[]{:S(2)}, u32[]{:S(2)}) collective-permute-start(f32[24,16,128]{2,1,0:T(8,128)S(1)} %get-tuple-element.12), channel_id=1, source_target_pairs={{0,16},{16,0},{1,17},{17,1},{2,18},{18,2},{3,19},{19,3},{4,20},{20... | collective-permute-start | bytes 589832 | tf_op jit(solution)/shard_map/ppermute | solution.py:210

commit v4 on v3

--- a/solution.py
+++ b/solution.py
@@ -81,7 +81,7 @@
 
 def eliminate(gram, right):
     size, width = gram.shape[0], LANES + right.shape[1]
-    whole = jnp.concatenate([jnp.pad(gram, ((0, 0), (0, LANES - size))), right], axis=1)
+    whole = jnp.concatenate([gram, jnp.zeros((size, LANES - size), F32), right], axis=1)
     tiles = [whole[i : i + SUBLANES] for i in range(0, size, SUBLANES)]
     spread = lambda x: jnp.broadcast_to(x, (SUBLANES, LANES))
     widen = lambda x: jnp.concatenate([x] * (width // LANES), axis=1)
@@ -123,16 +123,24 @@
     return jnp.concatenate(solved, axis=0)
 
 
-def multiply(factor, pairs_ref, first, out_refs):
-    count = factor.shape[0]
-    ranks, span, lanes = out_refs[0].shape
+def twice(factor):
     high, low = (part.astype(F32) for part in split(factor, 2))
     left = jnp.concatenate([high, low], axis=0)
-    left = jnp.concatenate([left, left], axis=1).astype(BF16)
+    return jnp.concatenate([left, left], axis=1).astype(BF16)
+
+
+def times(left, pair):
+    product = lax.dot_general(left, pair, NN, preferred_element_type=F32)
+    half = left.shape[0] // 2
+    return product[:half] + product[half:]
+
+
+def multiply(factor, pairs_ref, first, out_refs):
+    ranks, span, lanes = out_refs[0].shape
+    left = twice(factor)
     flat = [ref.reshape(ranks * span, lanes) for ref in out_refs]
     for pair in range(span // 2):
-        product = lax.dot_general(left, pairs_ref[first + pair], NN, preferred_element_type=F32)
-        product = product[:count] + product[count:]
+        product = times(left, pairs_ref[first + pair])
         for q in range(2):
             for d, ref in enumerate(flat):
                 ref[pl.ds(2 * pair + q, ranks, stride=span), :] = product[
@@ -158,70 +166,100 @@
     multiply(jnp.concatenate(ordered[1:], axis=0), pairs_ref, 0, out_refs)
 
 
-def more_kernel(first, begin, factor_ref, pairs_ref, *out_refs):
+def ranks_kernel(first, begin, factor_ref, pairs_ref, *out_refs):
     ranks = out_refs[0].shape[0]
     multiply(factor_ref[begin : begin + ranks * len(out_refs), :], pairs_ref, first, out_refs)
 
 
-def add_kernel(own_ref, *refs):
-    *others, out_ref = refs
-    place = 0
-    span = others[0].shape[1]
-    parties = len(others) * span // own_ref.shape[1]
-    for chunk in range(len(others) // parties):
-        part = pl.ds(chunk * span, span)
-        total = own_ref[:, part, :]
-        for ref in others[chunk * parties : (chunk + 1) * parties]:
-            total = total + ref[...]
-        out_ref[:, part, :] = total
+def add_kernel(parties, own_ref, *refs):
+    *others, out_hbm, total_ref, sems = refs
+    copies, place = [], 0
+    for chunk in range(len(others) // (parties - 1)):
+        parts = others[chunk * (parties - 1) : (chunk + 1) * (parties - 1)]
+        here = pl.ds(place, parts[0].shape[1])
+        total = own_ref[:, here, :]
+        for part in parts:
+            total = total + part[...]
+        total_ref[:, here, :] = total
+        copies.append(pltpu.make_async_copy(total_ref.at[:, here], out_hbm.at[:, here], sems.at[chunk]))
+        copies[-1].start()
+        place += parts[0].shape[1]
+    for copy in copies:
+        copy.wait()
 
 
 PARAMS = pltpu.CompilerParams(vmem_limit_bytes=VMEM_LIMIT)
-
-
-def project(sketch, pairs, axis, parties, chunks):
+COST = pl.CostEstimate(flops=1 << 30, bytes_accessed=1 << 25, transcendentals=0)
+
+
+def project(sketch, pairs, sizes, spans):
+    parties = sizes["gx"]
     columns, rows = sketch.shape[0], pairs.shape[1] // 2
     lanes = pairs.shape[2] // 2
     ranks, second = columns // parties, 2 * pairs.shape[0]
-    chunk = jax.ShapeDtypeStruct((ranks, second // chunks, lanes), F32)
+    chunks = [jax.ShapeDtypeStruct((ranks, span, lanes), F32) for span in spans]
     factor, *sent = pl.pallas_call(
-        functools.partial(solve_kernel, axis),
-        out_shape=[jax.ShapeDtypeStruct((columns, rows), F32)] + [chunk] * (parties - 1),
+        functools.partial(solve_kernel, "gx"),
+        out_shape=[jax.ShapeDtypeStruct((columns, rows), F32)] + [chunks[0]] * (parties - 1),
         compiler_params=PARAMS,
+        cost_estimate=COST,
         name="solve",
     )(sketch, pairs)
-    received = [exchange(x, axis, parties, d + 1) for d, x in enumerate(sent)]
-    for step in range(1, chunks):
+    received = [exchange(x, sizes, gx=d + 1) for d, x in enumerate(sent)]
+    place = spans[0]
+    for chunk in chunks[1:]:
         sent = pl.pallas_call(
-            functools.partial(more_kernel, step * (second // chunks) // 2, ranks),
+            functools.partial(ranks_kernel, place // 2, ranks),
             out_shape=[chunk] * (parties - 1),
             compiler_params=PARAMS,
+            cost_estimate=COST,
             name="others_ranks",
         )(factor, pairs)
-        received += [exchange(x, axis, parties, d + 1) for d, x in enumerate(sent)]
+        received += [exchange(x, sizes, gx=d + 1) for d, x in enumerate(sent)]
+        place += chunk.shape[1]
     own = jax.ShapeDtypeStruct((ranks, second, lanes), F32)
     (core,) = pl.pallas_call(
-        functools.partial(more_kernel, 0, 0), out_shape=[own], compiler_params=PARAMS, name="own_ranks"
+        functools.partial(ranks_kernel, 0, 0),
+        out_shape=[own],
+        compiler_params=PARAMS,
+        cost_estimate=pl.CostEstimate(flops=1 << 20, bytes_accessed=1 << 22, transcendentals=0),
+        name="own_ranks",
     )(factor, pairs)
-    return pl.pallas_call(add_kernel, out_shape=own, compiler_params=PARAMS, name="add_ranks")(core, *received)
-
-
-def exchange(x, axis, size, bit):
-    return lax.ppermute(x, axis, [(i, i ^ bit) for i in range(size)])
-
-
-def bits(size):
+    return pl.pallas_call(
+        functools.partial(add_kernel, parties),
+        out_shape=own,
+        out_specs=pl.BlockSpec(memory_space=pl.ANY),
+        scratch_shapes=[pltpu.VMEM(own.shape, F32), pltpu.SemaphoreType.DMA((len(chunks),))],
+        compiler_params=PARAMS,
+        name="add_ranks",
+    )(core, *received)
+
+
+AXES = ("gx", "gy", "gz")
+
+
+def exchange(x, sizes, **bits):
+    order = [(gx, gy, gz) for gx in range(sizes["gx"]) for gy in range(sizes["gy"]) for gz in range(sizes["gz"])]
+    place = {index: at for at, index in enumerate(order)}
+    moves = [bits.get(axis, 0) for axis in AXES]
+    pairs = [(at, place[tuple(i ^ move for i, move in zip(index, moves))]) for at, index in enumerate(order)]
+    return lax.ppermute(x, AXES, pairs)
+
+
+def steps_of(size):
     return [1 << b for b in range(size.bit_length() - 1)]
 
 
 def body(sizes, field, test):
+    second = field.shape[1]
     sketch, pairs = partial_sketch(field, test)
-    for axis in ("gz", "gy"):
-        for bit in bits(sizes[axis]):
-            sketch = sketch + exchange(sketch, axis, sizes[axis], bit)
-    for bit in bits(sizes["gx"]):
-        sketch = jnp.concatenate([sketch, exchange(sketch, "gx", sizes["gx"], bit)], axis=1)
-    return project(sketch, pairs, "gx", sizes["gx"], 2)
+    for bit in steps_of(sizes["gz"]):
+        sketch = sketch + exchange(sketch, sizes, gz=bit | 1)
+    for bit in steps_of(sizes["gy"]):
+        sketch = sketch + exchange(sketch, sizes, gy=bit)
+    for bit in steps_of(sizes["gx"]):
+        sketch = jnp.concatenate([sketch, exchange(sketch, sizes, gx=bit)], axis=1)
+    return project(sketch, pairs, sizes, (3 * second // 4, second // 4))
 
 
 def solution(mesh):

time: 32.7 us -> 32.1 us (0.982)
  transfers between devices with their start and end apart: 7 -> 7, of which waited for: 7 -> 6; matrix products, arithmetic and copies ran while one was open for 0% -> 0% of each run, Pallas kernels for 2% -> 2%
where the time goes in v4:
time: 32.1 us; the launch traced here: 32 us
  waiting for transfers between devices  13.2 us (41%)
  starting transfers between devices  12.2 us (38%)
  Pallas kernels  6.58 us (20%)
    ppermute x7, waiting for transfers between devices, exchange(): return lax.ppermute(x, AXES, pairs)  13.2 us
    ppermute x7, starting transfers between devices, exchange(): return lax.ppermute(x, AXES, pairs)  12.2 us
    pallas_call x1, Pallas kernels, partial_sketch(): pl.pallas_call(functools.partial(sketch_kernel, span), in_specs=[pl.Block...  2.87 us
    pallas_call x1, Pallas kernels, project(): pl.pallas_call(functools.partial(solve_kernel, 'gx'), out_shape=[jax.Shap...  2.17 us
    pallas_call x1, Pallas kernels, project(): pl.pallas_call(functools.partial(add_kernel, parties), out_shape=own, out...  0.8 us
  transfers between devices with their start and end apart: 7, of which 6 were waited for; matrix products, arithmetic and copies ran while one was open for 0% of the time, Pallas kernels for 2%

profile of v4, /device:TPU:0, one launch (start us, length us, event | category | flops | bytes accessed | tf_op | source)
XLA Modules:
  0.0 32.0 jit_solution(16092259599962902283)
XLA Ops:
  0.0 2.9 %partial_sketch.1 = (f32[48,128]{1,0:T(8,128)S(1)}, bf16[16,256,256]{2,1,0:T(8,128)(2,1)S(1)}) custom-call(f32[128,32,128]{2,1,0:T(8,128)} %field_hbm.1, f32[48,32,128]{2,1,0:T(8,128)} %test_hbm.1), custom_call_target="tpu_custom_call" | custom-call | tf_op jit(solution)/shard_map/partial_sketch/pallas_call | solution.py:65
  2.9 0.5 %collective-permute-start = (f32[48,128]{1,0:T(8,128)S(1)}, f32[48,128]{1,0:T(8,128)S(1)}, u32[]{:S(2)}, u32[]{:S(2)}) collective-permute-start(f32[48,128]{1,0:T(8,128)S(1)} %get-tuple-element.9), channel_id=1, source_target_pairs={{0,1},{1,0},{2,3},{3,2},{4,5},{5,4},{6,7},{7,6},{8,9},{9,8},{10,11... | collective-permute-start | bytes 73736 | tf_op jit(solution)/shard_map/ppermute | solution.py:246
  3.4 0.8 %collective-permute-done = f32[48,128]{1,0:T(8,128)S(1)} collective-permute-done((f32[48,128]{1,0:T(8,128)S(1)}, f32[48,128]{1,0:T(8,128)S(1)}, u32[]{:S(2)}, u32[]{:S(2)}) %collective-permute-start) | collective-permute-done | bytes 24608 | tf_op jit(solution)/shard_map/ppermute | solution.py:246
  4.3 2.6 %collective-permute-start.1 = (f32[48,128]{1,0:T(8,128)S(1)}, f32[48,128]{1,0:T(8,128)S(1)}, u32[]{:S(2)}, u32[]{:S(2)}) collective-permute-start(f32[48,128]{1,0:T(8,128)S(1)} %add.12), channel_id=1, source_target_pairs={{0,3},{1,2},{2,1},{3,0},{4,7},{5,6},{6,5},{7,4},{8,11},{9,10},{10,... | collective-permute-start | bytes 73736 | tf_op jit(solution)/shard_map/ppermute | solution.py:246
  6.9 1.5 %collective-permute-done.1 = f32[48,128]{1,0:T(8,128)S(1)} collective-permute-done((f32[48,128]{1,0:T(8,128)S(1)}, f32[48,128]{1,0:T(8,128)S(1)}, u32[]{:S(2)}, u32[]{:S(2)}) %collective-permute-start.1) | collective-permute-done | bytes 24608 | tf_op jit(solution)/shard_map/ppermute | solution.py:246
  8.4 2.0 %collective-permute-start.2 = (f32[48,128]{1,0:T(8,128)S(1)}, f32[48,128]{1,0:T(8,128)S(1)}, u32[]{:S(2)}, u32[]{:S(2)}) collective-permute-start(f32[48,128]{1,0:T(8,128)S(1)} %add.13), channel_id=1, source_target_pairs={{0,4},{1,5},{2,6},{3,7},{4,0},{5,1},{6,2},{7,3},{8,12},{9,13},{10,... | collective-permute-start | bytes 73736 | tf_op jit(solution)/shard_map/ppermute | solution.py:246
  10.4 1.8 %collective-permute-done.2 = f32[48,128]{1,0:T(8,128)S(1)} collective-permute-done((f32[48,128]{1,0:T(8,128)S(1)}, f32[48,128]{1,0:T(8,128)S(1)}, u32[]{:S(2)}, u32[]{:S(2)}) %collective-permute-start.2) | collective-permute-done | bytes 24608 | tf_op jit(solution)/shard_map/ppermute | solution.py:246
  12.2 3.0 %collective-permute-start.3 = (f32[48,128]{1,0:T(8,128)S(1)}, f32[48,128]{1,0:T(8,128)S(1)}, u32[]{:S(2)}, u32[]{:S(2)}) collective-permute-start(f32[48,128]{1,0:T(8,128)S(1)} %add.14), channel_id=1, source_target_pairs={{0,8},{1,9},{2,10},{3,11},{4,12},{5,13},{6,14},{7,15},{8,0},{9,1},... | collective-permute-start | bytes 73736 | tf_op jit(solution)/shard_map/ppermute | solution.py:246
  15.3 1.8 %collective-permute-done.3 = f32[48,128]{1,0:T(8,128)S(1)} collective-permute-done((f32[48,128]{1,0:T(8,128)S(1)}, f32[48,128]{1,0:T(8,128)S(1)}, u32[]{:S(2)}, u32[]{:S(2)}) %collective-permute-start.3) | collective-permute-done | bytes 24608 | tf_op jit(solution)/shard_map/ppermute | solution.py:246
  17.1 1.8 %collective-permute-start.4 = (f32[48,128]{1,0:T(8,128)S(1)}, f32[48,128]{1,0:T(8,128)S(1)}, u32[]{:S(2)}, u32[]{:S(2)}) collective-permute-start(f32[48,128]{1,0:T(8,128)S(1)} %add.15), channel_id=1, source_target_pairs={{0,16},{1,17},{2,18},{3,19},{4,20},{5,21},{6,22},{7,23},{8,24},{9,... | collective-permute-start | bytes 73736 | tf_op jit(solution)/shard_map/ppermute | solution.py:246
  18.9 2.0 %collective-permute-done.4 = f32[48,128]{1,0:T(8,128)S(1)} collective-permute-done((f32[48,128]{1,0:T(8,128)S(1)}, f32[48,128]{1,0:T(8,128)S(1)}, u32[]{:S(2)}, u32[]{:S(2)}) %collective-permute-start.4) | collective-permute-done | bytes 24608 | tf_op jit(solution)/shard_map/ppermute | solution.py:246
  20.9 2.2 %solve.1 = (f32[48,128]{1,0:T(8,128)S(1)}, f32[24,24,128]{2,1,0:T(8,128)S(1)}) custom-call(f32[48,256]{1,0:T(8,128)S(1)} %pad_maximum_fusion.sketch_ref, bf16[16,256,256]{2,1,0:T(8,128)(2,1)S(1)} %get-tuple-element.10.pairs_ref), custom_call_target="tpu_custom_call" | custom-call | flops 1073741824 | bytes 33554432 | tf_op jit(solution)/shard_map/solve/pallas_call | solution.py:201
  23.1 1.9 %collective-permute-start.5 = (f32[24,24,128]{2,1,0:T(8,128)S(1)}, f32[24,24,128]{2,1,0:T(8,128)S(1)}, u32[]{:S(2)}, u32[]{:S(2)}) collective-permute-start(f32[24,24,128]{2,1,0:T(8,128)S(1)} %get-tuple-element.12), channel_id=1, source_target_pairs={{0,16},{1,17},{2,18},{3,19},{4,20},{5,21},{6,22},{7,23},{8,24},{9,... | collective-permute-start | bytes 884744 | tf_op jit(solution)/shard_map/ppermute | solution.py:246
  25.0 0.2 others_ranks.1
  25.2 0.3 collective-permute-start.6
  25.5 0.5 %own_ranks.1.own_ref = f32[24,32,128]{2,1,0:T(8,128)S(1)} custom-call(f32[48,128]{1,0:T(8,128)S(1)} %get-tuple-element.11.factor_ref, bf16[16,256,256]{2,1,0:T(8,128)(2,1)S(1)} %get-tuple-element.10.pairs_ref), custom_call_target="tpu_custom_call" | custom-call | flops 1048576 | bytes 4194304 | tf_op jit(solution)/shard_map/own_ranks/pallas_call | solution.py:221
  26.0 5.2 %collective-permute-done.6.refs_1_ = f32[24,8,128]{2,1,0:T(8,128)S(1)} collective-permute-done((f32[24,8,128]{2,1,0:T(8,128)S(1)}, f32[24,8,128]{2,1,0:T(8,128)S(1)}, u32[]{:S(2)}, u32[]{:S(2)}) %collective-permute-start.6) | collective-permute-done | bytes 98336 | tf_op jit(solution)/shard_map/ppermute | solution.py:246
  31.2 0.0 collective-permute-done.5.refs_0_
  31.2 0.8 %add_ranks.1 = f32[24,32,128]{2,1,0:T(8,128)} custom-call(f32[24,32,128]{2,1,0:T(8,128)S(1)} %own_ranks.1.own_ref, f32[24,24,128]{2,1,0:T(8,128)S(1)} %collective-permute-done.5.refs_0_, f32[24,8,128]{2,1,0:T(8,128)S(1)} %collective-permute-done.6.refs_1_), custom_call_target="tpu_custom_call" | custom-call | tf_op jit(solution)/shard_map/add_ranks/pallas_call | solution.py:228
  (5 shorter events, 0.0 us)
Async XLA Ops:
  2.9 1.4 %collective-permute-start = (f32[48,128]{1,0:T(8,128)S(1)}, f32[48,128]{1,0:T(8,128)S(1)}, u32[]{:S(2)}, u32[]{:S(2)}) collective-permute-start(f32[48,128]{1,0:T(8,128)S(1)} %get-tuple-element.9), channel_id=1, source_target_pairs={{0,1},{1,0},{2,3},{3,2},{4,5},{5,4},{6,7},{7,6},{8,9},{9,8},{10,11... | collective-permute-start | bytes 73736 | tf_op jit(solution)/shard_map/ppermute | solution.py:246
  4.3 4.2 %collective-permute-start.1 = (f32[48,128]{1,0:T(8,128)S(1)}, f32[48,128]{1,0:T(8,128)S(1)}, u32[]{:S(2)}, u32[]{:S(2)}) collective-permute-start(f32[48,128]{1,0:T(8,128)S(1)} %add.12), channel_id=1, source_target_pairs={{0,3},{1,2},{2,1},{3,0},{4,7},{5,6},{6,5},{7,4},{8,11},{9,10},{10,... | collective-permute-start | bytes 73736 | tf_op jit(solution)/shard_map/ppermute | solution.py:246
  8.4 3.8 %collective-permute-start.2 = (f32[48,128]{1,0:T(8,128)S(1)}, f32[48,128]{1,0:T(8,128)S(1)}, u32[]{:S(2)}, u32[]{:S(2)}) collective-permute-start(f32[48,128]{1,0:T(8,128)S(1)} %add.13), channel_id=1, source_target_pairs={{0,4},{1,5},{2,6},{3,7},{4,0},{5,1},{6,2},{7,3},{8,12},{9,13},{10,... | collective-permute-start | bytes 73736 | tf_op jit(solution)/shard_map/ppermute | solution.py:246
  12.2 4.8 %collective-permute-start.3 = (f32[48,128]{1,0:T(8,128)S(1)}, f32[48,128]{1,0:T(8,128)S(1)}, u32[]{:S(2)}, u32[]{:S(2)}) collective-permute-start(f32[48,128]{1,0:T(8,128)S(1)} %add.14), channel_id=1, source_target_pairs={{0,8},{1,9},{2,10},{3,11},{4,12},{5,13},{6,14},{7,15},{8,0},{9,1},... | collective-permute-start | bytes 73736 | tf_op jit(solution)/shard_map/ppermute | solution.py:246
  17.1 3.8 %collective-permute-start.4 = (f32[48,128]{1,0:T(8,128)S(1)}, f32[48,128]{1,0:T(8,128)S(1)}, u32[]{:S(2)}, u32[]{:S(2)}) collective-permute-start(f32[48,128]{1,0:T(8,128)S(1)} %add.15), channel_id=1, source_target_pairs={{0,16},{1,17},{2,18},{3,19},{4,20},{5,21},{6,22},{7,23},{8,24},{9,... | collective-permute-start | bytes 73736 | tf_op jit(solution)/shard_map/ppermute | solution.py:246
  23.1 8.1 %collective-permute-start.5 = (f32[24,24,128]{2,1,0:T(8,128)S(1)}, f32[24,24,128]{2,1,0:T(8,128)S(1)}, u32[]{:S(2)}, u32[]{:S(2)}) collective-permute-start(f32[24,24,128]{2,1,0:T(8,128)S(1)} %get-tuple-element.12), channel_id=1, source_target_pairs={{0,16},{1,17},{2,18},{3,19},{4,20},{5,21},{6,22},{7,23},{8,24},{9,... | collective-permute-start | bytes 884744 | tf_op jit(solution)/shard_map/ppermute | solution.py:246
  25.2 6.0 %collective-permute-start.6 = (f32[24,8,128]{2,1,0:T(8,128)S(1)}, f32[24,8,128]{2,1,0:T(8,128)S(1)}, u32[]{:S(2)}, u32[]{:S(2)}) collective-permute-start(f32[24,8,128]{2,1,0:T(8,128)S(1)} %others_ranks.1), channel_id=1, source_target_pairs={{0,16},{1,17},{2,18},{3,19},{4,20},{5,21},{6,22},{7,23},{8,24},{9,... | collective-permute-start | bytes 294920 | tf_op jit(solution)/shard_map/ppermute | solution.py:246

commit v5 on v4

--- a/solution.py
+++ b/solution.py
@@ -79,7 +79,7 @@
     )(*(pltpu.with_memory_space_constraint(array, pltpu.HBM) for array in (field, test)))
 
 
-def eliminate(gram, right):
+def eliminate(gram, right, spread_ref):
     size, width = gram.shape[0], LANES + right.shape[1]
     whole = jnp.concatenate([gram, jnp.zeros((size, LANES - size), F32), right], axis=1)
     tiles = [whole[i : i + SUBLANES] for i in range(0, size, SUBLANES)]
@@ -89,8 +89,9 @@
     solved = []
     for t, tile in enumerate(tiles):
         start = t * SUBLANES
-        columns = [spread(tile[:, start + j : start + j + 1]) for j in block]
-        entry = {(i, j): spread(columns[j][i : i + 1]) for j in block for i in range(j, SUBLANES)}
+        for j in block:
+            spread_ref[t, j] = spread(tile[:, start + j : start + j + 1])
+        entry = {(i, j): spread(spread_ref[t, j, i : i + 1, :]) for j in block for i in range(j, SUBLANES)}
         inverse, lower = [], {}
         for j in block:
             inverse.append(1.0 / entry[j, j])
@@ -148,11 +149,12 @@
                 ]
 
 
-def solve_kernel(axis, sketch_ref, pairs_ref, factor_ref, *out_refs):
+def solve_kernel(axis, sketch_ref, pairs_ref, factor_ref, *refs):
+    *out_refs, spread_ref = refs
     rows = pairs_ref.shape[1] // 2
     sketch = sketch_ref[...]
     gram = lax.dot_general(sketch, sketch, NT, precision=PRECISE, preferred_element_type=F32)
-    factor = eliminate(gram, sketch[:, :rows])
+    factor = eliminate(gram, sketch[:, :rows], spread_ref)
     parties = len(out_refs) + 1
     ranks = factor.shape[0] // parties
     me = lax.axis_index(axis)
@@ -201,6 +203,7 @@
     factor, *sent = pl.pallas_call(
         functools.partial(solve_kernel, "gx"),
         out_shape=[jax.ShapeDtypeStruct((columns, rows), F32)] + [chunks[0]] * (parties - 1),
+        scratch_shapes=[pltpu.VMEM((columns // SUBLANES, SUBLANES, SUBLANES, LANES), F32)],
         compiler_params=PARAMS,
         cost_estimate=COST,
         name="solve",

time: 32.1 us -> 31.8 us (level)
  no operation moved by 1% of the time
where the time goes in v5:
time: 31.8 us; the launch traced here: 31.7 us
  waiting for transfers between devices  13.2 us (42%)
  starting transfers between devices  12.2 us (38%)
  Pallas kernels  6.3 us (20%)
    ppermute x7, waiting for transfers between devices, exchange(): return lax.ppermute(x, AXES, pairs)  13.2 us
    ppermute x7, starting transfers between devices, exchange(): return lax.ppermute(x, AXES, pairs)  12.2 us
    pallas_call x1, Pallas kernels, partial_sketch(): pl.pallas_call(functools.partial(sketch_kernel, span), in_specs=[pl.Block...  2.87 us
    pallas_call x1, Pallas kernels, project(): pl.pallas_call(functools.partial(solve_kernel, 'gx'), out_shape=[jax.Shap...  1.89 us
    pallas_call x1, Pallas kernels, project(): pl.pallas_call(functools.partial(add_kernel, parties), out_shape=own, out...  0.8 us
  transfers between devices with their start and end apart: 7, of which 6 were waited for; matrix products, arithmetic and copies ran while one was open for 0% of the time, Pallas kernels for 2%

profile of v5, /device:TPU:0, one launch (start us, length us, event | category | flops | bytes accessed | tf_op | source)
XLA Modules:
  0.0 31.7 jit_solution(8259107665462789212)
XLA Ops:
  0.0 2.9 %partial_sketch.1 = (f32[48,128]{1,0:T(8,128)S(1)}, bf16[16,256,256]{2,1,0:T(8,128)(2,1)S(1)}) custom-call(f32[128,32,128]{2,1,0:T(8,128)} %field_hbm.1, f32[48,32,128]{2,1,0:T(8,128)} %test_hbm.1), custom_call_target="tpu_custom_call" | custom-call | tf_op jit(solution)/shard_map/partial_sketch/pallas_call | solution.py:65
  2.9 0.5 %collective-permute-start = (f32[48,128]{1,0:T(8,128)S(1)}, f32[48,128]{1,0:T(8,128)S(1)}, u32[]{:S(2)}, u32[]{:S(2)}) collective-permute-start(f32[48,128]{1,0:T(8,128)S(1)} %get-tuple-element.9), channel_id=1, source_target_pairs={{0,1},{1,0},{2,3},{3,2},{4,5},{5,4},{6,7},{7,6},{8,9},{9,8},{10,11... | collective-permute-start | bytes 73736 | tf_op jit(solution)/shard_map/ppermute | solution.py:249
  3.4 0.8 %collective-permute-done = f32[48,128]{1,0:T(8,128)S(1)} collective-permute-done((f32[48,128]{1,0:T(8,128)S(1)}, f32[48,128]{1,0:T(8,128)S(1)}, u32[]{:S(2)}, u32[]{:S(2)}) %collective-permute-start) | collective-permute-done | bytes 24608 | tf_op jit(solution)/shard_map/ppermute | solution.py:249
  4.3 2.6 %collective-permute-start.1 = (f32[48,128]{1,0:T(8,128)S(1)}, f32[48,128]{1,0:T(8,128)S(1)}, u32[]{:S(2)}, u32[]{:S(2)}) collective-permute-start(f32[48,128]{1,0:T(8,128)S(1)} %add.12), channel_id=1, source_target_pairs={{0,3},{1,2},{2,1},{3,0},{4,7},{5,6},{6,5},{7,4},{8,11},{9,10},{10,... | collective-permute-start | bytes 73736 | tf_op jit(solution)/shard_map/ppermute | solution.py:249
  6.9 1.5 %collective-permute-done.1 = f32[48,128]{1,0:T(8,128)S(1)} collective-permute-done((f32[48,128]{1,0:T(8,128)S(1)}, f32[48,128]{1,0:T(8,128)S(1)}, u32[]{:S(2)}, u32[]{:S(2)}) %collective-permute-start.1) | collective-permute-done | bytes 24608 | tf_op jit(solution)/shard_map/ppermute | solution.py:249
  8.4 2.0 %collective-permute-start.2 = (f32[48,128]{1,0:T(8,128)S(1)}, f32[48,128]{1,0:T(8,128)S(1)}, u32[]{:S(2)}, u32[]{:S(2)}) collective-permute-start(f32[48,128]{1,0:T(8,128)S(1)} %add.13), channel_id=1, source_target_pairs={{0,4},{1,5},{2,6},{3,7},{4,0},{5,1},{6,2},{7,3},{8,12},{9,13},{10,... | collective-permute-start | bytes 73736 | tf_op jit(solution)/shard_map/ppermute | solution.py:249
  10.4 1.8 %collective-permute-done.2 = f32[48,128]{1,0:T(8,128)S(1)} collective-permute-done((f32[48,128]{1,0:T(8,128)S(1)}, f32[48,128]{1,0:T(8,128)S(1)}, u32[]{:S(2)}, u32[]{:S(2)}) %collective-permute-start.2) | collective-permute-done | bytes 24608 | tf_op jit(solution)/shard_map/ppermute | solution.py:249
  12.2 3.0 %collective-permute-start.3 = (f32[48,128]{1,0:T(8,128)S(1)}, f32[48,128]{1,0:T(8,128)S(1)}, u32[]{:S(2)}, u32[]{:S(2)}) collective-permute-start(f32[48,128]{1,0:T(8,128)S(1)} %add.14), channel_id=1, source_target_pairs={{0,8},{1,9},{2,10},{3,11},{4,12},{5,13},{6,14},{7,15},{8,0},{9,1},... | collective-permute-start | bytes 73736 | tf_op jit(solution)/shard_map/ppermute | solution.py:249
  15.3 1.8 %collective-permute-done.3 = f32[48,128]{1,0:T(8,128)S(1)} collective-permute-done((f32[48,128]{1,0:T(8,128)S(1)}, f32[48,128]{1,0:T(8,128)S(1)}, u32[]{:S(2)}, u32[]{:S(2)}) %collective-permute-start.3) | collective-permute-done | bytes 24608 | tf_op jit(solution)/shard_map/ppermute | solution.py:249
  17.1 1.8 %collective-permute-start.4 = (f32[48,128]{1,0:T(8,128)S(1)}, f32[48,128]{1,0:T(8,128)S(1)}, u32[]{:S(2)}, u32[]{:S(2)}) collective-permute-start(f32[48,128]{1,0:T(8,128)S(1)} %add.15), channel_id=1, source_target_pairs={{0,16},{1,17},{2,18},{3,19},{4,20},{5,21},{6,22},{7,23},{8,24},{9,... | collective-permute-start | bytes 73736 | tf_op jit(solution)/shard_map/ppermute | solution.py:249
  18.9 2.0 %collective-permute-done.4 = f32[48,128]{1,0:T(8,128)S(1)} collective-permute-done((f32[48,128]{1,0:T(8,128)S(1)}, f32[48,128]{1,0:T(8,128)S(1)}, u32[]{:S(2)}, u32[]{:S(2)}) %collective-permute-start.4) | collective-permute-done | bytes 24608 | tf_op jit(solution)/shard_map/ppermute | solution.py:249
  20.9 1.9 %solve.1 = (f32[48,128]{1,0:T(8,128)S(1)}, f32[24,24,128]{2,1,0:T(8,128)S(1)}) custom-call(f32[48,256]{1,0:T(8,128)S(1)} %pad_maximum_fusion.sketch_ref, bf16[16,256,256]{2,1,0:T(8,128)(2,1)S(1)} %get-tuple-element.10.pairs_ref), custom_call_target="tpu_custom_call" | custom-call | flops 1073741824 | bytes 33554432 | tf_op jit(solution)/shard_map/solve/pallas_call | solution.py:203
  22.8 1.9 %collective-permute-start.5 = (f32[24,24,128]{2,1,0:T(8,128)S(1)}, f32[24,24,128]{2,1,0:T(8,128)S(1)}, u32[]{:S(2)}, u32[]{:S(2)}) collective-permute-start(f32[24,24,128]{2,1,0:T(8,128)S(1)} %get-tuple-element.12), channel_id=1, source_target_pairs={{0,16},{1,17},{2,18},{3,19},{4,20},{5,21},{6,22},{7,23},{8,24},{9,... | collective-permute-start | bytes 884744 | tf_op jit(solution)/shard_map/ppermute | solution.py:249
  24.7 0.2 others_ranks.1
  24.9 0.3 collective-permute-start.6
  25.2 0.5 %own_ranks.1.own_ref = f32[24,32,128]{2,1,0:T(8,128)S(1)} custom-call(f32[48,128]{1,0:T(8,128)S(1)} %get-tuple-element.11.factor_ref, bf16[16,256,256]{2,1,0:T(8,128)(2,1)S(1)} %get-tuple-element.10.pairs_ref), custom_call_target="tpu_custom_call" | custom-call | flops 1048576 | bytes 4194304 | tf_op jit(solution)/shard_map/own_ranks/pallas_call | solution.py:224
  25.7 5.2 %collective-permute-done.6.refs_1_ = f32[24,8,128]{2,1,0:T(8,128)S(1)} collective-permute-done((f32[24,8,128]{2,1,0:T(8,128)S(1)}, f32[24,8,128]{2,1,0:T(8,128)S(1)}, u32[]{:S(2)}, u32[]{:S(2)}) %collective-permute-start.6) | collective-permute-done | bytes 98336 | tf_op jit(solution)/shard_map/ppermute | solution.py:249
  30.9 0.0 collective-permute-done.5.refs_0_
  30.9 0.8 %add_ranks.1 = f32[24,32,128]{2,1,0:T(8,128)} custom-call(f32[24,32,128]{2,1,0:T(8,128)S(1)} %own_ranks.1.own_ref, f32[24,24,128]{2,1,0:T(8,128)S(1)} %collective-permute-done.5.refs_0_, f32[24,8,128]{2,1,0:T(8,128)S(1)} %collective-permute-done.6.refs_1_), custom_call_target="tpu_custom_call" | custom-call | tf_op jit(solution)/shard_map/add_ranks/pallas_call | solution.py:231
  (5 shorter events, 0.0 us)
Async XLA Ops:
  2.9 1.4 %collective-permute-start = (f32[48,128]{1,0:T(8,128)S(1)}, f32[48,128]{1,0:T(8,128)S(1)}, u32[]{:S(2)}, u32[]{:S(2)}) collective-permute-start(f32[48,128]{1,0:T(8,128)S(1)} %get-tuple-element.9), channel_id=1, source_target_pairs={{0,1},{1,0},{2,3},{3,2},{4,5},{5,4},{6,7},{7,6},{8,9},{9,8},{10,11... | collective-permute-start | bytes 73736 | tf_op jit(solution)/shard_map/ppermute | solution.py:249
  4.3 4.2 %collective-permute-start.1 = (f32[48,128]{1,0:T(8,128)S(1)}, f32[48,128]{1,0:T(8,128)S(1)}, u32[]{:S(2)}, u32[]{:S(2)}) collective-permute-start(f32[48,128]{1,0:T(8,128)S(1)} %add.12), channel_id=1, source_target_pairs={{0,3},{1,2},{2,1},{3,0},{4,7},{5,6},{6,5},{7,4},{8,11},{9,10},{10,... | collective-permute-start | bytes 73736 | tf_op jit(solution)/shard_map/ppermute | solution.py:249
  8.4 3.8 %collective-permute-start.2 = (f32[48,128]{1,0:T(8,128)S(1)}, f32[48,128]{1,0:T(8,128)S(1)}, u32[]{:S(2)}, u32[]{:S(2)}) collective-permute-start(f32[48,128]{1,0:T(8,128)S(1)} %add.13), channel_id=1, source_target_pairs={{0,4},{1,5},{2,6},{3,7},{4,0},{5,1},{6,2},{7,3},{8,12},{9,13},{10,... | collective-permute-start | bytes 73736 | tf_op jit(solution)/shard_map/ppermute | solution.py:249
  12.2 4.8 %collective-permute-start.3 = (f32[48,128]{1,0:T(8,128)S(1)}, f32[48,128]{1,0:T(8,128)S(1)}, u32[]{:S(2)}, u32[]{:S(2)}) collective-permute-start(f32[48,128]{1,0:T(8,128)S(1)} %add.14), channel_id=1, source_target_pairs={{0,8},{1,9},{2,10},{3,11},{4,12},{5,13},{6,14},{7,15},{8,0},{9,1},... | collective-permute-start | bytes 73736 | tf_op jit(solution)/shard_map/ppermute | solution.py:249
  17.1 3.8 %collective-permute-start.4 = (f32[48,128]{1,0:T(8,128)S(1)}, f32[48,128]{1,0:T(8,128)S(1)}, u32[]{:S(2)}, u32[]{:S(2)}) collective-permute-start(f32[48,128]{1,0:T(8,128)S(1)} %add.15), channel_id=1, source_target_pairs={{0,16},{1,17},{2,18},{3,19},{4,20},{5,21},{6,22},{7,23},{8,24},{9,... | collective-permute-start | bytes 73736 | tf_op jit(solution)/shard_map/ppermute | solution.py:249
  22.8 8.1 %collective-permute-start.5 = (f32[24,24,128]{2,1,0:T(8,128)S(1)}, f32[24,24,128]{2,1,0:T(8,128)S(1)}, u32[]{:S(2)}, u32[]{:S(2)}) collective-permute-start(f32[24,24,128]{2,1,0:T(8,128)S(1)} %get-tuple-element.12), channel_id=1, source_target_pairs={{0,16},{1,17},{2,18},{3,19},{4,20},{5,21},{6,22},{7,23},{8,24},{9,... | collective-permute-start | bytes 884744 | tf_op jit(solution)/shard_map/ppermute | solution.py:249
  24.9 6.0 %collective-permute-start.6 = (f32[24,8,128]{2,1,0:T(8,128)S(1)}, f32[24,8,128]{2,1,0:T(8,128)S(1)}, u32[]{:S(2)}, u32[]{:S(2)}) collective-permute-start(f32[24,8,128]{2,1,0:T(8,128)S(1)} %others_ranks.1), channel_id=1, source_target_pairs={{0,16},{1,17},{2,18},{3,19},{4,20},{5,21},{6,22},{7,23},{8,24},{9,... | collective-permute-start | bytes 294920 | tf_op jit(solution)/shard_map/ppermute | solution.py:249

commit v6 on v5

--- a/solution.py
+++ b/solution.py
@@ -79,16 +79,22 @@
     )(*(pltpu.with_memory_space_constraint(array, pltpu.HBM) for array in (field, test)))
 
 
+def unit(size):
+    return jnp.where(
+        lax.broadcasted_iota(jnp.int32, (size, size), 0) == lax.broadcasted_iota(jnp.int32, (size, size), 1), 1.0, 0.0
+    ).astype(F32)
+
+
 def eliminate(gram, right, spread_ref):
     size, width = gram.shape[0], LANES + right.shape[1]
-    whole = jnp.concatenate([gram, jnp.zeros((size, LANES - size), F32), right], axis=1)
+    whole = jnp.concatenate([unit(size), gram, jnp.zeros((size, LANES - 2 * size), F32), right], axis=1)
     tiles = [whole[i : i + SUBLANES] for i in range(0, size, SUBLANES)]
     spread = lambda x: jnp.broadcast_to(x, (SUBLANES, LANES))
     widen = lambda x: jnp.concatenate([x] * (width // LANES), axis=1)
     block = range(SUBLANES)
     solved = []
     for t, tile in enumerate(tiles):
-        start = t * SUBLANES
+        start = size + t * SUBLANES
         for j in block:
             spread_ref[t, j] = spread(tile[:, start + j : start + j + 1])
         entry = {(i, j): spread(spread_ref[t, j, i : i + 1, :]) for j in block for i in range(j, SUBLANES)}
@@ -107,7 +113,7 @@
             for j in range(i):
                 row = row - lower[i, j] * reduced[j]
             reduced.append(row)
-            solved.append(row[:1, LANES:] * widen(lax.rsqrt(entry[i, i]))[:1, LANES:])
+            solved.append((row * widen(lax.rsqrt(entry[i, i])))[:1])
         if t == len(tiles) - 1:
             break
         scaled = [None] * SUBLANES
@@ -136,106 +142,143 @@
     return product[:half] + product[half:]
 
 
-def multiply(factor, pairs_ref, first, out_refs):
-    ranks, span, lanes = out_refs[0].shape
+def multiply(factor, pairs_ref, first, out_refs, begin=0):
+    span, ranks, lanes = out_refs[0].shape
     left = twice(factor)
-    flat = [ref.reshape(ranks * span, lanes) for ref in out_refs]
-    for pair in range(span // 2):
+    for pair in range((span - begin) // 2):
         product = times(left, pairs_ref[first + pair])
         for q in range(2):
-            for d, ref in enumerate(flat):
-                ref[pl.ds(2 * pair + q, ranks, stride=span), :] = product[
-                    d * ranks : (d + 1) * ranks, q * lanes : (q + 1) * lanes
-                ]
-
-
-def solve_kernel(axis, sketch_ref, pairs_ref, factor_ref, *refs):
+            for d, ref in enumerate(out_refs):
+                ref[begin + 2 * pair + q] = product[d * ranks : (d + 1) * ranks, q * lanes : (q + 1) * lanes]
+
+
+def raw_kernel(sketch_ref, pairs_ref, out_ref):
+    multiply(sketch_ref[...], pairs_ref, 0, [out_ref])
+
+
+def solve_kernel(axis, first, sketch_ref, pairs_ref, solved_ref, *refs):
     *out_refs, spread_ref = refs
     rows = pairs_ref.shape[1] // 2
     sketch = sketch_ref[...]
     gram = lax.dot_general(sketch, sketch, NT, precision=PRECISE, preferred_element_type=F32)
-    factor = eliminate(gram, sketch[:, :rows], spread_ref)
+    solved = eliminate(gram, sketch[:, :rows], spread_ref)
     parties = len(out_refs) + 1
-    ranks = factor.shape[0] // parties
+    ranks = solved.shape[0] // parties
     me = lax.axis_index(axis)
     ordered = []
     for d in range(parties):
-        rank_rows = factor[:ranks]
+        rank_rows = solved[:ranks]
         for e in range(1, parties):
-            rank_rows = jnp.where((me ^ d) == e, factor[e * ranks : (e + 1) * ranks], rank_rows)
+            rank_rows = jnp.where((me ^ d) == e, solved[e * ranks : (e + 1) * ranks], rank_rows)
         ordered.append(rank_rows)
-    factor_ref[...] = jnp.concatenate(ordered, axis=0)
-    multiply(jnp.concatenate(ordered[1:], axis=0), pairs_ref, 0, out_refs)
-
-
-def ranks_kernel(first, begin, factor_ref, pairs_ref, *out_refs):
-    ranks = out_refs[0].shape[0]
-    multiply(factor_ref[begin : begin + ranks * len(out_refs), :], pairs_ref, first, out_refs)
-
-
-def add_kernel(parties, own_ref, *refs):
-    *others, out_hbm, total_ref, sems = refs
-    copies, place = [], 0
-    for chunk in range(len(others) // (parties - 1)):
-        parts = others[chunk * (parties - 1) : (chunk + 1) * (parties - 1)]
-        here = pl.ds(place, parts[0].shape[1])
-        total = own_ref[:, here, :]
-        for part in parts:
-            total = total + part[...]
-        total_ref[:, here, :] = total
-        copies.append(pltpu.make_async_copy(total_ref.at[:, here], out_hbm.at[:, here], sems.at[chunk]))
-        copies[-1].start()
-        place += parts[0].shape[1]
-    for copy in copies:
-        copy.wait()
+    solved_ref[...] = jnp.concatenate(ordered, axis=0)
+    multiply(jnp.concatenate(ordered[1:], axis=0)[:, LANES:], pairs_ref, first, out_refs)
+
+
+def others_kernel(first, solved_ref, pairs_ref, *out_refs):
+    ranks = out_refs[0].shape[1]
+    multiply(solved_ref[ranks : ranks * (1 + len(out_refs)), LANES:], pairs_ref, first, out_refs)
+
+
+def own_kernel(first, solved_ref, pairs_ref, *refs):
+    *raw_refs, out_ref = refs
+    span, ranks, lanes = out_ref.shape
+    solved = solved_ref[:ranks, :]
+    multiply(solved[:, LANES:], pairs_ref, first, [out_ref], 2 * first)
+    for pair in range(first):
+        right = []
+        for at in (2 * pair, 2 * pair + 1):
+            total = raw_refs[0][at]
+            for ref in raw_refs[1:]:
+                total = total + ref[at]
+            right.append(total)
+        columns = right[0].shape[0]
+        product = lax.dot_general(
+            solved[:, :columns], jnp.concatenate(right, axis=1), NN, precision=PRECISE, preferred_element_type=F32
+        )
+        for q in range(2):
+            out_ref[2 * pair + q] = product[:, q * lanes : (q + 1) * lanes]
+
+
+def add_kernel(parties, begin, size, own_ref, *refs):
+    *others, out_hbm, total_ref, sem = refs
+    others = others[: parties - 1]
+    ranks, span, lanes = total_ref.shape
+    flat = total_ref.reshape(ranks * span, lanes)
+    bare = size - others[0].shape[0]
+    for at in range(size):
+        total = own_ref[begin + at]
+        for part in others if at >= bare else ():
+            total = total + part[at - bare]
+        flat[pl.ds(at, ranks, stride=span), :] = total
+    copy = pltpu.make_async_copy(total_ref, out_hbm.at[:, pl.ds(begin, size)], sem)
+    copy.start()
+    copy.wait()
 
 
 PARAMS = pltpu.CompilerParams(vmem_limit_bytes=VMEM_LIMIT)
 COST = pl.CostEstimate(flops=1 << 30, bytes_accessed=1 << 25, transcendentals=0)
 
 
-def project(sketch, pairs, sizes, spans):
+def run(kernel, name, out_shape, *operands, cost=COST, scratch=()):
+    return pl.pallas_call(
+        kernel, out_shape=out_shape, compiler_params=PARAMS, cost_estimate=cost, name=name, scratch_shapes=scratch
+    )(*operands)
+
+
+def project(sketch, pairs, sizes, raw, spans):
     parties = sizes["gx"]
     columns, rows = sketch.shape[0], pairs.shape[1] // 2
     lanes = pairs.shape[2] // 2
     ranks, second = columns // parties, 2 * pairs.shape[0]
-    chunks = [jax.ShapeDtypeStruct((ranks, span, lanes), F32) for span in spans]
-    factor, *sent = pl.pallas_call(
-        functools.partial(solve_kernel, "gx"),
-        out_shape=[jax.ShapeDtypeStruct((columns, rows), F32)] + [chunks[0]] * (parties - 1),
-        scratch_shapes=[pltpu.VMEM((columns // SUBLANES, SUBLANES, SUBLANES, LANES), F32)],
-        compiler_params=PARAMS,
-        cost_estimate=COST,
-        name="solve",
-    )(sketch, pairs)
-    received = [exchange(x, sizes, gx=d + 1) for d, x in enumerate(sent)]
-    place = spans[0]
-    for chunk in chunks[1:]:
-        sent = pl.pallas_call(
-            functools.partial(ranks_kernel, place // 2, ranks),
-            out_shape=[chunk] * (parties - 1),
+    piece = lambda span, height: jax.ShapeDtypeStruct((span, height, lanes), F32)
+    whole = sketch
+    for bit in steps_of(parties):
+        whole = jnp.concatenate([whole, exchange(whole, sizes, gx=bit)], axis=1)
+    raw_parts = []
+    if raw:
+        mine = run(raw_kernel, "raw_product", piece(raw, columns), sketch, pairs)
+        raw_parts = [mine] + [exchange(mine, sizes, gx=d) for d in range(1, parties)]
+    place, received = raw, []
+    solved, *sent = run(
+        functools.partial(solve_kernel, "gx", place // 2),
+        "solve",
+        [jax.ShapeDtypeStruct((columns, LANES + rows), F32)] + [piece(spans[0], ranks)] * (parties - 1),
+        whole,
+        pairs,
+        scratch=[pltpu.VMEM((columns // SUBLANES, SUBLANES, SUBLANES, LANES), F32)],
+    )
+    for step, span in enumerate(spans):
+        if step:
+            sent = run(
+                functools.partial(others_kernel, place // 2),
+                "others_ranks",
+                [piece(span, ranks)] * (parties - 1),
+                solved,
+                pairs,
+            )
+        received += [exchange(x, sizes, gx=d + 1) for d, x in enumerate(sent)]
+        place += span
+    core = run(functools.partial(own_kernel, raw // 2), "own_ranks", piece(second, ranks), solved, pairs, *raw_parts)
+    out, begin = None, 0
+    for step, span in enumerate(spans):
+        size = span if step else raw + span
+        whole_before = [] if out is None else [out]
+        count = 1 + (parties - 1)
+        parts = received[step * (parties - 1) : (step + 1) * (parties - 1)]
+        out = pl.pallas_call(
+            functools.partial(add_kernel, parties, begin, size),
+            out_shape=jax.ShapeDtypeStruct((ranks, second, lanes), F32),
+            in_specs=[pl.BlockSpec(memory_space=pltpu.VMEM)] * count + [pl.BlockSpec(memory_space=pl.ANY)] * len(whole_before),
+            out_specs=pl.BlockSpec(memory_space=pl.ANY),
+            input_output_aliases={count: 0} if whole_before else {},
+            scratch_shapes=[pltpu.VMEM((ranks, size, lanes), F32), pltpu.SemaphoreType.DMA],
             compiler_params=PARAMS,
-            cost_estimate=COST,
-            name="others_ranks",
-        )(factor, pairs)
-        received += [exchange(x, sizes, gx=d + 1) for d, x in enumerate(sent)]
-        place += chunk.shape[1]
-    own = jax.ShapeDtypeStruct((ranks, second, lanes), F32)
-    (core,) = pl.pallas_call(
-        functools.partial(ranks_kernel, 0, 0),
-        out_shape=[own],
-        compiler_params=PARAMS,
-        cost_estimate=pl.CostEstimate(flops=1 << 20, bytes_accessed=1 << 22, transcendentals=0),
-        name="own_ranks",
-    )(factor, pairs)
-    return pl.pallas_call(
-        functools.partial(add_kernel, parties),
-        out_shape=own,
-        out_specs=pl.BlockSpec(memory_space=pl.ANY),
-        scratch_shapes=[pltpu.VMEM(own.shape, F32), pltpu.SemaphoreType.DMA((len(chunks),))],
-        compiler_params=PARAMS,
-        name="add_ranks",
-    )(core, *received)
+            cost_estimate=COST if step < len(spans) - 1 else None,
+            name="add_ranks",
+        )(core, *parts, *whole_before)
+        begin += size
+    return out
 
 
 AXES = ("gx", "gy", "gz")
@@ -259,10 +302,9 @@
     for bit in steps_of(sizes["gz"]):
         sketch = sketch + exchange(sketch, sizes, gz=bit | 1)
     for bit in steps_of(sizes["gy"]):
-        sketch = sketch + exchange(sketch, sizes, gy=bit)
-    for bit in steps_of(sizes["gx"]):
-        sketch = jnp.concatenate([sketch, exchange(sketch, sizes, gx=bit)], axis=1)
-    return project(sketch, pairs, sizes, (3 * second // 4, second // 4))
+        sketch = sketch + exchange(sketch, sizes, gy=bit, gz=1)
+    raw, last = second * 3 // 16, second // 4
+    return project(sketch, pairs, sizes, raw, (second - raw - last, last))
 
 
 def solution(mesh):

time: 31.8 us -> 31.3 us (0.984)
  waiting for transfers between devices: 13.2 us -> 12.1 us
  Pallas kernels: 6.3 us -> 7.12 us
    ppermute x7 -> x8, waiting for transfers between devices: 13.2 us -> 12.1 us  [exchange(): return lax.ppermute(x, AXES, pairs)]
    pallas_call x4 -> x6, Pallas kernels: 3.43 us -> 4.25 us  [the longest x4 2.79 us: run(): pl.pallas_call(kernel, out_shape=out_shape, compiler_params=PARAMS, cost_...]
    ppermute x7 -> x8, starting transfers between devices: 12.2 us -> 11.9 us  [exchange(): return lax.ppermute(x, AXES, pairs)]
  transfers between devices with their start and end apart: 7 -> 8, of which waited for: 6 -> 7; matrix products, arithmetic and copies ran while one was open for 0% -> 0% of each run, Pallas kernels for 2% -> 11%
where the time goes in v6:
time: 31.3 us; the launch traced here: 31.2 us
  waiting for transfers between devices  12.1 us (39%)
  starting transfers between devices  11.9 us (38%)
  Pallas kernels  7.12 us (23%)
    ppermute x8, waiting for transfers between devices, exchange(): return lax.ppermute(x, AXES, pairs)  12.1 us
    ppermute x8, starting transfers between devices, exchange(): return lax.ppermute(x, AXES, pairs)  11.9 us
    pallas_call x1, Pallas kernels, partial_sketch(): pl.pallas_call(functools.partial(sketch_kernel, span), in_specs=[pl.Block...  2.87 us
    pallas_call x4, Pallas kernels, run(): pl.pallas_call(kernel, out_shape=out_shape, compiler_params=PARAMS, cost_...  2.79 us
    pallas_call x2, Pallas kernels, project(): pl.pallas_call(functools.partial(add_kernel, parties, begin, size), out_s...  1.46 us
  transfers between devices with their start and end apart: 8, of which 7 were waited for; matrix products, arithmetic and copies ran while one was open for 0% of the time, Pallas kernels for 11%

profile of v6, /device:TPU:0, one launch (start us, length us, event | category | flops | bytes accessed | tf_op | source)
XLA Modules:
  0.0 31.2 jit_solution(6644668364870087338)
XLA Ops:
  0.0 2.9 %partial_sketch.1 = (f32[48,128]{1,0:T(8,128)S(1)}, bf16[16,256,256]{2,1,0:T(8,128)(2,1)S(1)}) custom-call(f32[128,32,128]{2,1,0:T(8,128)} %field_hbm.1, f32[48,32,128]{2,1,0:T(8,128)} %test_hbm.1), custom_call_target="tpu_custom_call" | custom-call | tf_op jit(solution)/shard_map/partial_sketch/pallas_call | solution.py:65
  2.9 0.5 %collective-permute-start = (f32[48,128]{1,0:T(8,128)S(1)}, f32[48,128]{1,0:T(8,128)S(1)}, u32[]{:S(2)}, u32[]{:S(2)}) collective-permute-start(f32[48,128]{1,0:T(8,128)S(1)} %get-tuple-element.9), channel_id=1, source_target_pairs={{0,1},{1,0},{2,3},{3,2},{4,5},{5,4},{6,7},{7,6},{8,9},{9,8},{10,11... | collective-permute-start | bytes 73736 | tf_op jit(solution)/shard_map/ppermute | solution.py:292
  3.4 0.8 %collective-permute-done = f32[48,128]{1,0:T(8,128)S(1)} collective-permute-done((f32[48,128]{1,0:T(8,128)S(1)}, f32[48,128]{1,0:T(8,128)S(1)}, u32[]{:S(2)}, u32[]{:S(2)}) %collective-permute-start) | collective-permute-done | bytes 24608 | tf_op jit(solution)/shard_map/ppermute | solution.py:292
  4.3 2.6 %collective-permute-start.1 = (f32[48,128]{1,0:T(8,128)S(1)}, f32[48,128]{1,0:T(8,128)S(1)}, u32[]{:S(2)}, u32[]{:S(2)}) collective-permute-start(f32[48,128]{1,0:T(8,128)S(1)} %add.12), channel_id=1, source_target_pairs={{0,3},{1,2},{2,1},{3,0},{4,7},{5,6},{6,5},{7,4},{8,11},{9,10},{10,... | collective-permute-start | bytes 73736 | tf_op jit(solution)/shard_map/ppermute | solution.py:292
  6.9 1.5 %collective-permute-done.1 = f32[48,128]{1,0:T(8,128)S(1)} collective-permute-done((f32[48,128]{1,0:T(8,128)S(1)}, f32[48,128]{1,0:T(8,128)S(1)}, u32[]{:S(2)}, u32[]{:S(2)}) %collective-permute-start.1) | collective-permute-done | bytes 24608 | tf_op jit(solution)/shard_map/ppermute | solution.py:292
  8.4 1.8 %collective-permute-start.2 = (f32[48,128]{1,0:T(8,128)S(1)}, f32[48,128]{1,0:T(8,128)S(1)}, u32[]{:S(2)}, u32[]{:S(2)}) collective-permute-start(f32[48,128]{1,0:T(8,128)S(1)} %add.13), channel_id=1, source_target_pairs={{0,5},{1,4},{2,7},{3,6},{4,1},{5,0},{6,3},{7,2},{8,13},{9,12},{10,... | collective-permute-start | bytes 73736 | tf_op jit(solution)/shard_map/ppermute | solution.py:292
  10.2 1.5 %collective-permute-done.2 = f32[48,128]{1,0:T(8,128)S(1)} collective-permute-done((f32[48,128]{1,0:T(8,128)S(1)}, f32[48,128]{1,0:T(8,128)S(1)}, u32[]{:S(2)}, u32[]{:S(2)}) %collective-permute-start.2) | collective-permute-done | bytes 24608 | tf_op jit(solution)/shard_map/ppermute | solution.py:292
  11.7 2.7 %collective-permute-start.3 = (f32[48,128]{1,0:T(8,128)S(1)}, f32[48,128]{1,0:T(8,128)S(1)}, u32[]{:S(2)}, u32[]{:S(2)}) collective-permute-start(f32[48,128]{1,0:T(8,128)S(1)} %add.14), channel_id=1, source_target_pairs={{0,9},{1,8},{2,11},{3,10},{4,13},{5,12},{6,15},{7,14},{8,1},{9,0},... | collective-permute-start | bytes 73736 | tf_op jit(solution)/shard_map/ppermute | solution.py:292
  14.5 1.5 %collective-permute-done.3 = f32[48,128]{1,0:T(8,128)S(1)} collective-permute-done((f32[48,128]{1,0:T(8,128)S(1)}, f32[48,128]{1,0:T(8,128)S(1)}, u32[]{:S(2)}, u32[]{:S(2)}) %collective-permute-start.3) | collective-permute-done | bytes 24608 | tf_op jit(solution)/shard_map/ppermute | solution.py:292
  16.0 1.8 %collective-permute-start.4 = (f32[48,128]{1,0:T(8,128)S(1)}, f32[48,128]{1,0:T(8,128)S(1)}, u32[]{:S(2)}, u32[]{:S(2)}) collective-permute-start(f32[48,128]{1,0:T(8,128)S(1)} %add.15.sketch_ref), channel_id=1, source_target_pairs={{0,16},{1,17},{2,18},{3,19},{4,20},{5,21},{6,22},{7,23},{8,24},{9,... | collective-permute-start | bytes 73736 | tf_op jit(solution)/shard_map/ppermute | solution.py:292
  17.8 0.2 raw_product.1.refs_0_
  18.0 0.3 %collective-permute-start.5 = (f32[6,48,128]{2,1,0:T(8,128)S(1)}, f32[6,48,128]{2,1,0:T(8,128)S(1)}, u32[]{:S(2)}, u32[]{:S(2)}) collective-permute-start(f32[6,48,128]{2,1,0:T(8,128)S(1)} %raw_product.1.refs_0_), channel_id=1, source_target_pairs={{0,16},{1,17},{2,18},{3,19},{4,20},{5,21},{6,22},{7,23},{8,24},{9,... | collective-permute-start | bytes 442376 | tf_op jit(solution)/shard_map/ppermute | solution.py:292
  18.3 1.5 %collective-permute-done.4 = f32[48,128]{1,0:T(8,128)S(1)} collective-permute-done((f32[48,128]{1,0:T(8,128)S(1)}, f32[48,128]{1,0:T(8,128)S(1)}, u32[]{:S(2)}, u32[]{:S(2)}) %collective-permute-start.4) | collective-permute-done | bytes 24608 | tf_op jit(solution)/shard_map/ppermute | solution.py:292
  19.8 1.9 %solve.1 = (f32[48,256]{1,0:T(8,128)S(1)}, f32[18,24,128]{2,1,0:T(8,128)S(1)}) custom-call(f32[48,256]{1,0:T(8,128)S(1)} %pad_maximum_fusion.sketch_ref, bf16[16,256,256]{2,1,0:T(8,128)(2,1)S(1)} %get-tuple-element.10.pairs_ref), custom_call_target="tpu_custom_call" | custom-call | flops 1073741824 | bytes 33554432 | tf_op jit(solution)/shard_map/solve/pallas_call | solution.py:224
  21.7 2.0 %collective-permute-start.7 = (f32[18,24,128]{2,1,0:T(8,128)S(1)}, f32[18,24,128]{2,1,0:T(8,128)S(1)}, u32[]{:S(2)}, u32[]{:S(2)}) collective-permute-start(f32[18,24,128]{2,1,0:T(8,128)S(1)} %get-tuple-element.12), channel_id=1, source_target_pairs={{0,16},{1,17},{2,18},{3,19},{4,20},{5,21},{6,22},{7,23},{8,24},{9,... | collective-permute-start | bytes 663560 | tf_op jit(solution)/shard_map/ppermute | solution.py:292
  23.8 0.2 others_ranks.1
  24.0 0.2 collective-permute-start.6
  24.1 0.0 collective-permute-done.5.refs_1_
  24.1 0.5 %own_ranks.1.own_ref = f32[32,24,128]{2,1,0:T(8,128)S(1)} custom-call(f32[48,256]{1,0:T(8,128)S(1)} %get-tuple-element.11.solved_ref, bf16[16,256,256]{2,1,0:T(8,128)(2,1)S(1)} %get-tuple-element.10.pairs_ref, f32[6,48,128]{2,1,0:T(8,128)S(1)} %raw_product.1.refs_0_, f32[6,48,128]{2,1,0:T(8,128)S(1)} %collective-permute-done.5.refs_1_), custom_call_target="tpu_custom_call" | custom-call | flops 1073741824 | bytes 33554432 | tf_op jit(solution)/shard_map/own_ranks/pallas_call | solution.py:224
  24.6 4.9 %collective-permute-done.7.refs_0_ = f32[18,24,128]{2,1,0:T(8,128)S(1)} collective-permute-done((f32[18,24,128]{2,1,0:T(8,128)S(1)}, f32[18,24,128]{2,1,0:T(8,128)S(1)}, u32[]{:S(2)}, u32[]{:S(2)}) %collective-permute-start.7) | collective-permute-done | bytes 221216 | tf_op jit(solution)/shard_map/ppermute | solution.py:292
  29.5 0.8 %add_ranks.2.refs_1_ = f32[24,32,128]{2,1,0:T(8,128)} custom-call(f32[32,24,128]{2,1,0:T(8,128)S(1)} %own_ranks.1.own_ref, f32[18,24,128]{2,1,0:T(8,128)S(1)} %collective-permute-done.7.refs_0_), custom_call_target="tpu_custom_call" | custom-call | flops 1073741824 | bytes 33554432 | tf_op jit(solution)/shard_map/add_ranks/pallas_call | solution.py:269
  30.3 0.3 collective-permute-done.6.refs_0_
  30.5 0.7 %add_ranks.3 = f32[24,32,128]{2,1,0:T(8,128)} custom-call(f32[32,24,128]{2,1,0:T(8,128)S(1)} %own_ranks.1.own_ref, f32[8,24,128]{2,1,0:T(8,128)S(1)} %collective-permute-done.6.refs_0_, f32[24,32,128]{2,1,0:T(8,128)} %add_ranks.2.refs_1_), custom_call_target="tpu_custom_call", output_to_operand_aliasing={{}: (2, {})} | custom-call | tf_op jit(solution)/shard_map/add_ranks/pallas_call | solution.py:269
  (5 shorter events, 0.0 us)
Async XLA Ops:
  2.9 1.4 %collective-permute-start = (f32[48,128]{1,0:T(8,128)S(1)}, f32[48,128]{1,0:T(8,128)S(1)}, u32[]{:S(2)}, u32[]{:S(2)}) collective-permute-start(f32[48,128]{1,0:T(8,128)S(1)} %get-tuple-element.9), channel_id=1, source_target_pairs={{0,1},{1,0},{2,3},{3,2},{4,5},{5,4},{6,7},{7,6},{8,9},{9,8},{10,11... | collective-permute-start | bytes 73736 | tf_op jit(solution)/shard_map/ppermute | solution.py:292
  4.3 4.2 %collective-permute-start.1 = (f32[48,128]{1,0:T(8,128)S(1)}, f32[48,128]{1,0:T(8,128)S(1)}, u32[]{:S(2)}, u32[]{:S(2)}) collective-permute-start(f32[48,128]{1,0:T(8,128)S(1)} %add.12), channel_id=1, source_target_pairs={{0,3},{1,2},{2,1},{3,0},{4,7},{5,6},{6,5},{7,4},{8,11},{9,10},{10,... | collective-permute-start | bytes 73736 | tf_op jit(solution)/shard_map/ppermute | solution.py:292
  8.4 3.3 %collective-permute-start.2 = (f32[48,128]{1,0:T(8,128)S(1)}, f32[48,128]{1,0:T(8,128)S(1)}, u32[]{:S(2)}, u32[]{:S(2)}) collective-permute-start(f32[48,128]{1,0:T(8,128)S(1)} %add.13), channel_id=1, source_target_pairs={{0,5},{1,4},{2,7},{3,6},{4,1},{5,0},{6,3},{7,2},{8,13},{9,12},{10,... | collective-permute-start | bytes 73736 | tf_op jit(solution)/shard_map/ppermute | solution.py:292
  11.7 4.3 %collective-permute-start.3 = (f32[48,128]{1,0:T(8,128)S(1)}, f32[48,128]{1,0:T(8,128)S(1)}, u32[]{:S(2)}, u32[]{:S(2)}) collective-permute-start(f32[48,128]{1,0:T(8,128)S(1)} %add.14), channel_id=1, source_target_pairs={{0,9},{1,8},{2,11},{3,10},{4,13},{5,12},{6,15},{7,14},{8,1},{9,0},... | collective-permute-start | bytes 73736 | tf_op jit(solution)/shard_map/ppermute | solution.py:292
  16.0 3.8 %collective-permute-start.4 = (f32[48,128]{1,0:T(8,128)S(1)}, f32[48,128]{1,0:T(8,128)S(1)}, u32[]{:S(2)}, u32[]{:S(2)}) collective-permute-start(f32[48,128]{1,0:T(8,128)S(1)} %add.15.sketch_ref), channel_id=1, source_target_pairs={{0,16},{1,17},{2,18},{3,19},{4,20},{5,21},{6,22},{7,23},{8,24},{9,... | collective-permute-start | bytes 73736 | tf_op jit(solution)/shard_map/ppermute | solution.py:292
  18.0 6.1 %collective-permute-start.5 = (f32[6,48,128]{2,1,0:T(8,128)S(1)}, f32[6,48,128]{2,1,0:T(8,128)S(1)}, u32[]{:S(2)}, u32[]{:S(2)}) collective-permute-start(f32[6,48,128]{2,1,0:T(8,128)S(1)} %raw_product.1.refs_0_), channel_id=1, source_target_pairs={{0,16},{1,17},{2,18},{3,19},{4,20},{5,21},{6,22},{7,23},{8,24},{9,... | collective-permute-start | bytes 442376 | tf_op jit(solution)/shard_map/ppermute | solution.py:292
  21.7 7.7 %collective-permute-start.7 = (f32[18,24,128]{2,1,0:T(8,128)S(1)}, f32[18,24,128]{2,1,0:T(8,128)S(1)}, u32[]{:S(2)}, u32[]{:S(2)}) collective-permute-start(f32[18,24,128]{2,1,0:T(8,128)S(1)} %get-tuple-element.12), channel_id=1, source_target_pairs={{0,16},{1,17},{2,18},{3,19},{4,20},{5,21},{6,22},{7,23},{8,24},{9,... | collective-permute-start | bytes 663560 | tf_op jit(solution)/shard_map/ppermute | solution.py:292
  24.0 6.6 %collective-permute-start.6 = (f32[8,24,128]{2,1,0:T(8,128)S(1)}, f32[8,24,128]{2,1,0:T(8,128)S(1)}, u32[]{:S(2)}, u32[]{:S(2)}) collective-permute-start(f32[8,24,128]{2,1,0:T(8,128)S(1)} %others_ranks.1), channel_id=1, source_target_pairs={{0,16},{1,17},{2,18},{3,19},{4,20},{5,21},{6,22},{7,23},{8,24},{9,... | collective-permute-start | bytes 294920 | tf_op jit(solution)/shard_map/ppermute | solution.py:292

commit v7 on v6

--- a/solution.py
+++ b/solution.py
@@ -23,7 +23,7 @@
     return terms + [x.astype(BF16)]
 
 
-def sketch_kernel(span, field_hbm, test_hbm, sketch_ref, pairs_ref, field, test, sems):
+def sketch_kernel(span, field_hbm, test_hbm, sketch_ref, pairs_ref, first_ref, field, test, sems):
     rows, second, lanes = field_hbm.shape
     columns = test_hbm.shape[0]
     steps = second // span
@@ -41,7 +41,11 @@
         flat_field = field.at[step].reshape(rows * span, lanes)
         flat_test = test.at[step].reshape(columns * span, lanes)
         for pair in range(span // 2):
-            x = jnp.concatenate([flat_field[pl.ds(2 * pair + q, rows, stride=span), :] for q in range(2)], axis=1)
+            x = [flat_field[pl.ds(2 * pair + q, rows, stride=span), :] for q in range(2)]
+            for q in range(2):
+                if step * span + 2 * pair + q < first_ref.shape[0]:
+                    first_ref[step * span + 2 * pair + q] = x[q]
+            x = jnp.concatenate(x, axis=1)
             t = jnp.concatenate([flat_test[pl.ds(2 * pair + q, columns, stride=span), :] for q in range(2)], axis=1)
             x = split(x, 3)
             t = split(t, 3)
@@ -57,7 +61,7 @@
     sketch_ref[...] = low
 
 
-def partial_sketch(field, test):
+def partial_sketch(field, test, first):
     rows, second, lanes = field.shape
     columns = test.shape[0]
     span = SUBLANES
@@ -68,6 +72,7 @@
         out_shape=[
             jax.ShapeDtypeStruct((columns, rows), F32),
             jax.ShapeDtypeStruct((second // 2, 2 * rows, 2 * lanes), BF16),
+            jax.ShapeDtypeStruct((first, rows, lanes), F32),
         ],
         scratch_shapes=[
             pltpu.VMEM((steps, rows, span, lanes), F32),
@@ -152,8 +157,12 @@
                 ref[begin + 2 * pair + q] = product[d * ranks : (d + 1) * ranks, q * lanes : (q + 1) * lanes]
 
 
-def raw_kernel(sketch_ref, pairs_ref, out_ref):
-    multiply(sketch_ref[...], pairs_ref, 0, [out_ref])
+def copy_kernel(sketch_ref, field_ref, out_ref):
+    out_ref[...] = field_ref[...]
+
+
+def raw_kernel(first, sketch_ref, pairs_ref, out_ref):
+    multiply(sketch_ref[...], pairs_ref, first, [out_ref])
 
 
 def solve_kernel(axis, first, sketch_ref, pairs_ref, solved_ref, *refs):
@@ -180,22 +189,32 @@
     multiply(solved_ref[ranks : ranks * (1 + len(out_refs)), LANES:], pairs_ref, first, out_refs)
 
 
-def own_kernel(first, solved_ref, pairs_ref, *refs):
-    *raw_refs, out_ref = refs
+def own_kernel(parties, whole_pairs, raw_pairs, sketch_ref, solved_ref, pairs_ref, *refs):
+    *refs, out_ref = refs
+    field_refs, raw_refs = refs[: parties - 1], refs[parties - 1 :]
     span, ranks, lanes = out_ref.shape
+    columns, rows = sketch_ref.shape[0], sketch_ref.shape[1] // parties
     solved = solved_ref[:ranks, :]
-    multiply(solved[:, LANES:], pairs_ref, first, [out_ref], 2 * first)
-    for pair in range(first):
-        right = []
-        for at in (2 * pair, 2 * pair + 1):
-            total = raw_refs[0][at]
-            for ref in raw_refs[1:]:
-                total = total + ref[at]
-            right.append(total)
-        columns = right[0].shape[0]
-        product = lax.dot_general(
-            solved[:, :columns], jnp.concatenate(right, axis=1), NN, precision=PRECISE, preferred_element_type=F32
-        )
+    inverse = solved[:, :columns]
+    apply = functools.partial(lax.dot_general, dimension_numbers=NN, precision=PRECISE, preferred_element_type=F32)
+    done = whole_pairs + raw_pairs
+    multiply(solved[:, LANES:], pairs_ref, done, [out_ref], 2 * done)
+    lefts = [twice(solved[:, LANES:])]
+    lefts += [twice(apply(inverse, sketch_ref[:, d * rows : (d + 1) * rows])) for d in range(1, parties)]
+    for pair in range(done):
+        if pair < whole_pairs:
+            product = times(lefts[0], pairs_ref[pair])
+            for left, ref in zip(lefts[1:], field_refs):
+                terms = split(jnp.concatenate([ref[2 * pair], ref[2 * pair + 1]], axis=1), 2)
+                product = product + times(left, jnp.concatenate(terms, axis=0))
+        else:
+            right = []
+            for at in (2 * (pair - whole_pairs), 2 * (pair - whole_pairs) + 1):
+                total = raw_refs[0][at]
+                for ref in raw_refs[1:]:
+                    total = total + ref[at]
+                right.append(total)
+            product = apply(inverse, jnp.concatenate(right, axis=1))
         for q in range(2):
             out_ref[2 * pair + q] = product[:, q * lanes : (q + 1) * lanes]
 
@@ -221,25 +240,29 @@
 
 
 def run(kernel, name, out_shape, *operands, cost=COST, scratch=()):
+    if isinstance(out_shape, jax.Array):
+        out_shape = jax.ShapeDtypeStruct(out_shape.shape, out_shape.dtype)
     return pl.pallas_call(
         kernel, out_shape=out_shape, compiler_params=PARAMS, cost_estimate=cost, name=name, scratch_shapes=scratch
     )(*operands)
 
 
-def project(sketch, pairs, sizes, raw, spans):
+def project(sketch, pairs, first_field, sizes, raw, spans):
     parties = sizes["gx"]
     columns, rows = sketch.shape[0], pairs.shape[1] // 2
     lanes = pairs.shape[2] // 2
     ranks, second = columns // parties, 2 * pairs.shape[0]
     piece = lambda span, height: jax.ShapeDtypeStruct((span, height, lanes), F32)
+    early = first_field.shape[0]
+    fields = [exchange(first_field, sizes, gx=d) for d in range(1, parties)]
     whole = sketch
+    summed = whole
     for bit in steps_of(parties):
         whole = jnp.concatenate([whole, exchange(whole, sizes, gx=bit)], axis=1)
-    raw_parts = []
-    if raw:
-        mine = run(raw_kernel, "raw_product", piece(raw, columns), sketch, pairs)
-        raw_parts = [mine] + [exchange(mine, sizes, gx=d) for d in range(1, parties)]
-    place, received = raw, []
+    mine = run(functools.partial(raw_kernel, early // 2), "raw_product", piece(raw, columns), summed, pairs)
+    raw_parts = [mine] + [exchange(mine, sizes, gx=d) for d in range(1, parties)]
+    whole, *fields = lax.optimization_barrier([whole, *fields])
+    place, received = early + raw, []
     solved, *sent = run(
         functools.partial(solve_kernel, "gx", place // 2),
         "solve",
@@ -259,10 +282,19 @@
             )
         received += [exchange(x, sizes, gx=d + 1) for d, x in enumerate(sent)]
         place += span
-    core = run(functools.partial(own_kernel, raw // 2), "own_ranks", piece(second, ranks), solved, pairs, *raw_parts)
+    core = run(
+        functools.partial(own_kernel, parties, early // 2, raw // 2),
+        "own_ranks",
+        piece(second, ranks),
+        whole,
+        solved,
+        pairs,
+        *fields,
+        *raw_parts,
+    )
     out, begin = None, 0
     for step, span in enumerate(spans):
-        size = span if step else raw + span
+        size = span if step else early + raw + span
         whole_before = [] if out is None else [out]
         count = 1 + (parties - 1)
         parts = received[step * (parties - 1) : (step + 1) * (parties - 1)]
@@ -298,13 +330,15 @@
 
 def body(sizes, field, test):
     second = field.shape[1]
-    sketch, pairs = partial_sketch(field, test)
+    early, raw, last = second * 4 // 32, second * 6 // 32, second * 8 // 32
+    sketch, pairs, first_field = partial_sketch(field, test, early)
     for bit in steps_of(sizes["gz"]):
         sketch = sketch + exchange(sketch, sizes, gz=bit | 1)
+        if bit == 1:
+            first_field = run(copy_kernel, "first_field", first_field, sketch, first_field)
     for bit in steps_of(sizes["gy"]):
         sketch = sketch + exchange(sketch, sizes, gy=bit, gz=1)
-    raw, last = second * 3 // 16, second // 4
-    return project(sketch, pairs, sizes, raw, (second - raw - last, last))
+    return project(sketch, pairs, first_field, sizes, raw, (second - early - raw - last, last))
 
 
 def solution(mesh):

time: 31.3 us -> 30.3 us (0.968)
  waiting for transfers between devices: 12.1 us -> 9.4 us
  starting transfers between devices: 11.9 us -> 13.4 us
    ppermute x8 -> x9, waiting for transfers between devices: 12.1 us -> 9.4 us  [exchange(): return lax.ppermute(x, AXES, pairs)]
    ppermute x8 -> x9, starting transfers between devices: 11.9 us -> 13.4 us  [exchange(): return lax.ppermute(x, AXES, pairs)]
    pallas_call x4 -> x5, Pallas kernels: 2.79 us -> 2.91 us  [run(): pl.pallas_call(kernel, out_shape=out_shape, compiler_params=PARAMS, cost_...]
  transfers between devices with their start and end apart: 8 -> 9, of which waited for: 7 -> 6; matrix products, arithmetic and copies ran while one was open for 0% -> 0% of each run, Pallas kernels for 11% -> 12%
where the time goes in v7:
time: 30.3 us; the launch traced here: 30.1 us
  starting transfers between devices  13.4 us (44%)
  waiting for transfers between devices  9.4 us (31%)
  Pallas kernels  7.22 us (24%)
    ppermute x9, starting transfers between devices, exchange(): return lax.ppermute(x, AXES, pairs)  13.4 us
    ppermute x9, waiting for transfers between devices, exchange(): return lax.ppermute(x, AXES, pairs)  9.4 us
    pallas_call x5, Pallas kernels, run(): pl.pallas_call(kernel, out_shape=out_shape, compiler_params=PARAMS, cost_...  2.91 us
    pallas_call x1, Pallas kernels, partial_sketch(): pl.pallas_call(functools.partial(sketch_kernel, span), in_specs=[pl.Block...  2.87 us
    pallas_call x2, Pallas kernels, project(): pl.pallas_call(functools.partial(add_kernel, parties, begin, size), out_s...  1.44 us
  transfers between devices with their start and end apart: 9, of which 6 were waited for; matrix products, arithmetic and copies ran while one was open for 0% of the time, Pallas kernels for 12%

profile of v7, /device:TPU:0, one launch (start us, length us, event | category | flops | bytes accessed | tf_op | source)
XLA Modules:
  0.0 30.1 jit_solution(12045085897877453835)
XLA Ops:
  0.0 2.9 %partial_sketch.1 = (f32[48,128]{1,0:T(8,128)S(1)}, bf16[16,256,256]{2,1,0:T(8,128)(2,1)S(1)}, f32[4,128,128]{2,1,0:T(8,128)S(1)}) custom-call(f32[128,32,128]{2,1,0:T(8,128)} %field_hbm.1, f32[48,32,128]{2,1,0:T(8,128)} %test_hbm.1), custom_call_target="tpu_custom_call" | custom-call | tf_op jit(solution)/shard_map/partial_sketch/pallas_call | solution.py:69
  2.9 0.5 %collective-permute-start = (f32[48,128]{1,0:T(8,128)S(1)}, f32[48,128]{1,0:T(8,128)S(1)}, u32[]{:S(2)}, u32[]{:S(2)}) collective-permute-start(f32[48,128]{1,0:T(8,128)S(1)} %get-tuple-element.12), channel_id=1, source_target_pairs={{0,1},{1,0},{2,3},{3,2},{4,5},{5,4},{6,7},{7,6},{8,9},{9,8},{10,11... | collective-permute-start | bytes 73736 | tf_op jit(solution)/shard_map/ppermute | solution.py:324
  3.4 0.8 %collective-permute-done = f32[48,128]{1,0:T(8,128)S(1)} collective-permute-done((f32[48,128]{1,0:T(8,128)S(1)}, f32[48,128]{1,0:T(8,128)S(1)}, u32[]{:S(2)}, u32[]{:S(2)}) %collective-permute-start) | collective-permute-done | bytes 24608 | tf_op jit(solution)/shard_map/ppermute | solution.py:324
  4.3 2.6 %collective-permute-start.1 = (f32[48,128]{1,0:T(8,128)S(1)}, f32[48,128]{1,0:T(8,128)S(1)}, u32[]{:S(2)}, u32[]{:S(2)}) collective-permute-start(f32[48,128]{1,0:T(8,128)S(1)} %add.12.sketch_ref), channel_id=1, source_target_pairs={{0,3},{1,2},{2,1},{3,0},{4,7},{5,6},{6,5},{7,4},{8,11},{9,10},{10,... | collective-permute-start | bytes 73736 | tf_op jit(solution)/shard_map/ppermute | solution.py:324
  6.9 1.5 %collective-permute-done.1 = f32[48,128]{1,0:T(8,128)S(1)} collective-permute-done((f32[48,128]{1,0:T(8,128)S(1)}, f32[48,128]{1,0:T(8,128)S(1)}, u32[]{:S(2)}, u32[]{:S(2)}) %collective-permute-start.1) | collective-permute-done | bytes 24608 | tf_op jit(solution)/shard_map/ppermute | solution.py:324
  8.4 1.8 %collective-permute-start.2 = (f32[48,128]{1,0:T(8,128)S(1)}, f32[48,128]{1,0:T(8,128)S(1)}, u32[]{:S(2)}, u32[]{:S(2)}) collective-permute-start(f32[48,128]{1,0:T(8,128)S(1)} %add.13), channel_id=1, source_target_pairs={{0,5},{1,4},{2,7},{3,6},{4,1},{5,0},{6,3},{7,2},{8,13},{9,12},{10,... | collective-permute-start | bytes 73736 | tf_op jit(solution)/shard_map/ppermute | solution.py:324
  10.2 1.6 %collective-permute-start.5 = (f32[4,128,128]{2,1,0:T(8,128)S(1)}, f32[4,128,128]{2,1,0:T(8,128)S(1)}, u32[]{:S(2)}, u32[]{:S(2)}) collective-permute-start(f32[4,128,128]{2,1,0:T(8,128)S(1)} %first_field.1), channel_id=1, source_target_pairs={{0,16},{1,17},{2,18},{3,19},{4,20},{5,21},{6,22},{7,23},{8,24},{9,... | collective-permute-start | bytes 786440 | tf_op jit(solution)/shard_map/ppermute | solution.py:324
  11.8 0.0 collective-permute-done.2
  11.8 2.7 %collective-permute-start.3 = (f32[48,128]{1,0:T(8,128)S(1)}, f32[48,128]{1,0:T(8,128)S(1)}, u32[]{:S(2)}, u32[]{:S(2)}) collective-permute-start(f32[48,128]{1,0:T(8,128)S(1)} %add.14), channel_id=1, source_target_pairs={{0,9},{1,8},{2,11},{3,10},{4,13},{5,12},{6,15},{7,14},{8,1},{9,0},... | collective-permute-start | bytes 73736 | tf_op jit(solution)/shard_map/ppermute | solution.py:324
  14.5 1.5 %collective-permute-done.3 = f32[48,128]{1,0:T(8,128)S(1)} collective-permute-done((f32[48,128]{1,0:T(8,128)S(1)}, f32[48,128]{1,0:T(8,128)S(1)}, u32[]{:S(2)}, u32[]{:S(2)}) %collective-permute-start.3) | collective-permute-done | bytes 24608 | tf_op jit(solution)/shard_map/ppermute | solution.py:324
  16.0 1.7 %collective-permute-start.4 = (f32[48,128]{1,0:T(8,128)S(1)}, f32[48,128]{1,0:T(8,128)S(1)}, u32[]{:S(2)}, u32[]{:S(2)}) collective-permute-start(f32[48,128]{1,0:T(8,128)S(1)} %add.15.sketch_ref), channel_id=1, source_target_pairs={{0,16},{1,17},{2,18},{3,19},{4,20},{5,21},{6,22},{7,23},{8,24},{9,... | collective-permute-start | bytes 73736 | tf_op jit(solution)/shard_map/ppermute | solution.py:324
  17.8 0.2 raw_product.1.refs_1_
  18.0 0.3 %collective-permute-start.6 = (f32[6,48,128]{2,1,0:T(8,128)S(1)}, f32[6,48,128]{2,1,0:T(8,128)S(1)}, u32[]{:S(2)}, u32[]{:S(2)}) collective-permute-start(f32[6,48,128]{2,1,0:T(8,128)S(1)} %raw_product.1.refs_1_), channel_id=1, source_target_pairs={{0,16},{1,17},{2,18},{3,19},{4,20},{5,21},{6,22},{7,23},{8,24},{9,... | collective-permute-start | bytes 442376 | tf_op jit(solution)/shard_map/ppermute | solution.py:324
  18.3 1.5 %collective-permute-done.4 = f32[48,128]{1,0:T(8,128)S(1)} collective-permute-done((f32[48,128]{1,0:T(8,128)S(1)}, f32[48,128]{1,0:T(8,128)S(1)}, u32[]{:S(2)}, u32[]{:S(2)}) %collective-permute-start.4) | collective-permute-done | bytes 24608 | tf_op jit(solution)/shard_map/ppermute | solution.py:324
  19.8 0.0 collective-permute-done.5.refs_0_
  19.8 1.9 %solve.1 = (f32[48,256]{1,0:T(8,128)S(1)}, f32[14,24,128]{2,1,0:T(8,128)S(1)}) custom-call(f32[48,256]{1,0:T(8,128)S(1)} %pad_maximum_fusion.sketch_ref, bf16[16,256,256]{2,1,0:T(8,128)(2,1)S(1)} %get-tuple-element.15.pairs_ref), custom_call_target="tpu_custom_call" | custom-call | flops 1073741824 | bytes 33554432 | tf_op jit(solution)/shard_map/solve/pallas_call | solution.py:245
  21.7 2.0 %collective-permute-start.8 = (f32[14,24,128]{2,1,0:T(8,128)S(1)}, f32[14,24,128]{2,1,0:T(8,128)S(1)}, u32[]{:S(2)}, u32[]{:S(2)}) collective-permute-start(f32[14,24,128]{2,1,0:T(8,128)S(1)} %get-tuple-element.18), channel_id=1, source_target_pairs={{0,16},{1,17},{2,18},{3,19},{4,20},{5,21},{6,22},{7,23},{8,24},{9,... | collective-permute-start | bytes 516104 | tf_op jit(solution)/shard_map/ppermute | solution.py:324
  23.7 0.2 others_ranks.1
  23.9 0.2 collective-permute-start.7
  24.1 0.6 %own_ranks.1.own_ref = f32[32,24,128]{2,1,0:T(8,128)S(1)} custom-call(f32[48,256]{1,0:T(8,128)S(1)} %pad_maximum_fusion.sketch_ref, f32[48,256]{1,0:T(8,128)S(1)} %get-tuple-element.16.solved_ref, bf16[16,256,256]{2,1,0:T(8,128)(2,1)S(1)} %get-tuple-element.15.pairs_ref, f32[4,128,128]{2,1,0:T(8,128)S(1)} %collective-permute-done.5.refs_0_, ...), custom_call_target="tpu_custom_call" | custom-call | flops 1073741824 | bytes 33554432 | tf_op jit(solution)/shard_map/own_ranks/pallas_call | solution.py:245
  24.7 3.7 %collective-permute-done.8.refs_0_ = f32[14,24,128]{2,1,0:T(8,128)S(1)} collective-permute-done((f32[14,24,128]{2,1,0:T(8,128)S(1)}, f32[14,24,128]{2,1,0:T(8,128)S(1)}, u32[]{:S(2)}, u32[]{:S(2)}) %collective-permute-start.8) | collective-permute-done | bytes 172064 | tf_op jit(solution)/shard_map/ppermute | solution.py:324
  28.4 0.8 %add_ranks.2.refs_1_ = f32[24,32,128]{2,1,0:T(8,128)} custom-call(f32[32,24,128]{2,1,0:T(8,128)S(1)} %own_ranks.1.own_ref, f32[14,24,128]{2,1,0:T(8,128)S(1)} %collective-permute-done.8.refs_0_), custom_call_target="tpu_custom_call" | custom-call | flops 1073741824 | bytes 33554432 | tf_op jit(solution)/shard_map/add_ranks/pallas_call | solution.py:301
  29.2 0.3 collective-permute-done.7.refs_0_
  29.5 0.7 %add_ranks.3 = f32[24,32,128]{2,1,0:T(8,128)} custom-call(f32[32,24,128]{2,1,0:T(8,128)S(1)} %own_ranks.1.own_ref, f32[8,24,128]{2,1,0:T(8,128)S(1)} %collective-permute-done.7.refs_0_, f32[24,32,128]{2,1,0:T(8,128)} %add_ranks.2.refs_1_), custom_call_target="tpu_custom_call", output_to_operand_aliasing={{}: (2, {})} | custom-call | tf_op jit(solution)/shard_map/add_ranks/pallas_call | solution.py:301
  (7 shorter events, 0.0 us)
Async XLA Ops:
  2.9 1.4 %collective-permute-start = (f32[48,128]{1,0:T(8,128)S(1)}, f32[48,128]{1,0:T(8,128)S(1)}, u32[]{:S(2)}, u32[]{:S(2)}) collective-permute-start(f32[48,128]{1,0:T(8,128)S(1)} %get-tuple-element.12), channel_id=1, source_target_pairs={{0,1},{1,0},{2,3},{3,2},{4,5},{5,4},{6,7},{7,6},{8,9},{9,8},{10,11... | collective-permute-start | bytes 73736 | tf_op jit(solution)/shard_map/ppermute | solution.py:324
  4.3 4.2 %collective-permute-start.1 = (f32[48,128]{1,0:T(8,128)S(1)}, f32[48,128]{1,0:T(8,128)S(1)}, u32[]{:S(2)}, u32[]{:S(2)}) collective-permute-start(f32[48,128]{1,0:T(8,128)S(1)} %add.12.sketch_ref), channel_id=1, source_target_pairs={{0,3},{1,2},{2,1},{3,0},{4,7},{5,6},{6,5},{7,4},{8,11},{9,10},{10,... | collective-permute-start | bytes 73736 | tf_op jit(solution)/shard_map/ppermute | solution.py:324
  8.4 3.4 %collective-permute-start.2 = (f32[48,128]{1,0:T(8,128)S(1)}, f32[48,128]{1,0:T(8,128)S(1)}, u32[]{:S(2)}, u32[]{:S(2)}) collective-permute-start(f32[48,128]{1,0:T(8,128)S(1)} %add.13), channel_id=1, source_target_pairs={{0,5},{1,4},{2,7},{3,6},{4,1},{5,0},{6,3},{7,2},{8,13},{9,12},{10,... | collective-permute-start | bytes 73736 | tf_op jit(solution)/shard_map/ppermute | solution.py:324
  10.2 9.6 %collective-permute-start.5 = (f32[4,128,128]{2,1,0:T(8,128)S(1)}, f32[4,128,128]{2,1,0:T(8,128)S(1)}, u32[]{:S(2)}, u32[]{:S(2)}) collective-permute-start(f32[4,128,128]{2,1,0:T(8,128)S(1)} %first_field.1), channel_id=1, source_target_pairs={{0,16},{1,17},{2,18},{3,19},{4,20},{5,21},{6,22},{7,23},{8,24},{9,... | collective-permute-start | bytes 786440 | tf_op jit(solution)/shard_map/ppermute | solution.py:324
  11.8 4.2 %collective-permute-start.3 = (f32[48,128]{1,0:T(8,128)S(1)}, f32[48,128]{1,0:T(8,128)S(1)}, u32[]{:S(2)}, u32[]{:S(2)}) collective-permute-start(f32[48,128]{1,0:T(8,128)S(1)} %add.14), channel_id=1, source_target_pairs={{0,9},{1,8},{2,11},{3,10},{4,13},{5,12},{6,15},{7,14},{8,1},{9,0},... | collective-permute-start | bytes 73736 | tf_op jit(solution)/shard_map/ppermute | solution.py:324
  16.0 3.8 %collective-permute-start.4 = (f32[48,128]{1,0:T(8,128)S(1)}, f32[48,128]{1,0:T(8,128)S(1)}, u32[]{:S(2)}, u32[]{:S(2)}) collective-permute-start(f32[48,128]{1,0:T(8,128)S(1)} %add.15.sketch_ref), channel_id=1, source_target_pairs={{0,16},{1,17},{2,18},{3,19},{4,20},{5,21},{6,22},{7,23},{8,24},{9,... | collective-permute-start | bytes 73736 | tf_op jit(solution)/shard_map/ppermute | solution.py:324
  18.0 6.1 %collective-permute-start.6 = (f32[6,48,128]{2,1,0:T(8,128)S(1)}, f32[6,48,128]{2,1,0:T(8,128)S(1)}, u32[]{:S(2)}, u32[]{:S(2)}) collective-permute-start(f32[6,48,128]{2,1,0:T(8,128)S(1)} %raw_product.1.refs_1_), channel_id=1, source_target_pairs={{0,16},{1,17},{2,18},{3,19},{4,20},{5,21},{6,22},{7,23},{8,24},{9,... | collective-permute-start | bytes 442376 | tf_op jit(solution)/shard_map/ppermute | solution.py:324
  21.7 6.7 %collective-permute-start.8 = (f32[14,24,128]{2,1,0:T(8,128)S(1)}, f32[14,24,128]{2,1,0:T(8,128)S(1)}, u32[]{:S(2)}, u32[]{:S(2)}) collective-permute-start(f32[14,24,128]{2,1,0:T(8,128)S(1)} %get-tuple-element.18), channel_id=1, source_target_pairs={{0,16},{1,17},{2,18},{3,19},{4,20},{5,21},{6,22},{7,23},{8,24},{9,... | collective-permute-start | bytes 516104 | tf_op jit(solution)/shard_map/ppermute | solution.py:324
  23.9 5.5 %collective-permute-start.7 = (f32[8,24,128]{2,1,0:T(8,128)S(1)}, f32[8,24,128]{2,1,0:T(8,128)S(1)}, u32[]{:S(2)}, u32[]{:S(2)}) collective-permute-start(f32[8,24,128]{2,1,0:T(8,128)S(1)} %others_ranks.1), channel_id=1, source_target_pairs={{0,16},{1,17},{2,18},{3,19},{4,20},{5,21},{6,22},{7,23},{8,24},{9,... | collective-permute-start | bytes 294920 | tf_op jit(solution)/shard_map/ppermute | solution.py:324

commit v8 on v7

--- a/solution.py
+++ b/solution.py
@@ -161,6 +161,10 @@
     out_ref[...] = field_ref[...]
 
 
+def mark_kernel(sketch_ref, out_ref):
+    out_ref[...] = sketch_ref[...]
+
+
 def raw_kernel(first, sketch_ref, pairs_ref, out_ref):
     multiply(sketch_ref[...], pairs_ref, first, [out_ref])
 
@@ -259,7 +263,7 @@
     summed = whole
     for bit in steps_of(parties):
         whole = jnp.concatenate([whole, exchange(whole, sizes, gx=bit)], axis=1)
-    mine = run(functools.partial(raw_kernel, early // 2), "raw_product", piece(raw, columns), summed, pairs)
+    mine = run(functools.partial(raw_kernel, early // 2), "raw_product", piece(raw, columns), summed, pairs, cost=RAW_COST)
     raw_parts = [mine] + [exchange(mine, sizes, gx=d) for d in range(1, parties)]
     whole, *fields = lax.optimization_barrier([whole, *fields])
     place, received = early + raw, []
@@ -313,6 +317,8 @@
     return out
 
 
+HELD_COST = pl.CostEstimate(flops=1 << 30, bytes_accessed=8 << 20, transcendentals=0)
+RAW_COST = pl.CostEstimate(flops=1 << 30, bytes_accessed=32 << 20, transcendentals=0)
 AXES = ("gx", "gy", "gz")
 
 
@@ -330,14 +336,17 @@
 
 def body(sizes, field, test):
     second = field.shape[1]
-    early, raw, last = second * 4 // 32, second * 6 // 32, second * 8 // 32
+    early, raw, last = second * 6 // 32, second * 6 // 32, second * 8 // 32
     sketch, pairs, first_field = partial_sketch(field, test, early)
     for bit in steps_of(sizes["gz"]):
         sketch = sketch + exchange(sketch, sizes, gz=bit | 1)
         if bit == 1:
             first_field = run(copy_kernel, "first_field", first_field, sketch, first_field)
     for bit in steps_of(sizes["gy"]):
-        sketch = sketch + exchange(sketch, sizes, gy=bit, gz=1)
+        coming = exchange(sketch, sizes, gy=bit, gz=1)
+        if bit:
+            sketch = run(mark_kernel, "held", jax.ShapeDtypeStruct(sketch.shape, F32), sketch, cost=HELD_COST)
+        sketch = sketch + coming
     return project(sketch, pairs, first_field, sizes, raw, (second - early - raw - last, last))
 
 

time: 30.3 us -> 30 us (0.990)
  waiting for transfers between devices: 9.4 us -> 8.98 us
    ppermute x9, waiting for transfers between devices: 9.4 us -> 8.98 us  [exchange(): return lax.ppermute(x, AXES, pairs)]
    pallas_call x5 -> x7, Pallas kernels: 2.91 us -> 2.89 us  [run(): pl.pallas_call(kernel, out_shape=out_shape, compiler_params=PARAMS, cost_...]
where the time goes in v8:
time: 30 us; the launch traced here: 29.9 us
  starting transfers between devices  13.6 us (45%)
  waiting for transfers between devices  8.98 us (30%)
  Pallas kernels  7.2 us (24%)
    ppermute x9, starting transfers between devices, exchange(): return lax.ppermute(x, AXES, pairs)  13.6 us
    ppermute x9, waiting for transfers between devices, exchange(): return lax.ppermute(x, AXES, pairs)  8.98 us
    pallas_call x7, Pallas kernels, run(): pl.pallas_call(kernel, out_shape=out_shape, compiler_params=PARAMS, cost_...  2.89 us
    pallas_call x1, Pallas kernels, partial_sketch(): pl.pallas_call(functools.partial(sketch_kernel, span), in_specs=[pl.Block...  2.87 us
    pallas_call x2, Pallas kernels, project(): pl.pallas_call(functools.partial(add_kernel, parties, begin, size), out_s...  1.44 us
  transfers between devices with their start and end apart: 9, of which 6 were waited for; matrix products, arithmetic and copies ran while one was open for 0% of the time, Pallas kernels for 12%

profile of v8, /device:TPU:0, one launch (start us, length us, event | category | flops | bytes accessed | tf_op | source)
XLA Modules:
  0.0 29.9 jit_solution(4280061694119602336)
XLA Ops:
  0.0 2.9 %partial_sketch.1 = (f32[48,128]{1,0:T(8,128)S(1)}, bf16[16,256,256]{2,1,0:T(8,128)(2,1)S(1)}, f32[6,128,128]{2,1,0:T(8,128)S(1)}) custom-call(f32[128,32,128]{2,1,0:T(8,128)} %field_hbm.1, f32[48,32,128]{2,1,0:T(8,128)} %test_hbm.1), custom_call_target="tpu_custom_call" | custom-call | tf_op jit(solution)/shard_map/partial_sketch/pallas_call | solution.py:69
  2.9 0.5 %collective-permute-start = (f32[48,128]{1,0:T(8,128)S(1)}, f32[48,128]{1,0:T(8,128)S(1)}, u32[]{:S(2)}, u32[]{:S(2)}) collective-permute-start(f32[48,128]{1,0:T(8,128)S(1)} %get-tuple-element.12), channel_id=1, source_target_pairs={{0,1},{1,0},{2,3},{3,2},{4,5},{5,4},{6,7},{7,6},{8,9},{9,8},{10,11... | collective-permute-start | bytes 73736 | tf_op jit(solution)/shard_map/ppermute | solution.py:330
  3.4 0.8 %collective-permute-done = f32[48,128]{1,0:T(8,128)S(1)} collective-permute-done((f32[48,128]{1,0:T(8,128)S(1)}, f32[48,128]{1,0:T(8,128)S(1)}, u32[]{:S(2)}, u32[]{:S(2)}) %collective-permute-start) | collective-permute-done | bytes 24608 | tf_op jit(solution)/shard_map/ppermute | solution.py:330
  4.3 2.6 %collective-permute-start.1 = (f32[48,128]{1,0:T(8,128)S(1)}, f32[48,128]{1,0:T(8,128)S(1)}, u32[]{:S(2)}, u32[]{:S(2)}) collective-permute-start(f32[48,128]{1,0:T(8,128)S(1)} %add.12.sketch_ref), channel_id=1, source_target_pairs={{0,3},{1,2},{2,1},{3,0},{4,7},{5,6},{6,5},{7,4},{8,11},{9,10},{10,... | collective-permute-start | bytes 73736 | tf_op jit(solution)/shard_map/ppermute | solution.py:330
  6.9 1.6 %collective-permute-start.5 = (f32[6,128,128]{2,1,0:T(8,128)S(1)}, f32[6,128,128]{2,1,0:T(8,128)S(1)}, u32[]{:S(2)}, u32[]{:S(2)}) collective-permute-start(f32[6,128,128]{2,1,0:T(8,128)S(1)} %first_field.1), channel_id=1, source_target_pairs={{0,16},{1,17},{2,18},{3,19},{4,20},{5,21},{6,22},{7,23},{8,24},{9,... | collective-permute-start | bytes 1179656 | tf_op jit(solution)/shard_map/ppermute | solution.py:330
  8.5 0.0 collective-permute-done.1
  8.5 1.7 %collective-permute-start.2 = (f32[48,128]{1,0:T(8,128)S(1)}, f32[48,128]{1,0:T(8,128)S(1)}, u32[]{:S(2)}, u32[]{:S(2)}) collective-permute-start(f32[48,128]{1,0:T(8,128)S(1)} %add.13.sketch_ref), channel_id=1, source_target_pairs={{0,5},{1,4},{2,7},{3,6},{4,1},{5,0},{6,3},{7,2},{8,13},{9,12},{10,... | collective-permute-start | bytes 73736 | tf_op jit(solution)/shard_map/ppermute | solution.py:330
  10.2 1.6 %collective-permute-done.2 = f32[48,128]{1,0:T(8,128)S(1)} collective-permute-done((f32[48,128]{1,0:T(8,128)S(1)}, f32[48,128]{1,0:T(8,128)S(1)}, u32[]{:S(2)}, u32[]{:S(2)}) %collective-permute-start.2) | collective-permute-done | bytes 24608 | tf_op jit(solution)/shard_map/ppermute | solution.py:330
  11.8 3.0 %collective-permute-start.3 = (f32[48,128]{1,0:T(8,128)S(1)}, f32[48,128]{1,0:T(8,128)S(1)}, u32[]{:S(2)}, u32[]{:S(2)}) collective-permute-start(f32[48,128]{1,0:T(8,128)S(1)} %add.14.sketch_ref), channel_id=1, source_target_pairs={{0,9},{1,8},{2,11},{3,10},{4,13},{5,12},{6,15},{7,14},{8,1},{9,0},... | collective-permute-start | bytes 73736 | tf_op jit(solution)/shard_map/ppermute | solution.py:330
  14.8 1.5 %collective-permute-done.3 = f32[48,128]{1,0:T(8,128)S(1)} collective-permute-done((f32[48,128]{1,0:T(8,128)S(1)}, f32[48,128]{1,0:T(8,128)S(1)}, u32[]{:S(2)}, u32[]{:S(2)}) %collective-permute-start.3) | collective-permute-done | bytes 24608 | tf_op jit(solution)/shard_map/ppermute | solution.py:330
  16.3 1.5 %collective-permute-start.4 = (f32[48,128]{1,0:T(8,128)S(1)}, f32[48,128]{1,0:T(8,128)S(1)}, u32[]{:S(2)}, u32[]{:S(2)}) collective-permute-start(f32[48,128]{1,0:T(8,128)S(1)} %add.15.sketch_ref), channel_id=1, source_target_pairs={{0,16},{1,17},{2,18},{3,19},{4,20},{5,21},{6,22},{7,23},{8,24},{9,... | collective-permute-start | bytes 73736 | tf_op jit(solution)/shard_map/ppermute | solution.py:330
  17.8 0.2 raw_product.1.refs_1_
  18.0 0.6 %collective-permute-start.6 = (f32[6,48,128]{2,1,0:T(8,128)S(1)}, f32[6,48,128]{2,1,0:T(8,128)S(1)}, u32[]{:S(2)}, u32[]{:S(2)}) collective-permute-start(f32[6,48,128]{2,1,0:T(8,128)S(1)} %raw_product.1.refs_1_), channel_id=1, source_target_pairs={{0,16},{1,17},{2,18},{3,19},{4,20},{5,21},{6,22},{7,23},{8,24},{9,... | collective-permute-start | bytes 442376 | tf_op jit(solution)/shard_map/ppermute | solution.py:330
  18.6 1.5 %collective-permute-done.4 = f32[48,128]{1,0:T(8,128)S(1)} collective-permute-done((f32[48,128]{1,0:T(8,128)S(1)}, f32[48,128]{1,0:T(8,128)S(1)}, u32[]{:S(2)}, u32[]{:S(2)}) %collective-permute-start.4) | collective-permute-done | bytes 24608 | tf_op jit(solution)/shard_map/ppermute | solution.py:330
  20.1 1.8 %solve.1 = (f32[48,256]{1,0:T(8,128)S(1)}, f32[12,24,128]{2,1,0:T(8,128)S(1)}) custom-call(f32[48,256]{1,0:T(8,128)S(1)} %pad_maximum_fusion.sketch_ref, bf16[16,256,256]{2,1,0:T(8,128)(2,1)S(1)} %get-tuple-element.15.pairs_ref), custom_call_target="tpu_custom_call" | custom-call | flops 1073741824 | bytes 33554432 | tf_op jit(solution)/shard_map/solve/pallas_call | solution.py:249
  22.0 1.8 %collective-permute-start.8 = (f32[12,24,128]{2,1,0:T(8,128)S(1)}, f32[12,24,128]{2,1,0:T(8,128)S(1)}, u32[]{:S(2)}, u32[]{:S(2)}) collective-permute-start(f32[12,24,128]{2,1,0:T(8,128)S(1)} %get-tuple-element.18), channel_id=1, source_target_pairs={{0,16},{1,17},{2,18},{3,19},{4,20},{5,21},{6,22},{7,23},{8,24},{9,... | collective-permute-start | bytes 442376 | tf_op jit(solution)/shard_map/ppermute | solution.py:330
  23.8 0.2 others_ranks.1
  24.0 0.3 %collective-permute-start.7 = (f32[8,24,128]{2,1,0:T(8,128)S(1)}, f32[8,24,128]{2,1,0:T(8,128)S(1)}, u32[]{:S(2)}, u32[]{:S(2)}) collective-permute-start(f32[8,24,128]{2,1,0:T(8,128)S(1)} %others_ranks.1), channel_id=1, source_target_pairs={{0,16},{1,17},{2,18},{3,19},{4,20},{5,21},{6,22},{7,23},{8,24},{9,... | collective-permute-start | bytes 294920 | tf_op jit(solution)/shard_map/ppermute | solution.py:330
  24.3 0.0 collective-permute-done.6.refs_2_
  24.3 0.6 %own_ranks.1.own_ref = f32[32,24,128]{2,1,0:T(8,128)S(1)} custom-call(f32[48,256]{1,0:T(8,128)S(1)} %pad_maximum_fusion.sketch_ref, f32[48,256]{1,0:T(8,128)S(1)} %get-tuple-element.16.solved_ref, bf16[16,256,256]{2,1,0:T(8,128)(2,1)S(1)} %get-tuple-element.15.pairs_ref, f32[6,128,128]{2,1,0:T(8,128)S(1)} %collective-permute-done.5.refs_0_, ...), custom_call_target="tpu_custom_call" | custom-call | flops 1073741824 | bytes 33554432 | tf_op jit(solution)/shard_map/own_ranks/pallas_call | solution.py:249
  25.0 3.2 %collective-permute-done.8.refs_0_ = f32[12,24,128]{2,1,0:T(8,128)S(1)} collective-permute-done((f32[12,24,128]{2,1,0:T(8,128)S(1)}, f32[12,24,128]{2,1,0:T(8,128)S(1)}, u32[]{:S(2)}, u32[]{:S(2)}) %collective-permute-start.8) | collective-permute-done | bytes 147488 | tf_op jit(solution)/shard_map/ppermute | solution.py:330
  28.2 0.8 %add_ranks.2.refs_1_ = f32[24,32,128]{2,1,0:T(8,128)} custom-call(f32[32,24,128]{2,1,0:T(8,128)S(1)} %own_ranks.1.own_ref, f32[12,24,128]{2,1,0:T(8,128)S(1)} %collective-permute-done.8.refs_0_), custom_call_target="tpu_custom_call" | custom-call | flops 1073741824 | bytes 33554432 | tf_op jit(solution)/shard_map/add_ranks/pallas_call | solution.py:305
  29.0 0.3 collective-permute-done.7.refs_0_
  29.2 0.7 %add_ranks.3 = f32[24,32,128]{2,1,0:T(8,128)} custom-call(f32[32,24,128]{2,1,0:T(8,128)S(1)} %own_ranks.1.own_ref, f32[8,24,128]{2,1,0:T(8,128)S(1)} %collective-permute-done.7.refs_0_, f32[24,32,128]{2,1,0:T(8,128)} %add_ranks.2.refs_1_), custom_call_target="tpu_custom_call", output_to_operand_aliasing={{}: (2, {})} | custom-call | tf_op jit(solution)/shard_map/add_ranks/pallas_call | solution.py:305
  (9 shorter events, 0.1 us)
Async XLA Ops:
  2.9 1.4 %collective-permute-start = (f32[48,128]{1,0:T(8,128)S(1)}, f32[48,128]{1,0:T(8,128)S(1)}, u32[]{:S(2)}, u32[]{:S(2)}) collective-permute-start(f32[48,128]{1,0:T(8,128)S(1)} %get-tuple-element.12), channel_id=1, source_target_pairs={{0,1},{1,0},{2,3},{3,2},{4,5},{5,4},{6,7},{7,6},{8,9},{9,8},{10,11... | collective-permute-start | bytes 73736 | tf_op jit(solution)/shard_map/ppermute | solution.py:330
  4.3 4.2 %collective-permute-start.1 = (f32[48,128]{1,0:T(8,128)S(1)}, f32[48,128]{1,0:T(8,128)S(1)}, u32[]{:S(2)}, u32[]{:S(2)}) collective-permute-start(f32[48,128]{1,0:T(8,128)S(1)} %add.12.sketch_ref), channel_id=1, source_target_pairs={{0,3},{1,2},{2,1},{3,0},{4,7},{5,6},{6,5},{7,4},{8,11},{9,10},{10,... | collective-permute-start | bytes 73736 | tf_op jit(solution)/shard_map/ppermute | solution.py:330
  6.9 13.2 %collective-permute-start.5 = (f32[6,128,128]{2,1,0:T(8,128)S(1)}, f32[6,128,128]{2,1,0:T(8,128)S(1)}, u32[]{:S(2)}, u32[]{:S(2)}) collective-permute-start(f32[6,128,128]{2,1,0:T(8,128)S(1)} %first_field.1), channel_id=1, source_target_pairs={{0,16},{1,17},{2,18},{3,19},{4,20},{5,21},{6,22},{7,23},{8,24},{9,... | collective-permute-start | bytes 1179656 | tf_op jit(solution)/shard_map/ppermute | solution.py:330
  8.5 3.3 %collective-permute-start.2 = (f32[48,128]{1,0:T(8,128)S(1)}, f32[48,128]{1,0:T(8,128)S(1)}, u32[]{:S(2)}, u32[]{:S(2)}) collective-permute-start(f32[48,128]{1,0:T(8,128)S(1)} %add.13.sketch_ref), channel_id=1, source_target_pairs={{0,5},{1,4},{2,7},{3,6},{4,1},{5,0},{6,3},{7,2},{8,13},{9,12},{10,... | collective-permute-start | bytes 73736 | tf_op jit(solution)/shard_map/ppermute | solution.py:330
  11.8 4.5 %collective-permute-start.3 = (f32[48,128]{1,0:T(8,128)S(1)}, f32[48,128]{1,0:T(8,128)S(1)}, u32[]{:S(2)}, u32[]{:S(2)}) collective-permute-start(f32[48,128]{1,0:T(8,128)S(1)} %add.14.sketch_ref), channel_id=1, source_target_pairs={{0,9},{1,8},{2,11},{3,10},{4,13},{5,12},{6,15},{7,14},{8,1},{9,0},... | collective-permute-start | bytes 73736 | tf_op jit(solution)/shard_map/ppermute | solution.py:330
  16.3 3.8 %collective-permute-start.4 = (f32[48,128]{1,0:T(8,128)S(1)}, f32[48,128]{1,0:T(8,128)S(1)}, u32[]{:S(2)}, u32[]{:S(2)}) collective-permute-start(f32[48,128]{1,0:T(8,128)S(1)} %add.15.sketch_ref), channel_id=1, source_target_pairs={{0,16},{1,17},{2,18},{3,19},{4,20},{5,21},{6,22},{7,23},{8,24},{9,... | collective-permute-start | bytes 73736 | tf_op jit(solution)/shard_map/ppermute | solution.py:330
  18.0 6.3 %collective-permute-start.6 = (f32[6,48,128]{2,1,0:T(8,128)S(1)}, f32[6,48,128]{2,1,0:T(8,128)S(1)}, u32[]{:S(2)}, u32[]{:S(2)}) collective-permute-start(f32[6,48,128]{2,1,0:T(8,128)S(1)} %raw_product.1.refs_1_), channel_id=1, source_target_pairs={{0,16},{1,17},{2,18},{3,19},{4,20},{5,21},{6,22},{7,23},{8,24},{9,... | collective-permute-start | bytes 442376 | tf_op jit(solution)/shard_map/ppermute | solution.py:330
  22.0 6.2 %collective-permute-start.8 = (f32[12,24,128]{2,1,0:T(8,128)S(1)}, f32[12,24,128]{2,1,0:T(8,128)S(1)}, u32[]{:S(2)}, u32[]{:S(2)}) collective-permute-start(f32[12,24,128]{2,1,0:T(8,128)S(1)} %get-tuple-element.18), channel_id=1, source_target_pairs={{0,16},{1,17},{2,18},{3,19},{4,20},{5,21},{6,22},{7,23},{8,24},{9,... | collective-permute-start | bytes 442376 | tf_op jit(solution)/shard_map/ppermute | solution.py:330
  24.0 5.2 %collective-permute-start.7 = (f32[8,24,128]{2,1,0:T(8,128)S(1)}, f32[8,24,128]{2,1,0:T(8,128)S(1)}, u32[]{:S(2)}, u32[]{:S(2)}) collective-permute-start(f32[8,24,128]{2,1,0:T(8,128)S(1)} %others_ranks.1), channel_id=1, source_target_pairs={{0,16},{1,17},{2,18},{3,19},{4,20},{5,21},{6,22},{7,23},{8,24},{9,... | collective-permute-start | bytes 294920 | tf_op jit(solution)/shard_map/ppermute | solution.py:330

commit v9 on v8

--- a/solution.py
+++ b/solution.py
@@ -35,6 +35,7 @@
             copy.start()
             copies.append(copy)
     total = low = None
+    dot = functools.partial(lax.dot_general, dimension_numbers=NN, preferred_element_type=F32)
     for step in range(steps):
         copies[2 * step].wait()
         copies[2 * step + 1].wait()
@@ -42,22 +43,20 @@
         flat_test = test.at[step].reshape(columns * span, lanes)
         for pair in range(span // 2):
             x = [flat_field[pl.ds(2 * pair + q, rows, stride=span), :] for q in range(2)]
+            t = [flat_test[pl.ds(2 * pair + q, columns, stride=span), :] for q in range(2)]
             for q in range(2):
                 if step * span + 2 * pair + q < first_ref.shape[0]:
                     first_ref[step * span + 2 * pair + q] = x[q]
-            x = jnp.concatenate(x, axis=1)
-            t = jnp.concatenate([flat_test[pl.ds(2 * pair + q, columns, stride=span), :] for q in range(2)], axis=1)
-            x = split(x, 3)
-            t = split(t, 3)
-            weights = jnp.concatenate(x[:2], axis=0)
-            pairs_ref[step * span // 2 + pair] = weights
-            term = lax.dot_general(jnp.concatenate(t, axis=0), weights, NT, preferred_element_type=F32)
-            rest = lax.dot_general(t[0], x[2], NT, preferred_element_type=F32)
+            pairs_ref[step * span // 2 + pair] = jnp.concatenate(split(jnp.concatenate(x, axis=1), 2), axis=0)
+            t = split(jnp.concatenate(t, axis=1), 3)
+            turned = split(jnp.concatenate([part.T for part in x], axis=0), 3)
+            term = dot(jnp.concatenate(t, axis=0), jnp.concatenate(turned[:2], axis=1))
+            rest = dot(t[0], turned[2])
             total = term if total is None else total + term
             low = rest if low is None else low + rest
     for part in reversed(range(3)):
         block = total[part * columns : (part + 1) * columns]
-        low = low + block[:, rows:] + block[:, :rows] if part else (low + block[:, rows:]) + block[:, :rows]
+        low = (low + block[:, rows:]) + block[:, :rows]
     sketch_ref[...] = low
 
 

time: 30 us -> 30 us (level)
  no operation moved by 1% of the time
where the time goes in v9:
time: 30 us; the launch traced here: 29.8 us
  starting transfers between devices  13.6 us (45%)
  waiting for transfers between devices  8.97 us (30%)
  Pallas kernels  7.12 us (24%)
    ppermute x9, starting transfers between devices, exchange(): return lax.ppermute(x, AXES, pairs)  13.6 us
    ppermute x9, waiting for transfers between devices, exchange(): return lax.ppermute(x, AXES, pairs)  8.97 us
    pallas_call x7, Pallas kernels, run(): pl.pallas_call(kernel, out_shape=out_shape, compiler_params=PARAMS, cost_...  2.9 us
    pallas_call x1, Pallas kernels, partial_sketch(): pl.pallas_call(functools.partial(sketch_kernel, span), in_specs=[pl.Block...  2.78 us
    pallas_call x2, Pallas kernels, project(): pl.pallas_call(functools.partial(add_kernel, parties, begin, size), out_s...  1.44 us
  transfers between devices with their start and end apart: 9, of which 6 were waited for; matrix products, arithmetic and copies ran while one was open for 0% of the time, Pallas kernels for 12%

profile of v9, /device:TPU:0, one launch (start us, length us, event | category | flops | bytes accessed | tf_op | source)
XLA Modules:
  0.0 29.8 jit_solution(498749392058773361)
XLA Ops:
  0.0 2.8 %partial_sketch.1 = (f32[48,128]{1,0:T(8,128)S(1)}, bf16[16,256,256]{2,1,0:T(8,128)(2,1)S(1)}, f32[6,128,128]{2,1,0:T(8,128)S(1)}) custom-call(f32[128,32,128]{2,1,0:T(8,128)} %field_hbm.1, f32[48,32,128]{2,1,0:T(8,128)} %test_hbm.1), custom_call_target="tpu_custom_call" | custom-call | tf_op jit(solution)/shard_map/partial_sketch/pallas_call | solution.py:68
  2.8 0.5 %collective-permute-start = (f32[48,128]{1,0:T(8,128)S(1)}, f32[48,128]{1,0:T(8,128)S(1)}, u32[]{:S(2)}, u32[]{:S(2)}) collective-permute-start(f32[48,128]{1,0:T(8,128)S(1)} %get-tuple-element.12), channel_id=1, source_target_pairs={{0,1},{1,0},{2,3},{3,2},{4,5},{5,4},{6,7},{7,6},{8,9},{9,8},{10,11... | collective-permute-start | bytes 73736 | tf_op jit(solution)/shard_map/ppermute | solution.py:329
  3.3 0.8 %collective-permute-done = f32[48,128]{1,0:T(8,128)S(1)} collective-permute-done((f32[48,128]{1,0:T(8,128)S(1)}, f32[48,128]{1,0:T(8,128)S(1)}, u32[]{:S(2)}, u32[]{:S(2)}) %collective-permute-start) | collective-permute-done | bytes 24608 | tf_op jit(solution)/shard_map/ppermute | solution.py:329
  4.2 2.6 %collective-permute-start.1 = (f32[48,128]{1,0:T(8,128)S(1)}, f32[48,128]{1,0:T(8,128)S(1)}, u32[]{:S(2)}, u32[]{:S(2)}) collective-permute-start(f32[48,128]{1,0:T(8,128)S(1)} %add.12.sketch_ref), channel_id=1, source_target_pairs={{0,3},{1,2},{2,1},{3,0},{4,7},{5,6},{6,5},{7,4},{8,11},{9,10},{10,... | collective-permute-start | bytes 73736 | tf_op jit(solution)/shard_map/ppermute | solution.py:329
  6.8 1.6 %collective-permute-start.5 = (f32[6,128,128]{2,1,0:T(8,128)S(1)}, f32[6,128,128]{2,1,0:T(8,128)S(1)}, u32[]{:S(2)}, u32[]{:S(2)}) collective-permute-start(f32[6,128,128]{2,1,0:T(8,128)S(1)} %first_field.1), channel_id=1, source_target_pairs={{0,16},{1,17},{2,18},{3,19},{4,20},{5,21},{6,22},{7,23},{8,24},{9,... | collective-permute-start | bytes 1179656 | tf_op jit(solution)/shard_map/ppermute | solution.py:329
  8.4 0.0 collective-permute-done.1
  8.4 1.7 %collective-permute-start.2 = (f32[48,128]{1,0:T(8,128)S(1)}, f32[48,128]{1,0:T(8,128)S(1)}, u32[]{:S(2)}, u32[]{:S(2)}) collective-permute-start(f32[48,128]{1,0:T(8,128)S(1)} %add.13.sketch_ref), channel_id=1, source_target_pairs={{0,5},{1,4},{2,7},{3,6},{4,1},{5,0},{6,3},{7,2},{8,13},{9,12},{10,... | collective-permute-start | bytes 73736 | tf_op jit(solution)/shard_map/ppermute | solution.py:329
  10.1 1.6 %collective-permute-done.2 = f32[48,128]{1,0:T(8,128)S(1)} collective-permute-done((f32[48,128]{1,0:T(8,128)S(1)}, f32[48,128]{1,0:T(8,128)S(1)}, u32[]{:S(2)}, u32[]{:S(2)}) %collective-permute-start.2) | collective-permute-done | bytes 24608 | tf_op jit(solution)/shard_map/ppermute | solution.py:329
  11.7 3.0 %collective-permute-start.3 = (f32[48,128]{1,0:T(8,128)S(1)}, f32[48,128]{1,0:T(8,128)S(1)}, u32[]{:S(2)}, u32[]{:S(2)}) collective-permute-start(f32[48,128]{1,0:T(8,128)S(1)} %add.14.sketch_ref), channel_id=1, source_target_pairs={{0,9},{1,8},{2,11},{3,10},{4,13},{5,12},{6,15},{7,14},{8,1},{9,0},... | collective-permute-start | bytes 73736 | tf_op jit(solution)/shard_map/ppermute | solution.py:329
  14.7 1.5 %collective-permute-done.3 = f32[48,128]{1,0:T(8,128)S(1)} collective-permute-done((f32[48,128]{1,0:T(8,128)S(1)}, f32[48,128]{1,0:T(8,128)S(1)}, u32[]{:S(2)}, u32[]{:S(2)}) %collective-permute-start.3) | collective-permute-done | bytes 24608 | tf_op jit(solution)/shard_map/ppermute | solution.py:329
  16.2 1.5 %collective-permute-start.4 = (f32[48,128]{1,0:T(8,128)S(1)}, f32[48,128]{1,0:T(8,128)S(1)}, u32[]{:S(2)}, u32[]{:S(2)}) collective-permute-start(f32[48,128]{1,0:T(8,128)S(1)} %add.15.sketch_ref), channel_id=1, source_target_pairs={{0,16},{1,17},{2,18},{3,19},{4,20},{5,21},{6,22},{7,23},{8,24},{9,... | collective-permute-start | bytes 73736 | tf_op jit(solution)/shard_map/ppermute | solution.py:329
  17.7 0.2 raw_product.1.refs_1_
  17.9 0.6 %collective-permute-start.6 = (f32[6,48,128]{2,1,0:T(8,128)S(1)}, f32[6,48,128]{2,1,0:T(8,128)S(1)}, u32[]{:S(2)}, u32[]{:S(2)}) collective-permute-start(f32[6,48,128]{2,1,0:T(8,128)S(1)} %raw_product.1.refs_1_), channel_id=1, source_target_pairs={{0,16},{1,17},{2,18},{3,19},{4,20},{5,21},{6,22},{7,23},{8,24},{9,... | collective-permute-start | bytes 442376 | tf_op jit(solution)/shard_map/ppermute | solution.py:329
  18.5 1.5 %collective-permute-done.4 = f32[48,128]{1,0:T(8,128)S(1)} collective-permute-done((f32[48,128]{1,0:T(8,128)S(1)}, f32[48,128]{1,0:T(8,128)S(1)}, u32[]{:S(2)}, u32[]{:S(2)}) %collective-permute-start.4) | collective-permute-done | bytes 24608 | tf_op jit(solution)/shard_map/ppermute | solution.py:329
  20.0 1.8 %solve.1 = (f32[48,256]{1,0:T(8,128)S(1)}, f32[12,24,128]{2,1,0:T(8,128)S(1)}) custom-call(f32[48,256]{1,0:T(8,128)S(1)} %pad_maximum_fusion.sketch_ref, bf16[16,256,256]{2,1,0:T(8,128)(2,1)S(1)} %get-tuple-element.15.pairs_ref), custom_call_target="tpu_custom_call" | custom-call | flops 1073741824 | bytes 33554432 | tf_op jit(solution)/shard_map/solve/pallas_call | solution.py:248
  21.9 1.8 %collective-permute-start.8 = (f32[12,24,128]{2,1,0:T(8,128)S(1)}, f32[12,24,128]{2,1,0:T(8,128)S(1)}, u32[]{:S(2)}, u32[]{:S(2)}) collective-permute-start(f32[12,24,128]{2,1,0:T(8,128)S(1)} %get-tuple-element.18), channel_id=1, source_target_pairs={{0,16},{1,17},{2,18},{3,19},{4,20},{5,21},{6,22},{7,23},{8,24},{9,... | collective-permute-start | bytes 442376 | tf_op jit(solution)/shard_map/ppermute | solution.py:329
  23.7 0.2 others_ranks.1
  23.9 0.3 %collective-permute-start.7 = (f32[8,24,128]{2,1,0:T(8,128)S(1)}, f32[8,24,128]{2,1,0:T(8,128)S(1)}, u32[]{:S(2)}, u32[]{:S(2)}) collective-permute-start(f32[8,24,128]{2,1,0:T(8,128)S(1)} %others_ranks.1), channel_id=1, source_target_pairs={{0,16},{1,17},{2,18},{3,19},{4,20},{5,21},{6,22},{7,23},{8,24},{9,... | collective-permute-start | bytes 294920 | tf_op jit(solution)/shard_map/ppermute | solution.py:329
  24.2 0.0 collective-permute-done.6.refs_2_
  24.2 0.6 %own_ranks.1.own_ref = f32[32,24,128]{2,1,0:T(8,128)S(1)} custom-call(f32[48,256]{1,0:T(8,128)S(1)} %pad_maximum_fusion.sketch_ref, f32[48,256]{1,0:T(8,128)S(1)} %get-tuple-element.16.solved_ref, bf16[16,256,256]{2,1,0:T(8,128)(2,1)S(1)} %get-tuple-element.15.pairs_ref, f32[6,128,128]{2,1,0:T(8,128)S(1)} %collective-permute-done.5.refs_0_, ...), custom_call_target="tpu_custom_call" | custom-call | flops 1073741824 | bytes 33554432 | tf_op jit(solution)/shard_map/own_ranks/pallas_call | solution.py:248
  24.9 3.2 %collective-permute-done.8.refs_0_ = f32[12,24,128]{2,1,0:T(8,128)S(1)} collective-permute-done((f32[12,24,128]{2,1,0:T(8,128)S(1)}, f32[12,24,128]{2,1,0:T(8,128)S(1)}, u32[]{:S(2)}, u32[]{:S(2)}) %collective-permute-start.8) | collective-permute-done | bytes 147488 | tf_op jit(solution)/shard_map/ppermute | solution.py:329
  28.1 0.8 %add_ranks.2.refs_1_ = f32[24,32,128]{2,1,0:T(8,128)} custom-call(f32[32,24,128]{2,1,0:T(8,128)S(1)} %own_ranks.1.own_ref, f32[12,24,128]{2,1,0:T(8,128)S(1)} %collective-permute-done.8.refs_0_), custom_call_target="tpu_custom_call" | custom-call | flops 1073741824 | bytes 33554432 | tf_op jit(solution)/shard_map/add_ranks/pallas_call | solution.py:304
  28.9 0.3 collective-permute-done.7.refs_0_
  29.2 0.7 %add_ranks.3 = f32[24,32,128]{2,1,0:T(8,128)} custom-call(f32[32,24,128]{2,1,0:T(8,128)S(1)} %own_ranks.1.own_ref, f32[8,24,128]{2,1,0:T(8,128)S(1)} %collective-permute-done.7.refs_0_, f32[24,32,128]{2,1,0:T(8,128)} %add_ranks.2.refs_1_), custom_call_target="tpu_custom_call", output_to_operand_aliasing={{}: (2, {})} | custom-call | tf_op jit(solution)/shard_map/add_ranks/pallas_call | solution.py:304
  (9 shorter events, 0.1 us)
Async XLA Ops:
  2.8 1.4 %collective-permute-start = (f32[48,128]{1,0:T(8,128)S(1)}, f32[48,128]{1,0:T(8,128)S(1)}, u32[]{:S(2)}, u32[]{:S(2)}) collective-permute-start(f32[48,128]{1,0:T(8,128)S(1)} %get-tuple-element.12), channel_id=1, source_target_pairs={{0,1},{1,0},{2,3},{3,2},{4,5},{5,4},{6,7},{7,6},{8,9},{9,8},{10,11... | collective-permute-start | bytes 73736 | tf_op jit(solution)/shard_map/ppermute | solution.py:329
  4.2 4.2 %collective-permute-start.1 = (f32[48,128]{1,0:T(8,128)S(1)}, f32[48,128]{1,0:T(8,128)S(1)}, u32[]{:S(2)}, u32[]{:S(2)}) collective-permute-start(f32[48,128]{1,0:T(8,128)S(1)} %add.12.sketch_ref), channel_id=1, source_target_pairs={{0,3},{1,2},{2,1},{3,0},{4,7},{5,6},{6,5},{7,4},{8,11},{9,10},{10,... | collective-permute-start | bytes 73736 | tf_op jit(solution)/shard_map/ppermute | solution.py:329
  6.8 13.2 %collective-permute-start.5 = (f32[6,128,128]{2,1,0:T(8,128)S(1)}, f32[6,128,128]{2,1,0:T(8,128)S(1)}, u32[]{:S(2)}, u32[]{:S(2)}) collective-permute-start(f32[6,128,128]{2,1,0:T(8,128)S(1)} %first_field.1), channel_id=1, source_target_pairs={{0,16},{1,17},{2,18},{3,19},{4,20},{5,21},{6,22},{7,23},{8,24},{9,... | collective-permute-start | bytes 1179656 | tf_op jit(solution)/shard_map/ppermute | solution.py:329
  8.4 3.3 %collective-permute-start.2 = (f32[48,128]{1,0:T(8,128)S(1)}, f32[48,128]{1,0:T(8,128)S(1)}, u32[]{:S(2)}, u32[]{:S(2)}) collective-permute-start(f32[48,128]{1,0:T(8,128)S(1)} %add.13.sketch_ref), channel_id=1, source_target_pairs={{0,5},{1,4},{2,7},{3,6},{4,1},{5,0},{6,3},{7,2},{8,13},{9,12},{10,... | collective-permute-start | bytes 73736 | tf_op jit(solution)/shard_map/ppermute | solution.py:329
  11.7 4.5 %collective-permute-start.3 = (f32[48,128]{1,0:T(8,128)S(1)}, f32[48,128]{1,0:T(8,128)S(1)}, u32[]{:S(2)}, u32[]{:S(2)}) collective-permute-start(f32[48,128]{1,0:T(8,128)S(1)} %add.14.sketch_ref), channel_id=1, source_target_pairs={{0,9},{1,8},{2,11},{3,10},{4,13},{5,12},{6,15},{7,14},{8,1},{9,0},... | collective-permute-start | bytes 73736 | tf_op jit(solution)/shard_map/ppermute | solution.py:329
  16.2 3.8 %collective-permute-start.4 = (f32[48,128]{1,0:T(8,128)S(1)}, f32[48,128]{1,0:T(8,128)S(1)}, u32[]{:S(2)}, u32[]{:S(2)}) collective-permute-start(f32[48,128]{1,0:T(8,128)S(1)} %add.15.sketch_ref), channel_id=1, source_target_pairs={{0,16},{1,17},{2,18},{3,19},{4,20},{5,21},{6,22},{7,23},{8,24},{9,... | collective-permute-start | bytes 73736 | tf_op jit(solution)/shard_map/ppermute | solution.py:329
  17.9 6.3 %collective-permute-start.6 = (f32[6,48,128]{2,1,0:T(8,128)S(1)}, f32[6,48,128]{2,1,0:T(8,128)S(1)}, u32[]{:S(2)}, u32[]{:S(2)}) collective-permute-start(f32[6,48,128]{2,1,0:T(8,128)S(1)} %raw_product.1.refs_1_), channel_id=1, source_target_pairs={{0,16},{1,17},{2,18},{3,19},{4,20},{5,21},{6,22},{7,23},{8,24},{9,... | collective-permute-start | bytes 442376 | tf_op jit(solution)/shard_map/ppermute | solution.py:329
  21.9 6.2 %collective-permute-start.8 = (f32[12,24,128]{2,1,0:T(8,128)S(1)}, f32[12,24,128]{2,1,0:T(8,128)S(1)}, u32[]{:S(2)}, u32[]{:S(2)}) collective-permute-start(f32[12,24,128]{2,1,0:T(8,128)S(1)} %get-tuple-element.18), channel_id=1, source_target_pairs={{0,16},{1,17},{2,18},{3,19},{4,20},{5,21},{6,22},{7,23},{8,24},{9,... | collective-permute-start | bytes 442376 | tf_op jit(solution)/shard_map/ppermute | solution.py:329
  23.9 5.2 %collective-permute-start.7 = (f32[8,24,128]{2,1,0:T(8,128)S(1)}, f32[8,24,128]{2,1,0:T(8,128)S(1)}, u32[]{:S(2)}, u32[]{:S(2)}) collective-permute-start(f32[8,24,128]{2,1,0:T(8,128)S(1)} %others_ranks.1), channel_id=1, source_target_pairs={{0,16},{1,17},{2,18},{3,19},{4,20},{5,21},{6,22},{7,23},{8,24},{9,... | collective-permute-start | bytes 294920 | tf_op jit(solution)/shard_map/ppermute | solution.py:329

commit v10 on v9

--- a/solution.py
+++ b/solution.py
@@ -31,7 +31,9 @@
     for step in range(steps):
         part = pl.ds(step * span, span)
         for which, (source, target) in enumerate(((field_hbm, field), (test_hbm, test))):
-            copy = pltpu.make_async_copy(source.at[:, part], target.at[step], sems.at[which, step])
+            copy = pltpu.make_async_copy(
+                source.at[:, part], target.at[step, pl.ds(0, source.shape[0])], sems.at[which, step]
+            )
             copy.start()
             copies.append(copy)
     total = low = None
@@ -39,8 +41,8 @@
     for step in range(steps):
         copies[2 * step].wait()
         copies[2 * step + 1].wait()
-        flat_field = field.at[step].reshape(rows * span, lanes)
-        flat_test = test.at[step].reshape(columns * span, lanes)
+        flat_field = field.at[step].reshape((rows + 1) * span, lanes)
+        flat_test = test.at[step].reshape((columns + 1) * span, lanes)
         for pair in range(span // 2):
             x = [flat_field[pl.ds(2 * pair + q, rows, stride=span), :] for q in range(2)]
             t = [flat_test[pl.ds(2 * pair + q, columns, stride=span), :] for q in range(2)]
@@ -74,8 +76,8 @@
             jax.ShapeDtypeStruct((first, rows, lanes), F32),
         ],
         scratch_shapes=[
-            pltpu.VMEM((steps, rows, span, lanes), F32),
-            pltpu.VMEM((steps, columns, span, lanes), F32),
+            pltpu.VMEM((steps, rows + 1, span, lanes), F32),
+            pltpu.VMEM((steps, columns + 1, span, lanes), F32),
             pltpu.SemaphoreType.DMA((2, steps)),
         ],
         compiler_params=pltpu.CompilerParams(vmem_limit_bytes=VMEM_LIMIT),
@@ -225,15 +227,15 @@
 def add_kernel(parties, begin, size, own_ref, *refs):
     *others, out_hbm, total_ref, sem = refs
     others = others[: parties - 1]
-    ranks, span, lanes = total_ref.shape
-    flat = total_ref.reshape(ranks * span, lanes)
+    ranks, span, lanes = out_hbm.shape[0], *total_ref.shape[1:]
+    flat = total_ref.reshape((ranks + 1) * span, lanes)
     bare = size - others[0].shape[0]
     for at in range(size):
         total = own_ref[begin + at]
         for part in others if at >= bare else ():
             total = total + part[at - bare]
         flat[pl.ds(at, ranks, stride=span), :] = total
-    copy = pltpu.make_async_copy(total_ref, out_hbm.at[:, pl.ds(begin, size)], sem)
+    copy = pltpu.make_async_copy(total_ref.at[pl.ds(0, ranks)], out_hbm.at[:, pl.ds(begin, size)], sem)
     copy.start()
     copy.wait()
 
@@ -307,7 +309,7 @@
             in_specs=[pl.BlockSpec(memory_space=pltpu.VMEM)] * count + [pl.BlockSpec(memory_space=pl.ANY)] * len(whole_before),
             out_specs=pl.BlockSpec(memory_space=pl.ANY),
             input_output_aliases={count: 0} if whole_before else {},
-            scratch_shapes=[pltpu.VMEM((ranks, size, lanes), F32), pltpu.SemaphoreType.DMA],
+            scratch_shapes=[pltpu.VMEM((ranks + 1, size, lanes), F32), pltpu.SemaphoreType.DMA],
             compiler_params=PARAMS,
             cost_estimate=COST if step < len(spans) - 1 else None,
             name="add_ranks",

time: 30 us -> 30 us (level)
  no operation moved by 1% of the time
where the time goes in v10:
time: 30 us; the launch traced here: 29.8 us
  starting transfers between devices  13.6 us (45%)
  waiting for transfers between devices  8.97 us (30%)
  Pallas kernels  7.12 us (24%)
    ppermute x9, starting transfers between devices, exchange(): return lax.ppermute(x, AXES, pairs)  13.6 us
    ppermute x9, waiting for transfers between devices, exchange(): return lax.ppermute(x, AXES, pairs)  8.97 us
    pallas_call x7, Pallas kernels, run(): pl.pallas_call(kernel, out_shape=out_shape, compiler_params=PARAMS, cost_...  2.9 us
    pallas_call x1, Pallas kernels, partial_sketch(): pl.pallas_call(functools.partial(sketch_kernel, span), in_specs=[pl.Block...  2.78 us
    pallas_call x2, Pallas kernels, project(): pl.pallas_call(functools.partial(add_kernel, parties, begin, size), out_s...  1.44 us
  transfers between devices with their start and end apart: 9, of which 6 were waited for; matrix products, arithmetic and copies ran while one was open for 0% of the time, Pallas kernels for 12%

profile of v10, /device:TPU:0, one launch (start us, length us, event | category | flops | bytes accessed | tf_op | source)
XLA Modules:
  0.0 29.8 jit_solution(5558525072940950434)
XLA Ops:
  0.0 2.8 %partial_sketch.1 = (f32[48,128]{1,0:T(8,128)S(1)}, bf16[16,256,256]{2,1,0:T(8,128)(2,1)S(1)}, f32[6,128,128]{2,1,0:T(8,128)S(1)}) custom-call(f32[128,32,128]{2,1,0:T(8,128)} %field_hbm.1, f32[48,32,128]{2,1,0:T(8,128)} %test_hbm.1), custom_call_target="tpu_custom_call" | custom-call | tf_op jit(solution)/shard_map/partial_sketch/pallas_call | solution.py:70
  2.8 0.5 %collective-permute-start = (f32[48,128]{1,0:T(8,128)S(1)}, f32[48,128]{1,0:T(8,128)S(1)}, u32[]{:S(2)}, u32[]{:S(2)}) collective-permute-start(f32[48,128]{1,0:T(8,128)S(1)} %get-tuple-element.12), channel_id=1, source_target_pairs={{0,1},{1,0},{2,3},{3,2},{4,5},{5,4},{6,7},{7,6},{8,9},{9,8},{10,11... | collective-permute-start | bytes 73736 | tf_op jit(solution)/shard_map/ppermute | solution.py:331
  3.3 0.8 %collective-permute-done = f32[48,128]{1,0:T(8,128)S(1)} collective-permute-done((f32[48,128]{1,0:T(8,128)S(1)}, f32[48,128]{1,0:T(8,128)S(1)}, u32[]{:S(2)}, u32[]{:S(2)}) %collective-permute-start) | collective-permute-done | bytes 24608 | tf_op jit(solution)/shard_map/ppermute | solution.py:331
  4.2 2.6 %collective-permute-start.1 = (f32[48,128]{1,0:T(8,128)S(1)}, f32[48,128]{1,0:T(8,128)S(1)}, u32[]{:S(2)}, u32[]{:S(2)}) collective-permute-start(f32[48,128]{1,0:T(8,128)S(1)} %add.12.sketch_ref), channel_id=1, source_target_pairs={{0,3},{1,2},{2,1},{3,0},{4,7},{5,6},{6,5},{7,4},{8,11},{9,10},{10,... | collective-permute-start | bytes 73736 | tf_op jit(solution)/shard_map/ppermute | solution.py:331
  6.8 1.6 %collective-permute-start.5 = (f32[6,128,128]{2,1,0:T(8,128)S(1)}, f32[6,128,128]{2,1,0:T(8,128)S(1)}, u32[]{:S(2)}, u32[]{:S(2)}) collective-permute-start(f32[6,128,128]{2,1,0:T(8,128)S(1)} %first_field.1), channel_id=1, source_target_pairs={{0,16},{1,17},{2,18},{3,19},{4,20},{5,21},{6,22},{7,23},{8,24},{9,... | collective-permute-start | bytes 1179656 | tf_op jit(solution)/shard_map/ppermute | solution.py:331
  8.4 0.0 collective-permute-done.1
  8.4 1.7 %collective-permute-start.2 = (f32[48,128]{1,0:T(8,128)S(1)}, f32[48,128]{1,0:T(8,128)S(1)}, u32[]{:S(2)}, u32[]{:S(2)}) collective-permute-start(f32[48,128]{1,0:T(8,128)S(1)} %add.13.sketch_ref), channel_id=1, source_target_pairs={{0,5},{1,4},{2,7},{3,6},{4,1},{5,0},{6,3},{7,2},{8,13},{9,12},{10,... | collective-permute-start | bytes 73736 | tf_op jit(solution)/shard_map/ppermute | solution.py:331
  10.1 1.6 %collective-permute-done.2 = f32[48,128]{1,0:T(8,128)S(1)} collective-permute-done((f32[48,128]{1,0:T(8,128)S(1)}, f32[48,128]{1,0:T(8,128)S(1)}, u32[]{:S(2)}, u32[]{:S(2)}) %collective-permute-start.2) | collective-permute-done | bytes 24608 | tf_op jit(solution)/shard_map/ppermute | solution.py:331
  11.7 3.0 %collective-permute-start.3 = (f32[48,128]{1,0:T(8,128)S(1)}, f32[48,128]{1,0:T(8,128)S(1)}, u32[]{:S(2)}, u32[]{:S(2)}) collective-permute-start(f32[48,128]{1,0:T(8,128)S(1)} %add.14.sketch_ref), channel_id=1, source_target_pairs={{0,9},{1,8},{2,11},{3,10},{4,13},{5,12},{6,15},{7,14},{8,1},{9,0},... | collective-permute-start | bytes 73736 | tf_op jit(solution)/shard_map/ppermute | solution.py:331
  14.7 1.5 %collective-permute-done.3 = f32[48,128]{1,0:T(8,128)S(1)} collective-permute-done((f32[48,128]{1,0:T(8,128)S(1)}, f32[48,128]{1,0:T(8,128)S(1)}, u32[]{:S(2)}, u32[]{:S(2)}) %collective-permute-start.3) | collective-permute-done | bytes 24608 | tf_op jit(solution)/shard_map/ppermute | solution.py:331
  16.2 1.5 %collective-permute-start.4 = (f32[48,128]{1,0:T(8,128)S(1)}, f32[48,128]{1,0:T(8,128)S(1)}, u32[]{:S(2)}, u32[]{:S(2)}) collective-permute-start(f32[48,128]{1,0:T(8,128)S(1)} %add.15.sketch_ref), channel_id=1, source_target_pairs={{0,16},{1,17},{2,18},{3,19},{4,20},{5,21},{6,22},{7,23},{8,24},{9,... | collective-permute-start | bytes 73736 | tf_op jit(solution)/shard_map/ppermute | solution.py:331
  17.7 0.2 raw_product.1.refs_1_
  17.9 0.6 %collective-permute-start.6 = (f32[6,48,128]{2,1,0:T(8,128)S(1)}, f32[6,48,128]{2,1,0:T(8,128)S(1)}, u32[]{:S(2)}, u32[]{:S(2)}) collective-permute-start(f32[6,48,128]{2,1,0:T(8,128)S(1)} %raw_product.1.refs_1_), channel_id=1, source_target_pairs={{0,16},{1,17},{2,18},{3,19},{4,20},{5,21},{6,22},{7,23},{8,24},{9,... | collective-permute-start | bytes 442376 | tf_op jit(solution)/shard_map/ppermute | solution.py:331
  18.5 1.5 %collective-permute-done.4 = f32[48,128]{1,0:T(8,128)S(1)} collective-permute-done((f32[48,128]{1,0:T(8,128)S(1)}, f32[48,128]{1,0:T(8,128)S(1)}, u32[]{:S(2)}, u32[]{:S(2)}) %collective-permute-start.4) | collective-permute-done | bytes 24608 | tf_op jit(solution)/shard_map/ppermute | solution.py:331
  20.0 1.8 %solve.1 = (f32[48,256]{1,0:T(8,128)S(1)}, f32[12,24,128]{2,1,0:T(8,128)S(1)}) custom-call(f32[48,256]{1,0:T(8,128)S(1)} %pad_maximum_fusion.sketch_ref, bf16[16,256,256]{2,1,0:T(8,128)(2,1)S(1)} %get-tuple-element.15.pairs_ref), custom_call_target="tpu_custom_call" | custom-call | flops 1073741824 | bytes 33554432 | tf_op jit(solution)/shard_map/solve/pallas_call | solution.py:250
  21.9 1.8 %collective-permute-start.8 = (f32[12,24,128]{2,1,0:T(8,128)S(1)}, f32[12,24,128]{2,1,0:T(8,128)S(1)}, u32[]{:S(2)}, u32[]{:S(2)}) collective-permute-start(f32[12,24,128]{2,1,0:T(8,128)S(1)} %get-tuple-element.18), channel_id=1, source_target_pairs={{0,16},{1,17},{2,18},{3,19},{4,20},{5,21},{6,22},{7,23},{8,24},{9,... | collective-permute-start | bytes 442376 | tf_op jit(solution)/shard_map/ppermute | solution.py:331
  23.7 0.2 others_ranks.1
  23.9 0.3 %collective-permute-start.7 = (f32[8,24,128]{2,1,0:T(8,128)S(1)}, f32[8,24,128]{2,1,0:T(8,128)S(1)}, u32[]{:S(2)}, u32[]{:S(2)}) collective-permute-start(f32[8,24,128]{2,1,0:T(8,128)S(1)} %others_ranks.1), channel_id=1, source_target_pairs={{0,16},{1,17},{2,18},{3,19},{4,20},{5,21},{6,22},{7,23},{8,24},{9,... | collective-permute-start | bytes 294920 | tf_op jit(solution)/shard_map/ppermute | solution.py:331
  24.2 0.0 collective-permute-done.6.refs_2_
  24.2 0.6 %own_ranks.1.own_ref = f32[32,24,128]{2,1,0:T(8,128)S(1)} custom-call(f32[48,256]{1,0:T(8,128)S(1)} %pad_maximum_fusion.sketch_ref, f32[48,256]{1,0:T(8,128)S(1)} %get-tuple-element.16.solved_ref, bf16[16,256,256]{2,1,0:T(8,128)(2,1)S(1)} %get-tuple-element.15.pairs_ref, f32[6,128,128]{2,1,0:T(8,128)S(1)} %collective-permute-done.5.refs_0_, ...), custom_call_target="tpu_custom_call" | custom-call | flops 1073741824 | bytes 33554432 | tf_op jit(solution)/shard_map/own_ranks/pallas_call | solution.py:250
  24.9 3.2 %collective-permute-done.8.refs_0_ = f32[12,24,128]{2,1,0:T(8,128)S(1)} collective-permute-done((f32[12,24,128]{2,1,0:T(8,128)S(1)}, f32[12,24,128]{2,1,0:T(8,128)S(1)}, u32[]{:S(2)}, u32[]{:S(2)}) %collective-permute-start.8) | collective-permute-done | bytes 147488 | tf_op jit(solution)/shard_map/ppermute | solution.py:331
  28.1 0.8 %add_ranks.2.refs_1_ = f32[24,32,128]{2,1,0:T(8,128)} custom-call(f32[32,24,128]{2,1,0:T(8,128)S(1)} %own_ranks.1.own_ref, f32[12,24,128]{2,1,0:T(8,128)S(1)} %collective-permute-done.8.refs_0_), custom_call_target="tpu_custom_call" | custom-call | flops 1073741824 | bytes 33554432 | tf_op jit(solution)/shard_map/add_ranks/pallas_call | solution.py:306
  28.9 0.3 collective-permute-done.7.refs_0_
  29.2 0.7 %add_ranks.3 = f32[24,32,128]{2,1,0:T(8,128)} custom-call(f32[32,24,128]{2,1,0:T(8,128)S(1)} %own_ranks.1.own_ref, f32[8,24,128]{2,1,0:T(8,128)S(1)} %collective-permute-done.7.refs_0_, f32[24,32,128]{2,1,0:T(8,128)} %add_ranks.2.refs_1_), custom_call_target="tpu_custom_call", output_to_operand_aliasing={{}: (2, {})} | custom-call | tf_op jit(solution)/shard_map/add_ranks/pallas_call | solution.py:306
  (9 shorter events, 0.1 us)
Async XLA Ops:
  2.8 1.4 %collective-permute-start = (f32[48,128]{1,0:T(8,128)S(1)}, f32[48,128]{1,0:T(8,128)S(1)}, u32[]{:S(2)}, u32[]{:S(2)}) collective-permute-start(f32[48,128]{1,0:T(8,128)S(1)} %get-tuple-element.12), channel_id=1, source_target_pairs={{0,1},{1,0},{2,3},{3,2},{4,5},{5,4},{6,7},{7,6},{8,9},{9,8},{10,11... | collective-permute-start | bytes 73736 | tf_op jit(solution)/shard_map/ppermute | solution.py:331
  4.2 4.2 %collective-permute-start.1 = (f32[48,128]{1,0:T(8,128)S(1)}, f32[48,128]{1,0:T(8,128)S(1)}, u32[]{:S(2)}, u32[]{:S(2)}) collective-permute-start(f32[48,128]{1,0:T(8,128)S(1)} %add.12.sketch_ref), channel_id=1, source_target_pairs={{0,3},{1,2},{2,1},{3,0},{4,7},{5,6},{6,5},{7,4},{8,11},{9,10},{10,... | collective-permute-start | bytes 73736 | tf_op jit(solution)/shard_map/ppermute | solution.py:331
  6.8 13.2 %collective-permute-start.5 = (f32[6,128,128]{2,1,0:T(8,128)S(1)}, f32[6,128,128]{2,1,0:T(8,128)S(1)}, u32[]{:S(2)}, u32[]{:S(2)}) collective-permute-start(f32[6,128,128]{2,1,0:T(8,128)S(1)} %first_field.1), channel_id=1, source_target_pairs={{0,16},{1,17},{2,18},{3,19},{4,20},{5,21},{6,22},{7,23},{8,24},{9,... | collective-permute-start | bytes 1179656 | tf_op jit(solution)/shard_map/ppermute | solution.py:331
  8.4 3.3 %collective-permute-start.2 = (f32[48,128]{1,0:T(8,128)S(1)}, f32[48,128]{1,0:T(8,128)S(1)}, u32[]{:S(2)}, u32[]{:S(2)}) collective-permute-start(f32[48,128]{1,0:T(8,128)S(1)} %add.13.sketch_ref), channel_id=1, source_target_pairs={{0,5},{1,4},{2,7},{3,6},{4,1},{5,0},{6,3},{7,2},{8,13},{9,12},{10,... | collective-permute-start | bytes 73736 | tf_op jit(solution)/shard_map/ppermute | solution.py:331
  11.7 4.5 %collective-permute-start.3 = (f32[48,128]{1,0:T(8,128)S(1)}, f32[48,128]{1,0:T(8,128)S(1)}, u32[]{:S(2)}, u32[]{:S(2)}) collective-permute-start(f32[48,128]{1,0:T(8,128)S(1)} %add.14.sketch_ref), channel_id=1, source_target_pairs={{0,9},{1,8},{2,11},{3,10},{4,13},{5,12},{6,15},{7,14},{8,1},{9,0},... | collective-permute-start | bytes 73736 | tf_op jit(solution)/shard_map/ppermute | solution.py:331
  16.2 3.8 %collective-permute-start.4 = (f32[48,128]{1,0:T(8,128)S(1)}, f32[48,128]{1,0:T(8,128)S(1)}, u32[]{:S(2)}, u32[]{:S(2)}) collective-permute-start(f32[48,128]{1,0:T(8,128)S(1)} %add.15.sketch_ref), channel_id=1, source_target_pairs={{0,16},{1,17},{2,18},{3,19},{4,20},{5,21},{6,22},{7,23},{8,24},{9,... | collective-permute-start | bytes 73736 | tf_op jit(solution)/shard_map/ppermute | solution.py:331
  17.9 6.3 %collective-permute-start.6 = (f32[6,48,128]{2,1,0:T(8,128)S(1)}, f32[6,48,128]{2,1,0:T(8,128)S(1)}, u32[]{:S(2)}, u32[]{:S(2)}) collective-permute-start(f32[6,48,128]{2,1,0:T(8,128)S(1)} %raw_product.1.refs_1_), channel_id=1, source_target_pairs={{0,16},{1,17},{2,18},{3,19},{4,20},{5,21},{6,22},{7,23},{8,24},{9,... | collective-permute-start | bytes 442376 | tf_op jit(solution)/shard_map/ppermute | solution.py:331
  21.9 6.2 %collective-permute-start.8 = (f32[12,24,128]{2,1,0:T(8,128)S(1)}, f32[12,24,128]{2,1,0:T(8,128)S(1)}, u32[]{:S(2)}, u32[]{:S(2)}) collective-permute-start(f32[12,24,128]{2,1,0:T(8,128)S(1)} %get-tuple-element.18), channel_id=1, source_target_pairs={{0,16},{1,17},{2,18},{3,19},{4,20},{5,21},{6,22},{7,23},{8,24},{9,... | collective-permute-start | bytes 442376 | tf_op jit(solution)/shard_map/ppermute | solution.py:331
  23.9 5.2 %collective-permute-start.7 = (f32[8,24,128]{2,1,0:T(8,128)S(1)}, f32[8,24,128]{2,1,0:T(8,128)S(1)}, u32[]{:S(2)}, u32[]{:S(2)}) collective-permute-start(f32[8,24,128]{2,1,0:T(8,128)S(1)} %others_ranks.1), channel_id=1, source_target_pairs={{0,16},{1,17},{2,18},{3,19},{4,20},{5,21},{6,22},{7,23},{8,24},{9,... | collective-permute-start | bytes 294920 | tf_op jit(solution)/shard_map/ppermute | solution.py:331
